TPU v7x, 256 devices: a whole 4x4x8 slice. The times are simulated.
256 devices in a mesh: tm: 64 (over z, x, core), space: 4 (over y).
Axes of the slice: x: 4, y: 4, z: 8, core: 2. Of those that a mesh axis runs over, the one named last changes fastest.
Arguments:
- initial: float32 [256, 512], P('space'), may hold values from -6 to 6
- diffusivity: float32 [256, 512], P('space'), may hold values from 0.0008 to 0.0035
- forcing: float32 [1024, 256, 512], P('tm', 'space'), may hold values from -3 to 3
- guessed: float32 [256, 256, 512], P('tm', 'space'), may hold values from -6 to 6
Outputs:
- c_states: float32 [256, 256, 512], P('tm', 'space')
All inputs are finite; a program needn't handle non-finite values.
Results may differ from a plain program's by a relative error of at most 0.00002.
Values sent between devices are 32-bit elements; how exact they have to be, the bound alone decides.
No kernel may reach another device: no remote copies, remote signals or barrier semaphores. Data moves between devices by JAX's collectives and lax.ppermute only.
A program may use at most 64 MiB of HBM per device.

v0:
```python
import jax
import jax.numpy as jnp
from jax import lax
from jax.sharding import PartitionSpec as P

FACTOR = 4


def extended(array, sides, width):
    for axis, dim in sides:
        count, length = (lax.axis_size(axis), array.shape[dim])
        up = [(i, (i + 1) % count) for i in range(count - 1)]
        down = [(j, i) for i, j in up]
        last = lax.slice_in_dim(array, length - width, length, axis=dim)
        initial = lax.slice_in_dim(array, 0, width, axis=dim)
        before = lax.ppermute(last, axis, up)
        after = lax.ppermute(initial, axis, down)
        array = jnp.concatenate([before, array, after], axis=dim)
    return array


def shifted_2(array, axis, by):
    count = lax.axis_size(axis)
    pairs = [(i, i + by) for i in range(count) if 0 <= i + by < count]
    return lax.ppermute(array, axis, pairs)


def advance(fields, diffusivity, stride):
    padded = extended(fields, (("space", 1),), 1)
    padded = jnp.pad(padded, ((0, 0), (0, 0), (1, 1)))
    laplace = (
        padded[:, 2:, 1:-1]
        + padded[:, :-2, 1:-1]
        + padded[:, 1:-1, 2:]
        + padded[:, 1:-1, :-2]
        - 4.0 * fields
    )
    return fields + stride * diffusivity * laplace


def previous(fields):
    return shifted_2(fields, "tm", 1)


def march_on(starts, sources, number, diffusivity, stride):
    values = []
    current = starts
    for i in range(number):
        current = advance(current, diffusivity, stride) + sources[:, i]
        values.append(current)
    return values


def per_device(initial, diffusivity, forcing, guessed):
    position = lax.axis_index("tm")
    leading = position == 0
    within = position % FACTOR
    start_plane, diff_wide, forcing_wide, guessed_wide = (initial, diffusivity, forcing, guessed)
    sources = forcing_wide.reshape((FACTOR, FACTOR) + forcing_wide.shape[1:])
    start_field = start_plane[None]
    incoming = jnp.where(leading, start_field, previous(guessed_wide[-1:]))
    starts = jnp.concatenate([incoming, guessed_wide[:-1]], 0)
    relaxed = march_on(starts, sources, FACTOR, diff_wide, 1.0)[-1]
    arrived = jnp.where(leading, start_field, previous(relaxed[-1:]))
    starts = jnp.concatenate([arrived, relaxed[:-1]], 0)
    before = march_on(starts, sources, FACTOR - 1, diff_wide, 1.0)[-1]
    residual = sources[:, -1] + advance(before, diff_wide, 1.0) - relaxed
    stride_one = float(FACTOR)
    current = residual[:1]
    for i in range(1, FACTOR):
        current = advance(current, diff_wide, stride_one) + residual[i : i + 1]
    relaxed_one = current
    before_one = march_on(previous(relaxed_one), residual[None], FACTOR - 1, diff_wide, stride_one)[
        -1
    ]
    source_wide = residual[-1:] + advance(before_one, diff_wide, stride_one) - relaxed_one
    stride_two = float(FACTOR**2)
    stride_three = float(FACTOR**3)
    current = source_wide
    for t in range(1, FACTOR):
        candidate = advance(previous(current), diffusivity, stride_two) + source_wide
        current = jnp.where(within == t, candidate, current)
    for t in range(FACTOR - 1):
        candidate = advance(previous(current), diffusivity, stride_two) + source_wide
        current = jnp.where(within == t, candidate, current)
    source_three = source_wide + advance(previous(current), diffusivity, stride_two) - current
    gathered = lax.all_gather(source_three, "tm", axis=0, tiled=True)
    owners = gathered.reshape((-1, FACTOR) + gathered.shape[1:])[:, -1]
    owner_index = position // FACTOR

    def coarse_step(i, carried):
        marching, chosen, earlier = carried
        marching = advance(marching, diffusivity, stride_three) + lax.dynamic_slice_in_dim(
            owners, i, 1, 0
        )
        chosen = jnp.where(i == owner_index, marching, chosen)
        earlier = jnp.where(i == owner_index - 1, marching, earlier)
        return (marching, chosen, earlier)

    empty_state = jnp.zeros_like(source_three)
    final_state, coarsest, earlier = lax.fori_loop(
        0, owners.shape[0], coarse_step, (empty_state, empty_state, empty_state)
    )
    for t in range(FACTOR - 1):
        shifted = previous(current)
        if t == 0:
            shifted = jnp.where(within == 0, shifted + earlier, shifted)
        candidate = advance(shifted, diffusivity, stride_two) + source_wide
        current = jnp.where(within == t, candidate, current)
    current = jnp.where(within == FACTOR - 1, current + coarsest, current)
    corrected_one = relaxed_one + current
    values_one = march_on(
        previous(corrected_one), residual[None], FACTOR - 1, diff_wide, stride_one
    )
    errors = jnp.concatenate(values_one + [corrected_one], 0)
    result = relaxed + errors
    return result


def solution(mesh):
    return jax.shard_map(
        per_device,
        mesh=mesh,
        in_specs=(
            P("space", None),
            P("space", None),
            P("tm", "space", None),
            P("tm", "space", None),
        ),
        out_specs=P("tm", "space", None),
        check_vma=False,
    )
```

profile of v0, /device:TPU:56, one launch (start us, length us, event | category | flops | bytes accessed | tf_op | source)
XLA Modules:
  0.0 572.1 jit_solution(4842437319055456160)
XLA Ops:
  10.6 5.4 collective-permute-done.2
  17.0 2.6 collective-permute-start.3
  21.0 4.2 collective-permute-done.4
  25.9 2.4 collective-permute-start.5
  29.6 4.2 collective-permute-done.6
  38.2 4.2 collective-permute-done.8
  44.4 4.5 collective-permute-start.9
  53.0 6.4 %collective-permute-done.11 = f32[1,64,512]{2,1,0:T(8,128)S(1)} collective-permute-done((f32[1,64,512]{2,1,0:T(8,128)S(1)}, f32[1,64,512]{2,1,0:T(8,128)S(1)}, u32[]{:S(2)}, u32[]{:S(2)}) %collective-permute-start.11) | collective-permute-done | bytes 131104 | tf_op jit(solution)/shard_map/ppermute | solution.py:25
  59.5 4.2 collective-permute-start.12
  65.0 4.2 collective-permute-done.13
  73.2 4.2 collective-permute-done.15
  81.4 4.2 collective-permute-done.17
  89.6 4.2 collective-permute-done.19
  97.8 4.2 collective-permute-done.21
  105.4 4.2 collective-permute-done.23
  113.1 4.2 collective-permute-done.25
  119.5 6.5 %collective-permute-done.26 = f32[1,64,512]{2,1,0:T(8,128)S(1)} collective-permute-done((f32[1,64,512]{2,1,0:T(8,128)S(1)}, f32[1,64,512]{2,1,0:T(8,128)S(1)}, u32[]{:S(2)}, u32[]{:S(2)}) %collective-permute-start.26) | collective-permute-done | bytes 131104 | tf_op jit(solution)/shard_map/ppermute | solution.py:25
  129.2 4.2 collective-permute-done.28
  136.9 4.2 collective-permute-done.30
  144.5 4.2 collective-permute-done.32
  152.2 4.2 collective-permute-done.34
  158.6 6.5 %collective-permute-done.35 = f32[1,64,512]{2,1,0:T(8,128)S(1)} collective-permute-done((f32[1,64,512]{2,1,0:T(8,128)S(1)}, f32[1,64,512]{2,1,0:T(8,128)S(1)}, u32[]{:S(2)}, u32[]{:S(2)}) %collective-permute-start.35) | collective-permute-done | bytes 131104 | tf_op jit(solution)/shard_map/ppermute | solution.py:25
  168.3 4.2 collective-permute-done.37
  174.7 6.5 %collective-permute-done.38 = f32[1,64,512]{2,1,0:T(8,128)S(1)} collective-permute-done((f32[1,64,512]{2,1,0:T(8,128)S(1)}, f32[1,64,512]{2,1,0:T(8,128)S(1)}, u32[]{:S(2)}, u32[]{:S(2)}) %collective-permute-start.38) | collective-permute-done | bytes 131104 | tf_op jit(solution)/shard_map/ppermute | solution.py:25
  184.4 4.2 collective-permute-done.40
  190.7 6.5 %collective-permute-done.41 = f32[1,64,512]{2,1,0:T(8,128)S(1)} collective-permute-done((f32[1,64,512]{2,1,0:T(8,128)S(1)}, f32[1,64,512]{2,1,0:T(8,128)S(1)}, u32[]{:S(2)}, u32[]{:S(2)}) %collective-permute-start.41) | collective-permute-done | bytes 131104 | tf_op jit(solution)/shard_map/ppermute | solution.py:25
  200.4 4.2 collective-permute-done.43
  206.8 6.5 %collective-permute-done.44 = f32[1,64,512]{2,1,0:T(8,128)S(1)} collective-permute-done((f32[1,64,512]{2,1,0:T(8,128)S(1)}, f32[1,64,512]{2,1,0:T(8,128)S(1)}, u32[]{:S(2)}, u32[]{:S(2)}) %collective-permute-start.44) | collective-permute-done | bytes 131104 | tf_op jit(solution)/shard_map/ppermute | solution.py:25
  216.5 4.2 collective-permute-done.46
  222.8 6.5 %collective-permute-done.47 = f32[1,64,512]{2,1,0:T(8,128)S(1)} collective-permute-done((f32[1,64,512]{2,1,0:T(8,128)S(1)}, f32[1,64,512]{2,1,0:T(8,128)S(1)}, u32[]{:S(2)}, u32[]{:S(2)}) %collective-permute-start.47) | collective-permute-done | bytes 131104 | tf_op jit(solution)/shard_map/ppermute | solution.py:25
  232.5 4.2 collective-permute-done.49
  238.9 6.5 %collective-permute-done.50 = f32[1,64,512]{2,1,0:T(8,128)S(1)} collective-permute-done((f32[1,64,512]{2,1,0:T(8,128)S(1)}, f32[1,64,512]{2,1,0:T(8,128)S(1)}, u32[]{:S(2)}, u32[]{:S(2)}) %collective-permute-start.50) | collective-permute-done | bytes 131104 | tf_op jit(solution)/shard_map/ppermute | solution.py:25
  248.8 4.0 collective-permute-done.52
  255.0 6.5 %collective-permute-done.53 = f32[1,64,512]{2,1,0:T(8,128)S(1)} collective-permute-done((f32[1,64,512]{2,1,0:T(8,128)S(1)}, f32[1,64,512]{2,1,0:T(8,128)S(1)}, u32[]{:S(2)}, u32[]{:S(2)}) %collective-permute-start.53) | collective-permute-done | bytes 131104 | tf_op jit(solution)/shard_map/ppermute | solution.py:25
  264.7 4.2 collective-permute-done.55
  269.8 95.0 %all-gather.2.cloned.1.call-done = f32[64,64,512]{2,1,0:T(8,128)} async-done(((f32[1,64,512]{2,1,0:T(8,128)}), f32[64,64,512]{2,1,0:T(8,128)}) %all-gather.2.cloned.1.call-update) | async-done | bytes 8388624 | tf_op jit(solution)/shard_map/all_gather | solution.py:87
  366.6 126.3 %while.20 = (s32[]{:T(128)}, f32[1,64,512]{2,1,0:T(8,128)S(1)}, f32[1,64,512]{2,1,0:T(8,128)S(1)}, f32[1,64,512]{2,1,0:T(8,128)S(1)}, f32[64,512]{1,0:T(8,128)S(...) while((s32[]{:T(128)}, f32[1,64,512]{2,1,0:T(8,128)S(1)}, ...), condition=%wide.region_1.2_spmd.clone, body=%wide.region_0.1_spmd.clone.sunk | while | flops 795685 | bytes 2003697 | solution.py:101
  366.7 2.8 collective-permute-start
  370.9 4.2 collective-permute-done.1
  379.1 4.2 collective-permute-done.1
  383.6 2.4 collective-permute-start
  387.4 4.2 collective-permute-done.1
  395.1 4.2 collective-permute-done.1
  402.9 4.2 collective-permute-done.1
  410.7 4.2 collective-permute-done.1
  418.5 4.2 collective-permute-done.1
  426.2 4.2 collective-permute-done.1
  434.0 4.2 collective-permute-done.1
  441.8 4.2 collective-permute-done.1
  449.6 4.2 collective-permute-done.1
  457.3 4.2 collective-permute-done.1
  465.1 4.2 collective-permute-done.1
  472.9 4.2 collective-permute-done.1
  480.7 4.2 collective-permute-done.1
  488.4 4.2 collective-permute-done.1
  496.4 4.2 collective-permute-done.57
  502.7 6.5 %collective-permute-done.58 = f32[1,64,512]{2,1,0:T(8,128)S(1)} collective-permute-done((f32[1,64,512]{2,1,0:T(8,128)S(1)}, f32[1,64,512]{2,1,0:T(8,128)S(1)}, u32[]{:S(2)}, u32[]{:S(2)}) %collective-permute-start.58) | collective-permute-done | bytes 131104 | tf_op jit(solution)/shard_map/ppermute | solution.py:25
  512.4 4.2 collective-permute-done.60
  518.8 6.5 %collective-permute-done.61 = f32[1,64,512]{2,1,0:T(8,128)S(1)} collective-permute-done((f32[1,64,512]{2,1,0:T(8,128)S(1)}, f32[1,64,512]{2,1,0:T(8,128)S(1)}, u32[]{:S(2)}, u32[]{:S(2)}) %collective-permute-start.61) | collective-permute-done | bytes 131104 | tf_op jit(solution)/shard_map/ppermute | solution.py:25
  528.5 4.2 collective-permute-done.63
  534.9 6.5 %collective-permute-done.64 = f32[1,64,512]{2,1,0:T(8,128)S(1)} collective-permute-done((f32[1,64,512]{2,1,0:T(8,128)S(1)}, f32[1,64,512]{2,1,0:T(8,128)S(1)}, u32[]{:S(2)}, u32[]{:S(2)}) %collective-permute-start.64) | collective-permute-done | bytes 131104 | tf_op jit(solution)/shard_map/ppermute | solution.py:25
  544.6 4.2 collective-permute-done.66
  552.3 4.2 collective-permute-done.68
  560.0 4.2 collective-permute-done.70
  (335 shorter events, 179.9 us)
Async XLA Ops:
  6.5 358.2 %all-gather.2.cloned.1.call-start = ((), (), s32[]{:S(2)}) async-start(), calls=%async_computation | async-start | bytes 8519680 | tf_op jit(solution)/shard_map/all_gather | solution.py:87
  7.6 8.4 %collective-permute-start.2 = (f32[1,64,512]{2,1,0:T(8,128)S(1)}, f32[1,64,512]{2,1,0:T(8,128)S(1)}, u32[]{:S(2)}, u32[]{:S(2)}) collective-permute-start(f32[1,64,512]{2,1,0:T(8,128)S(1)} %slice.738), channel_id=1, source_target_pairs={{0,4},{4,8},{8,12},{12,16},{16,20},{20,24},{24,28},{28,32},{32,36}... | collective-permute-start | bytes 393224 | tf_op jit(solution)/shard_map/ppermute | solution.py:25
  17.0 4.0 collective-permute-start.3
  19.6 5.5 collective-permute-start.4
  25.9 3.7 collective-permute-start.5
  28.2 5.5 collective-permute-start.6
  36.9 5.5 collective-permute-start.8
  43.1 5.9 %collective-permute-start.10 = (f32[4,1,512]{2,1,0:T(1,128)S(1)}, f32[4,1,512]{2,1,0:T(1,128)S(1)}, u32[]{:S(2)}, u32[]{:S(2)}) collective-permute-start(f32[4,1,512]{2,1,0:T(1,128)S(1)} %get-tuple-element.248), channel_id=1, source_target_pairs={{0,1},{1,2},{2,3},{4,5},{5,6},{6,7},{8,9},{9,10},{10,11},{12,13},{... | collective-permute-start | bytes 24584 | tf_op jit(solution)/shard_map/ppermute | solution.py:16
  44.4 5.9 %collective-permute-start.9 = (f32[4,1,512]{2,1,0:T(1,128)S(1)}, f32[4,1,512]{2,1,0:T(1,128)S(1)}, u32[]{:S(2)}, u32[]{:S(2)}) collective-permute-start(f32[4,1,512]{2,1,0:T(1,128)S(1)} %get-tuple-element.249), channel_id=1, source_target_pairs={{1,0},{2,1},{3,2},{5,4},{6,5},{7,6},{9,8},{10,9},{11,10},{13,12},{... | collective-permute-start | bytes 24584 | tf_op jit(solution)/shard_map/ppermute | solution.py:17
  51.0 8.4 %collective-permute-start.11 = (f32[1,64,512]{2,1,0:T(8,128)S(1)}, f32[1,64,512]{2,1,0:T(8,128)S(1)}, u32[]{:S(2)}, u32[]{:S(2)}) collective-permute-start(f32[1,64,512]{2,1,0:T(8,128)S(1)} %slice.954), channel_id=1, source_target_pairs={{0,4},{4,8},{8,12},{12,16},{16,20},{20,24},{24,28},{28,32},{32,36}... | collective-permute-start | bytes 393224 | tf_op jit(solution)/shard_map/ppermute | solution.py:25
  59.5 5.5 collective-permute-start.12
  63.7 5.5 collective-permute-start.13
  71.9 5.5 collective-permute-start.15
  80.1 5.5 collective-permute-start.17
  88.2 5.5 collective-permute-start.19
  96.5 5.5 collective-permute-start.21
  104.1 5.5 collective-permute-start.23
  111.8 5.5 collective-permute-start.25
  117.6 8.4 %collective-permute-start.26 = (f32[1,64,512]{2,1,0:T(8,128)S(1)}, f32[1,64,512]{2,1,0:T(8,128)S(1)}, u32[]{:S(2)}, u32[]{:S(2)}) collective-permute-start(f32[1,64,512]{2,1,0:T(8,128)S(1)} %fusion.147), channel_id=1, source_target_pairs={{0,4},{4,8},{8,12},{12,16},{16,20},{20,24},{24,28},{28,32},{32,36}... | collective-permute-start | bytes 393224 | tf_op jit(solution)/shard_map/ppermute | solution.py:25
  127.9 5.5 collective-permute-start.28
  135.6 5.5 collective-permute-start.30
  143.2 5.5 collective-permute-start.32
  150.9 5.5 collective-permute-start.34
  156.7 8.4 %collective-permute-start.35 = (f32[1,64,512]{2,1,0:T(8,128)S(1)}, f32[1,64,512]{2,1,0:T(8,128)S(1)}, u32[]{:S(2)}, u32[]{:S(2)}) collective-permute-start(f32[1,64,512]{2,1,0:T(8,128)S(1)} %fusion.127), channel_id=1, source_target_pairs={{0,4},{4,8},{8,12},{12,16},{16,20},{20,24},{24,28},{28,32},{32,36}... | collective-permute-start | bytes 393224 | tf_op jit(solution)/shard_map/ppermute | solution.py:25
  167.0 5.5 collective-permute-start.37
  172.7 8.4 %collective-permute-start.38 = (f32[1,64,512]{2,1,0:T(8,128)S(1)}, f32[1,64,512]{2,1,0:T(8,128)S(1)}, u32[]{:S(2)}, u32[]{:S(2)}) collective-permute-start(f32[1,64,512]{2,1,0:T(8,128)S(1)} %add_select_fusion.2), channel_id=1, source_target_pairs={{0,4},{4,8},{8,12},{12,16},{16,20},{20,24},{24,28},{28,32},{32,36}... | collective-permute-start | bytes 393224 | tf_op jit(solution)/shard_map/ppermute | solution.py:25
  183.1 5.5 collective-permute-start.40
  188.8 8.4 %collective-permute-start.41 = (f32[1,64,512]{2,1,0:T(8,128)S(1)}, f32[1,64,512]{2,1,0:T(8,128)S(1)}, u32[]{:S(2)}, u32[]{:S(2)}) collective-permute-start(f32[1,64,512]{2,1,0:T(8,128)S(1)} %fusion.117), channel_id=1, source_target_pairs={{0,4},{4,8},{8,12},{12,16},{16,20},{20,24},{24,28},{28,32},{32,36}... | collective-permute-start | bytes 393224 | tf_op jit(solution)/shard_map/ppermute | solution.py:25
  199.1 5.5 collective-permute-start.43
  204.8 8.4 %collective-permute-start.44 = (f32[1,64,512]{2,1,0:T(8,128)S(1)}, f32[1,64,512]{2,1,0:T(8,128)S(1)}, u32[]{:S(2)}, u32[]{:S(2)}) collective-permute-start(f32[1,64,512]{2,1,0:T(8,128)S(1)} %fusion.111), channel_id=1, source_target_pairs={{0,4},{4,8},{8,12},{12,16},{16,20},{20,24},{24,28},{28,32},{32,36}... | collective-permute-start | bytes 393224 | tf_op jit(solution)/shard_map/ppermute | solution.py:25
  215.2 5.5 collective-permute-start.46
  220.9 8.4 %collective-permute-start.47 = (f32[1,64,512]{2,1,0:T(8,128)S(1)}, f32[1,64,512]{2,1,0:T(8,128)S(1)}, u32[]{:S(2)}, u32[]{:S(2)}) collective-permute-start(f32[1,64,512]{2,1,0:T(8,128)S(1)} %fusion.105), channel_id=1, source_target_pairs={{0,4},{4,8},{8,12},{12,16},{16,20},{20,24},{24,28},{28,32},{32,36}... | collective-permute-start | bytes 393224 | tf_op jit(solution)/shard_map/ppermute | solution.py:25
  231.2 5.5 collective-permute-start.49
  237.0 8.4 %collective-permute-start.50 = (f32[1,64,512]{2,1,0:T(8,128)S(1)}, f32[1,64,512]{2,1,0:T(8,128)S(1)}, u32[]{:S(2)}, u32[]{:S(2)}) collective-permute-start(f32[1,64,512]{2,1,0:T(8,128)S(1)} %fusion.99), channel_id=1, source_target_pairs={{0,4},{4,8},{8,12},{12,16},{16,20},{20,24},{24,28},{28,32},{32,36}... | collective-permute-start | bytes 393224 | tf_op jit(solution)/shard_map/ppermute | solution.py:25
  247.3 5.5 collective-permute-start.52
  253.0 8.4 %collective-permute-start.53 = (f32[1,64,512]{2,1,0:T(8,128)S(1)}, f32[1,64,512]{2,1,0:T(8,128)S(1)}, u32[]{:S(2)}, u32[]{:S(2)}) collective-permute-start(f32[1,64,512]{2,1,0:T(8,128)S(1)} %fusion.93), channel_id=1, source_target_pairs={{0,4},{4,8},{8,12},{12,16},{16,20},{20,24},{24,28},{28,32},{32,36}... | collective-permute-start | bytes 393224 | tf_op jit(solution)/shard_map/ppermute | solution.py:25
  263.3 5.5 collective-permute-start.55
  366.7 4.2 collective-permute-start
  369.5 5.5 collective-permute-start.1
  377.7 5.5 collective-permute-start.1
  383.6 3.8 collective-permute-start
  386.0 5.5 collective-permute-start.1
  393.8 5.5 collective-permute-start.1
  401.6 5.5 collective-permute-start.1
  409.4 5.5 collective-permute-start.1
  417.1 5.5 collective-permute-start.1
  424.9 5.5 collective-permute-start.1
  432.7 5.5 collective-permute-start.1
  440.5 5.5 collective-permute-start.1
  448.2 5.5 collective-permute-start.1
  456.0 5.5 collective-permute-start.1
  463.8 5.5 collective-permute-start.1
  471.6 5.5 collective-permute-start.1
  479.3 5.5 collective-permute-start.1
  487.1 5.5 collective-permute-start.1
  494.9 5.6 collective-permute-start.57
  500.8 8.4 %collective-permute-start.58 = (f32[1,64,512]{2,1,0:T(8,128)S(1)}, f32[1,64,512]{2,1,0:T(8,128)S(1)}, u32[]{:S(2)}, u32[]{:S(2)}) collective-permute-start(f32[1,64,512]{2,1,0:T(8,128)S(1)} %fusion.81), channel_id=1, source_target_pairs={{0,4},{4,8},{8,12},{12,16},{16,20},{20,24},{24,28},{28,32},{32,36}... | collective-permute-start | bytes 393224 | tf_op jit(solution)/shard_map/ppermute | solution.py:25
  511.1 5.5 collective-permute-start.60
  516.9 8.4 %collective-permute-start.61 = (f32[1,64,512]{2,1,0:T(8,128)S(1)}, f32[1,64,512]{2,1,0:T(8,128)S(1)}, u32[]{:S(2)}, u32[]{:S(2)}) collective-permute-start(f32[1,64,512]{2,1,0:T(8,128)S(1)} %fusion.75), channel_id=1, source_target_pairs={{0,4},{4,8},{8,12},{12,16},{16,20},{20,24},{24,28},{28,32},{32,36}... | collective-permute-start | bytes 393224 | tf_op jit(solution)/shard_map/ppermute | solution.py:25
  527.2 5.5 collective-permute-start.63
  533.0 8.4 %collective-permute-start.64 = (f32[1,64,512]{2,1,0:T(8,128)S(1)}, f32[1,64,512]{2,1,0:T(8,128)S(1)}, u32[]{:S(2)}, u32[]{:S(2)}) collective-permute-start(f32[1,64,512]{2,1,0:T(8,128)S(1)} %fusion.49), channel_id=1, source_target_pairs={{0,4},{4,8},{8,12},{12,16},{16,20},{20,24},{24,28},{28,32},{32,36}... | collective-permute-start | bytes 393224 | tf_op jit(solution)/shard_map/ppermute | solution.py:25
  543.3 5.5 collective-permute-start.66
  551.0 5.5 collective-permute-start.68
  558.6 5.5 collective-permute-start.70
  (46 other events, 382.6 us)
Sparse Core Ops, SparseCore 0:
  269.9 94.8 all-gather.1
where the time goes:
time: 575 us; the launch traced here: 572 us
  waiting for transfers between devices  359 us (62%)
  starting transfers between devices  175 us (30%)
  other arithmetic  18 us (3%)
  between operations  14.8 us (3%)
    ppermute x44, waiting for transfers between devices, extended(): before = lax.ppermute(last, axis, up)  179 us
    all_gather x1, waiting for transfers between devices, per_device(): gathered = lax.all_gather(source_three, 'tm', axis=0, tiled=True)  95 us
    ppermute x44, starting transfers between devices, extended(): after = lax.ppermute(initial, axis, down)  92.7 us
    ppermute x13, waiting for transfers between devices, shifted_2(): return lax.ppermute(array, axis, pairs)  83 us
    ppermute x44, starting transfers between devices, extended(): before = lax.ppermute(last, axis, up)  57.2 us
    ppermute x13, starting transfers between devices, shifted_2(): return lax.ppermute(array, axis, pairs)  25 us
  transfers between devices with their start and end apart: 102, of which 58 were waited for; matrix products, arithmetic and copies ran while one was open for 0% of the time, Pallas kernels for 0%

commit v1 on v0

v1 whole, which is shorter than its diff:
```python
import jax
import jax.numpy as jnp
from jax import lax
from jax.sharding import PartitionSpec as P

FACTOR = 4
E = 32
S0, S1, S2, S3 = 1.0, 4.0, 16.0, 64.0


def wide(v, e):
    pads = [(0, 0)] * (v.ndim - 2) + [(e, e), (0, 0)]
    return jnp.pad(v, pads)


def regrow(v, before, after):
    return wide(v, after - before)


def ring(axis, by):
    n = lax.axis_size(axis)
    return [(i, (i + by) % n) for i in range(n)]


def shift(v, axis, by):
    return lax.ppermute(v, axis, ring(axis, by))


def swap(v, bit):
    n = lax.axis_size("tm")
    return lax.ppermute(v, "tm", [(i, i ^ bit) for i in range(n)])


def per_device(initial, diffusivity, forcing, guessed):
    p = lax.axis_index("tm")
    y = lax.axis_index("space")
    ny = lax.axis_size("space")
    rows = diffusivity.shape[0]
    z, x, c = p // 8, (p // 2) % 4, p % 2
    h = x // 2
    odd = x % 2 == 1
    zero = jnp.float32(0)

    above = shift(diffusivity[rows - E :], "space", 1)
    below = shift(diffusivity[:E], "space", -1)
    above = jnp.where(y == 0, zero, above)
    below = jnp.where(y == ny - 1, zero, below)
    dwide = jnp.concatenate([above, diffusivity, below], 0)

    def step(v, s):
        e = (v.shape[-2] - rows) // 2
        d = dwide[E - e : E + rows + e]
        q = jnp.pad(v, [(0, 0)] * (v.ndim - 2) + [(1, 1), (1, 1)])
        lap = q[..., 2:, 1:-1] + q[..., :-2, 1:-1] + q[..., 1:-1, 2:] + q[..., 1:-1, :-2] - 4.0 * v
        return v + (s * d) * lap

    def steps(v, s, k):
        for _ in range(k):
            v = step(v, s)
        return v

    sources = forcing.reshape((FACTOR, FACTOR) + forcing.shape[1:])
    first = jnp.where(p == 0, initial, zero)[None]
    cur = wide(jnp.concatenate([first, guessed], 0), 8)
    src = wide(jnp.concatenate([sources, jnp.zeros_like(sources[:1])], 0), 8)
    for i in range(FACTOR):
        cur = step(cur, S0) + src[:, i]
    relaxed, gw = cur[:4], cur[4]
    d = relaxed - wide(guessed, 8)
    dw = regrow(d, 8, 16)
    gw16 = regrow(gw, 8, 16)
    xf = step(dw[0], S1) + dw[1]
    xf = step(xf, S1) + dw[2]
    yf = steps(step(dw[3], S1) + gw16, S1, 2)
    xy = steps(jnp.stack([xf, yf]), S0, 4)
    theirs = swap(xy, 1)
    x0 = jnp.where(c == 0, xy[0], theirs[0])
    x1 = jnp.where(c == 0, theirs[0], xy[0])
    y0 = jnp.where(c == 0, xy[1], theirs[1])
    y1 = jnp.where(c == 0, theirs[1], xy[1])
    r = x1 + y0

    even_field = step(step(x0, S2) + r, S2) + y1
    odd_field = steps(step(r, S2) + y1, S2, 2)
    f = jnp.where(odd, jnp.where(c == 0, x0, odd_field), jnp.where(c == 0, even_field, zero))
    role_b = (h == 0) & (c == 0)
    role_t = ((h == 1) & (c == 0)) | ((x == 1) & (c == 1))
    role_a = (x == 3) & (c == 1)

    def to_psi(v):
        g1 = step(v, S3)
        g2 = step(g1, S3)
        return jnp.where(role_b, g2, jnp.where(role_t, g1, v))

    psi = to_psi(f)
    f1 = jnp.where(z >= 1, shift(f, "tm", 8), zero)
    psi2 = jnp.where(z >= 2, shift(psi, "tm", 16), zero)
    q0 = (z == 0) & (x == 0)
    d3gw = shift(jnp.stack([dw[3], gw16])[:, 8:-8], "tm", 1)
    d3gw = jnp.where(p == 0, zero, d3gw)
    ry = shift(jnp.stack([r, y1]), "tm", 2)
    ry = jnp.where(q0, zero, ry)
    rp, yp = ry[0], ry[1]

    psi1 = to_psi(f1)
    u = regrow(psi2, 16, 24)
    u = steps(u, S3, 2) + regrow(psi1, 16, 24)
    u = steps(u, S3, 2) + regrow(psi, 16, 24)
    u2 = jnp.where(z >= 2, shift(u, "tm", 16), zero)
    u5 = jnp.where(z >= 5, shift(u, "tm", 40), zero)
    eps = regrow(u2, 24, 32) + steps(regrow(u5, 24, 32), S3, 6)
    f1w, fw = regrow(f1, 16, 32), regrow(f, 16, 32)
    eps = eps + jnp.where(role_b, f1w, zero)
    tau = jnp.where(role_t, f1w, zero)
    alpha = jnp.where(role_a, f1w, zero)
    b0 = jnp.where(role_b, fw, zero)
    b1 = jnp.where(role_t, fw, zero)
    eps1 = step(eps, S3) + tau
    tau1 = b0 + alpha
    eps2 = step(eps1, S3) + tau1
    tau2 = b1
    zs = steps(jnp.stack([eps, eps1, eps2]), S2, 4) + jnp.stack([tau, tau1, tau2])

    mine = jnp.where(c == 0, zs[:2], zs[1:])
    other = jnp.where(c == 0, zs[1:], zs[:2])
    mine = mine + swap(other, 1)
    keep = jnp.where(h == 0, mine[0], mine[1])
    give = jnp.where(h == 0, mine[1], mine[0])
    keep = keep + swap(give, 4)
    s1 = step(rp, S2) + jnp.where(c == 0, xy[0], x0) + yp
    moved = jnp.where(c == 0, steps(keep, S2, 2), keep)
    give = jnp.where(odd, keep, jnp.where(c == 0, moved + regrow(s1, 16, 32), moved))
    keep = jnp.where(odd, moved, keep) + swap(give, 2)

    n = rows + 2 * E
    from_above = shift(keep[n - 40 :], "space", 1)
    from_below = shift(keep[:40], "space", -1)
    from_above = jnp.where(y == 0, zero, from_above)
    from_below = jnp.where(y == ny - 1, zero, from_below)
    zfull = keep[E - 8 : E + rows + 8] + jnp.concatenate([from_above, from_below], 0)
    zother = swap(zfull, 1)
    qf = jnp.where(c == 0, zfull, zother)
    both = steps(jnp.stack([qf, zfull]), S1, 4)
    q, zn = both[0], both[1]
    qa = step(q, S2)
    e2a = jnp.where(c == 0, q, qa)
    e2b = jnp.where(c == 0, qa, jnp.where(odd, zn, step(qa, S2)))
    t1 = step(e2a, S1)
    t2 = step(t1, S1)
    t3 = step(t2, S1)
    correction = jnp.stack([t1, t2, t3, e2b])[:, 8:-8]

    r24, x024, yp24, rp24 = (regrow(v, 16, 24) for v in (r, x0, yp, rp))
    d3p, gwp = regrow(d3gw[0], 8, 24), regrow(d3gw[1], 8, 24)
    d0 = regrow(d[0], 8, 24) + gwp
    quad = steps(jnp.stack([d3p, d0, regrow(d[1], 8, 24)]), S0, 4)
    a3p, a0, a1 = quad[0], quad[1], quad[2]
    rprev = jnp.where(c == 0, rp24, x024 + yp24)
    rown = jnp.where(c == 0, x024 + yp24, r24)
    pair = steps(jnp.stack([rp24, step(rp24, S2) + x024 + yp24]), S1, 4)
    ea = jnp.where(c == 0, zero, pair[0])
    eb = jnp.where(c == 0, pair[0], jnp.where(odd, zero, pair[1]))
    y_1 = step(rprev + ea, S1) + a3p
    y_2 = step(y_1, S1) + a0
    y_3 = step(y_2, S1) + a1
    rel = regrow(relaxed, 8, 24)
    local = jnp.stack([rel[0] + gwp + y_1, rel[1] + y_2, rel[2] + y_3, rel[3] + rown + eb])
    m = rows + 48
    la = shift(local[:, m - 24 :], "space", 1)
    lb = shift(local[:, :24], "space", -1)
    la = jnp.where(y == 0, zero, la)
    lb = jnp.where(y == ny - 1, zero, lb)
    inner = local[:, 24:-24]
    inner = inner + jnp.pad(la, ((0, 0), (0, rows - 24), (0, 0))) + jnp.pad(lb, ((0, 0), (rows - 24, 0), (0, 0)))
    return inner + correction


def solution(mesh):
    return jax.shard_map(
        per_device,
        mesh=mesh,
        in_specs=(
            P("space", None),
            P("space", None),
            P("tm", "space", None),
            P("tm", "space", None),
        ),
        out_specs=P("tm", "space", None),
        check_vma=False,
    )
```

time: 575 us -> 115 us (0.20)
  the two profiles are of different devices: /device:TPU:56 before, /device:TPU:1 now
where the time goes in v1:
time: 115 us
  waiting for transfers between devices  55.5 us (48%)
  starting transfers between devices  34.3 us (30%)
  other arithmetic  22.6 us (20%)
  local copies, waits for them, and re-layouts  1.82 us (2%)
    ppermute x12, waiting for transfers between devices, shift(): return lax.ppermute(v, axis, ring(axis, by))  39 us
    ppermute x5, starting transfers between devices, swap(): return lax.ppermute(v, 'tm', [(i, i ^ bit) for i in range(n)])  20.2 us
    ppermute x5, waiting for transfers between devices, swap(): return lax.ppermute(v, 'tm', [(i, i ^ bit) for i in range(n)])  16.5 us
    ppermute x12, starting transfers between devices, shift(): return lax.ppermute(v, axis, ring(axis, by))  14 us
    add x30, other arithmetic, step(): return v + s * d * lap  8.5 us
    add x4, other arithmetic, per_device(): cur = step(cur, S0) + src[:, i]  4.72 us
  transfers between devices with their start and end apart: 17, of which 12 were waited for; matrix products, arithmetic and copies ran while one was open for 7% of the time, Pallas kernels for 0%

profile of v1, /device:TPU:1, one launch (start us, length us, event | category | flops | bytes accessed | tf_op | source)
XLA Modules:
  0.0 115.0 jit_solution(7076908348390682797)
XLA Ops:
  0.0 1.0 fusion.447
  1.0 3.6 %collective-permute-start.1 = (f32[32,512]{1,0:T(8,128)S(1)}, f32[32,512]{1,0:T(8,128)S(1)}, u32[]{:S(2)}, u32[]{:S(2)}) collective-permute-start(f32[32,512]{1,0:T(8,128)S(1)} %get-tuple-element.61), channel_id=1, source_target_pairs={{0,3},{1,0},{2,1},{3,2},{4,7},{5,4},{6,5},{7,6},{8,11},{9,8},{10,9... | collective-permute-start | bytes 196616 | tf_op jit(solution)/shard_map/ppermute | solution.py:26
  4.7 2.1 %select_maximum_fusion = f32[5,80,512]{2,1,0:T(8,128)} fusion(f32[4,64,512]{2,1,0:T(8,128)} %param.7, f32[1,64,512]{2,1,0:T(8,128)S(1)} %select_bitcast_fusion.2), kind=kLoop, calls=%fused_computation.95 | loop fusion | flops 1228800 | bytes 1474560 | tf_op jit(solution)/shard_map/concatenate | solution.py:64
  6.8 2.2 %collective-permute-done = f32[32,512]{1,0:T(8,128)S(1)} collective-permute-done((f32[32,512]{1,0:T(8,128)S(1)}, f32[32,512]{1,0:T(8,128)S(1)}, u32[]{:S(2)}, u32[]{:S(2)}) %collective-permute-start) | collective-permute-done | bytes 65568 | tf_op jit(solution)/shard_map/ppermute | solution.py:26
  9.1 3.2 %fusion.6 = f32[5,80,512]{2,1,0:T(8,128)S(1)} fusion(f32[5,80,512]{2,1,0:T(8,128)} %select_maximum_fusion, f32[4,4,64,512]{3,2,1,0:T(8,128)S(1)} %bitcast.171, f32[80,512]{1,0:T(8,128)S(1)} %get-tuple-element.45), kind=kLoop, calls=%fused_computation.69 | loop fusion | flops 1638400 | bytes 3899392 | tf_op jit(solution)/shard_map/add | solution.py:67
  12.3 0.5 fusion.13
  12.8 0.5 fusion.20
  13.4 0.5 fusion.27
  13.9 0.5 copy-done.2
  14.6 0.3 fusion.302
  14.9 0.3 fusion.446
  15.4 0.3 fusion.113
  15.7 0.3 fusion.119
  16.0 0.3 fusion.125
  16.3 3.3 %collective-permute-start.2 = (f32[2,80,512]{2,1,0:T(8,128)S(1)}, f32[2,80,512]{2,1,0:T(8,128)S(1)}, u32[]{:S(2)}, u32[]{:S(2)}) collective-permute-start(f32[2,80,512]{2,1,0:T(8,128)S(1)} %pad_maximum_fusion.9), channel_id=1, source_target_pairs={{0,4},{4,8},{8,12},{12,16},{16,20},{20,24},{24,28},{28,32},{32,36}... | collective-permute-start | bytes 983048 | tf_op jit(solution)/shard_map/ppermute | solution.py:26
  19.5 0.3 fusion.131
  20.0 3.6 %collective-permute-done.2 = f32[2,80,512]{2,1,0:T(8,128)S(1)} collective-permute-done((f32[2,80,512]{2,1,0:T(8,128)S(1)}, f32[2,80,512]{2,1,0:T(8,128)S(1)}, u32[]{:S(2)}, u32[]{:S(2)}) %collective-permute-start.2) | collective-permute-done | bytes 327712 | tf_op jit(solution)/shard_map/ppermute | solution.py:26
  23.7 1.3 %collective-permute-start.4 = (f32[2,96,512]{2,1,0:T(8,128)S(1)}, f32[2,96,512]{2,1,0:T(8,128)S(1)}, u32[]{:S(2)}, u32[]{:S(2)}) collective-permute-start(f32[2,96,512]{2,1,0:T(8,128)S(1)} %pad_maximum_fusion.8), channel_id=1, source_target_pairs={{0,8},{4,12},{8,16},{12,20},{16,24},{20,28},{24,32},{28,36},{32,40... | collective-permute-start | bytes 1179656 | tf_op jit(solution)/shard_map/ppermute | solution.py:26
  25.2 8.6 %collective-permute-done.4 = f32[2,96,512]{2,1,0:T(8,128)S(1)} collective-permute-done((f32[2,96,512]{2,1,0:T(8,128)S(1)}, f32[2,96,512]{2,1,0:T(8,128)S(1)}, u32[]{:S(2)}, u32[]{:S(2)}) %collective-permute-start.4) | collective-permute-done | bytes 393248 | tf_op jit(solution)/shard_map/ppermute | solution.py:26
  34.6 0.3 fusion.350
  34.9 1.2 %collective-permute-start.8 = (f32[96,512]{1,0:T(8,128)S(1)}, f32[96,512]{1,0:T(8,128)S(1)}, u32[]{:S(2)}, u32[]{:S(2)}) collective-permute-start(f32[96,512]{1,0:T(8,128)S(1)} %fusion.350), channel_id=1, source_target_pairs={{0,32},{4,36},{8,40},{12,44},{16,48},{20,52},{24,56},{28,60},{32,6... | collective-permute-start | bytes 589832 | tf_op jit(solution)/shard_map/ppermute | solution.py:26
  36.3 0.4 fusion.63
  36.7 0.4 fusion.69
  37.2 0.4 fusion.75
  37.6 0.4 fusion.81
  38.1 0.3 fusion.89
  38.4 0.3 fusion.95
  38.7 0.3 fusion.101
  39.0 0.3 fusion.107
  39.7 3.4 %collective-permute-done.8 = f32[96,512]{1,0:T(8,128)S(1)} collective-permute-done((f32[96,512]{1,0:T(8,128)S(1)}, f32[96,512]{1,0:T(8,128)S(1)}, u32[]{:S(2)}, u32[]{:S(2)}) %collective-permute-start.8) | collective-permute-done | bytes 196640 | tf_op jit(solution)/shard_map/ppermute | solution.py:26
  43.3 0.3 fusion.391
  44.0 9.3 %collective-permute-done.7 = f32[96,512]{1,0:T(8,128)S(1)} collective-permute-done((f32[96,512]{1,0:T(8,128)S(1)}, f32[96,512]{1,0:T(8,128)S(1)}, u32[]{:S(2)}, u32[]{:S(2)}) %collective-permute-start.7) | collective-permute-done | bytes 196640 | tf_op jit(solution)/shard_map/ppermute | solution.py:26
  53.4 0.3 fusion.258
  54.3 0.8 collective-permute-start.10
  55.1 0.6 collective-permute-start.9
  55.7 8.5 %collective-permute-done.10 = f32[112,512]{1,0:T(8,128)S(1)} collective-permute-done((f32[112,512]{1,0:T(8,128)S(1)}, f32[112,512]{1,0:T(8,128)S(1)}, u32[]{:S(2)}, u32[]{:S(2)}) %collective-permute-start.10) | collective-permute-done | bytes 229408 | tf_op jit(solution)/shard_map/ppermute | solution.py:26
  65.4 0.2 fusion.160
  65.6 0.2 fusion.157
  65.8 0.3 fusion.437
  66.1 0.5 fusion.38
  66.6 0.5 fusion.44
  67.1 0.5 fusion.50
  67.6 0.5 fusion.57
  68.1 16.1 %collective-permute-start.11 = (f32[2,128,512]{2,1,0:T(8,128)S(1)}, f32[2,128,512]{2,1,0:T(8,128)S(1)}, u32[]{:S(2)}, u32[]{:S(2)}) collective-permute-start(f32[2,128,512]{2,1,0:T(8,128)S(1)} %slice_select_fusion), channel_id=1, source_target_pairs={{0,4},{4,0},{8,12},{12,8},{16,20},{20,16},{24,28},{28,24},{32,36},... | collective-permute-start | bytes 1572872 | tf_op jit(solution)/shard_map/ppermute | solution.py:31
  84.2 1.5 %collective-permute-done.11 = f32[2,128,512]{2,1,0:T(8,128)S(1)} collective-permute-done((f32[2,128,512]{2,1,0:T(8,128)S(1)}, f32[2,128,512]{2,1,0:T(8,128)S(1)}, u32[]{:S(2)}, u32[]{:S(2)}) %collective-permute-start.11) | collective-permute-done | bytes 524320 | tf_op jit(solution)/shard_map/ppermute | solution.py:31
  85.9 0.3 collective-permute-start.12
  86.3 9.0 %collective-permute-done.12 = f32[128,512]{1,0:T(8,128)S(1)} collective-permute-done((f32[128,512]{1,0:T(8,128)S(1)}, f32[128,512]{1,0:T(8,128)S(1)}, u32[]{:S(2)}, u32[]{:S(2)}) %collective-permute-start.12) | collective-permute-done | bytes 262176 | tf_op jit(solution)/shard_map/ppermute | solution.py:31
  95.3 0.2 fusion.218
  95.5 0.2 fusion.161
  95.9 0.4 collective-permute-start.6
  96.3 1.1 collective-permute-start.5
  97.5 4.9 %collective-permute-done.13 = f32[128,512]{1,0:T(8,128)S(1)} collective-permute-done((f32[128,512]{1,0:T(8,128)S(1)}, f32[128,512]{1,0:T(8,128)S(1)}, u32[]{:S(2)}, u32[]{:S(2)}) %collective-permute-start.13) | collective-permute-done | bytes 262176 | tf_op jit(solution)/shard_map/ppermute | solution.py:31
  102.5 0.4 collective-permute-start.15
  103.0 1.2 %collective-permute-start.14 = (f32[40,512]{1,0:T(8,128)S(1)}, f32[40,512]{1,0:T(8,128)S(1)}, u32[]{:S(2)}, u32[]{:S(2)}) collective-permute-start(f32[40,512]{1,0:T(8,128)S(1)} %get-tuple-element.46), channel_id=1, source_target_pairs={{0,1},{1,2},{2,3},{3,0},{4,5},{5,6},{6,7},{7,4},{8,9},{9,10},{10,1... | collective-permute-start | bytes 245768 | tf_op jit(solution)/shard_map/ppermute | solution.py:26
  104.2 1.7 %collective-permute-done.15 = f32[40,512]{1,0:T(8,128)S(1)} collective-permute-done((f32[40,512]{1,0:T(8,128)S(1)}, f32[40,512]{1,0:T(8,128)S(1)}, u32[]{:S(2)}, u32[]{:S(2)}) %collective-permute-start.15) | collective-permute-done | bytes 81952 | tf_op jit(solution)/shard_map/ppermute | solution.py:26
  105.9 1.6 %collective-permute-done.14 = f32[40,512]{1,0:T(8,128)S(1)} collective-permute-done((f32[40,512]{1,0:T(8,128)S(1)}, f32[40,512]{1,0:T(8,128)S(1)}, u32[]{:S(2)}, u32[]{:S(2)}) %collective-permute-start.14) | collective-permute-done | bytes 81952 | tf_op jit(solution)/shard_map/ppermute | solution.py:26
  107.6 3.6 %collective-permute-start.16 = (f32[80,512]{1,0:T(8,128)S(1)}, f32[80,512]{1,0:T(8,128)S(1)}, u32[]{:S(2)}, u32[]{:S(2)}) collective-permute-start(f32[80,512]{1,0:T(8,128)S(1)} %slice_add_fusion.1), channel_id=1, source_target_pairs={{0,4},{4,0},{8,12},{12,8},{16,20},{20,16},{24,28},{28,24},{32,36},... | collective-permute-start | bytes 491528 | tf_op jit(solution)/shard_map/ppermute | solution.py:31
  111.2 1.0 collective-permute-done.16
  112.3 0.2 fusion.137
  112.6 0.2 fusion.143
  112.8 0.2 fusion.149
  113.1 0.2 fusion.155
  113.8 0.2 fusion.427
  114.1 0.9 fusion.82
  (81 shorter events, 5.8 us)
Async XLA Ops:
  0.0 9.0 %copy-start.1 = (f32[64,512]{1,0:T(8,128)S(1)}, f32[64,512]{1,0:T(8,128)}, u32[]{:S(2)}) copy-start(f32[64,512]{1,0:T(8,128)} %param.5) | copy-start | bytes 393220
  0.0 9.1 %copy-start = (f32[16,64,512]{2,1,0:T(8,128)S(1)}, f32[16,64,512]{2,1,0:T(8,128)}, u32[]{:S(2)}) copy-start(f32[16,64,512]{2,1,0:T(8,128)} %param.6) | copy-start | bytes 6291460
  1.0 5.7 %collective-permute-start.1 = (f32[32,512]{1,0:T(8,128)S(1)}, f32[32,512]{1,0:T(8,128)S(1)}, u32[]{:S(2)}, u32[]{:S(2)}) collective-permute-start(f32[32,512]{1,0:T(8,128)S(1)} %get-tuple-element.61), channel_id=1, source_target_pairs={{0,3},{1,0},{2,1},{3,2},{4,7},{5,4},{6,5},{7,6},{8,11},{9,8},{10,9... | collective-permute-start | bytes 196616 | tf_op jit(solution)/shard_map/ppermute | solution.py:26
  4.7 4.3 %collective-permute-start = (f32[32,512]{1,0:T(8,128)S(1)}, f32[32,512]{1,0:T(8,128)S(1)}, u32[]{:S(2)}, u32[]{:S(2)}) collective-permute-start(f32[32,512]{1,0:T(8,128)S(1)} %get-tuple-element.60), channel_id=1, source_target_pairs={{0,1},{1,2},{2,3},{3,0},{4,5},{5,6},{6,7},{7,4},{8,9},{9,10},{10,1... | collective-permute-start | bytes 196616 | tf_op jit(solution)/shard_map/ppermute | solution.py:26
  13.4 1.0 copy-start.2
  16.3 7.3 %collective-permute-start.2 = (f32[2,80,512]{2,1,0:T(8,128)S(1)}, f32[2,80,512]{2,1,0:T(8,128)S(1)}, u32[]{:S(2)}, u32[]{:S(2)}) collective-permute-start(f32[2,80,512]{2,1,0:T(8,128)S(1)} %pad_maximum_fusion.9), channel_id=1, source_target_pairs={{0,4},{4,8},{8,12},{12,16},{16,20},{20,24},{24,28},{28,32},{32,36}... | collective-permute-start | bytes 983048 | tf_op jit(solution)/shard_map/ppermute | solution.py:26
  19.8 3.8 %collective-permute-start.3 = (f32[2,96,512]{2,1,0:T(8,128)S(1)}, f32[2,96,512]{2,1,0:T(8,128)S(1)}, u32[]{:S(2)}, u32[]{:S(2)}) collective-permute-start(f32[2,96,512]{2,1,0:T(8,128)S(1)} %fusion.131), channel_id=1, source_target_pairs={{0,4},{4,0},{8,12},{12,8},{16,20},{20,16},{24,28},{28,24},{32,36},... | collective-permute-start | bytes 1179656 | tf_op jit(solution)/shard_map/ppermute | solution.py:31
  23.7 10.0 %collective-permute-start.4 = (f32[2,96,512]{2,1,0:T(8,128)S(1)}, f32[2,96,512]{2,1,0:T(8,128)S(1)}, u32[]{:S(2)}, u32[]{:S(2)}) collective-permute-start(f32[2,96,512]{2,1,0:T(8,128)S(1)} %pad_maximum_fusion.8), channel_id=1, source_target_pairs={{0,8},{4,12},{8,16},{12,20},{16,24},{20,28},{24,32},{28,36},{32,40... | collective-permute-start | bytes 1179656 | tf_op jit(solution)/shard_map/ppermute | solution.py:26
  34.9 8.2 %collective-permute-start.8 = (f32[96,512]{1,0:T(8,128)S(1)}, f32[96,512]{1,0:T(8,128)S(1)}, u32[]{:S(2)}, u32[]{:S(2)}) collective-permute-start(f32[96,512]{1,0:T(8,128)S(1)} %fusion.350), channel_id=1, source_target_pairs={{0,32},{4,36},{8,40},{12,44},{16,48},{20,52},{24,56},{28,60},{32,6... | collective-permute-start | bytes 589832 | tf_op jit(solution)/shard_map/ppermute | solution.py:26
  43.8 9.6 %collective-permute-start.7 = (f32[96,512]{1,0:T(8,128)S(1)}, f32[96,512]{1,0:T(8,128)S(1)}, u32[]{:S(2)}, u32[]{:S(2)}) collective-permute-start(f32[96,512]{1,0:T(8,128)S(1)} %fusion.378), channel_id=1, source_target_pairs={{0,64},{4,68},{8,72},{12,76},{16,80},{20,84},{24,88},{28,92},{32,9... | collective-permute-start | bytes 589832 | tf_op jit(solution)/shard_map/ppermute | solution.py:26
  54.3 9.9 %collective-permute-start.10 = (f32[112,512]{1,0:T(8,128)S(1)}, f32[112,512]{1,0:T(8,128)S(1)}, u32[]{:S(2)}, u32[]{:S(2)}) collective-permute-start(f32[112,512]{1,0:T(8,128)S(1)} %fusion.284), channel_id=1, source_target_pairs={{0,160},{4,164},{8,168},{12,172},{16,176},{20,180},{24,184},{28,18... | collective-permute-start | bytes 688136 | tf_op jit(solution)/shard_map/ppermute | solution.py:26
  55.1 10.2 %collective-permute-start.9 = (f32[112,512]{1,0:T(8,128)S(1)}, f32[112,512]{1,0:T(8,128)S(1)}, u32[]{:S(2)}, u32[]{:S(2)}) collective-permute-start(f32[112,512]{1,0:T(8,128)S(1)} %fusion.284), channel_id=1, source_target_pairs={{0,64},{4,68},{8,72},{12,76},{16,80},{20,84},{24,88},{28,92},{32,9... | collective-permute-start | bytes 688136 | tf_op jit(solution)/shard_map/ppermute | solution.py:26
  68.1 17.6 %collective-permute-start.11 = (f32[2,128,512]{2,1,0:T(8,128)S(1)}, f32[2,128,512]{2,1,0:T(8,128)S(1)}, u32[]{:S(2)}, u32[]{:S(2)}) collective-permute-start(f32[2,128,512]{2,1,0:T(8,128)S(1)} %slice_select_fusion), channel_id=1, source_target_pairs={{0,4},{4,0},{8,12},{12,8},{16,20},{20,16},{24,28},{28,24},{32,36},... | collective-permute-start | bytes 1572872 | tf_op jit(solution)/shard_map/ppermute | solution.py:31
  85.9 9.3 %collective-permute-start.12 = (f32[128,512]{1,0:T(8,128)S(1)}, f32[128,512]{1,0:T(8,128)S(1)}, u32[]{:S(2)}, u32[]{:S(2)}) collective-permute-start(f32[128,512]{1,0:T(8,128)S(1)} %select_bitcast_fusion), channel_id=1, source_target_pairs={{0,16},{4,20},{8,24},{12,28},{16,0},{20,4},{24,8},{28,12},{32,48},... | collective-permute-start | bytes 786440 | tf_op jit(solution)/shard_map/ppermute | solution.py:31
  95.8 6.7 %collective-permute-start.13 = (f32[128,512]{1,0:T(8,128)S(1)}, f32[128,512]{1,0:T(8,128)S(1)}, u32[]{:S(2)}, u32[]{:S(2)}) collective-permute-start(f32[128,512]{1,0:T(8,128)S(1)} %get-tuple-element.11), channel_id=1, source_target_pairs={{0,8},{4,12},{8,0},{12,4},{16,24},{20,28},{24,16},{28,20},{32,40},... | collective-permute-start | bytes 786440 | tf_op jit(solution)/shard_map/ppermute | solution.py:31
  95.9 7.0 %collective-permute-start.6 = (f32[4,24,512]{2,1,0:T(8,128)S(1)}, f32[4,24,512]{2,1,0:T(8,128)S(1)}, u32[]{:S(2)}, u32[]{:S(2)}) collective-permute-start(f32[4,24,512]{2,1,0:T(8,128)S(1)} %get-tuple-element.18), channel_id=1, source_target_pairs={{0,3},{1,0},{2,1},{3,2},{4,7},{5,4},{6,5},{7,6},{8,11},{9,8},{10,9... | collective-permute-start | bytes 589832 | tf_op jit(solution)/shard_map/ppermute | solution.py:26
  96.3 14.9 %collective-permute-start.5 = (f32[4,24,512]{2,1,0:T(8,128)S(1)}, f32[4,24,512]{2,1,0:T(8,128)S(1)}, u32[]{:S(2)}, u32[]{:S(2)}) collective-permute-start(f32[4,24,512]{2,1,0:T(8,128)S(1)} %get-tuple-element.17), channel_id=1, source_target_pairs={{0,1},{1,2},{2,3},{3,0},{4,5},{5,6},{6,7},{7,4},{8,9},{9,10},{10,1... | collective-permute-start | bytes 589832 | tf_op jit(solution)/shard_map/ppermute | solution.py:26
  102.5 3.4 %collective-permute-start.15 = (f32[40,512]{1,0:T(8,128)S(1)}, f32[40,512]{1,0:T(8,128)S(1)}, u32[]{:S(2)}, u32[]{:S(2)}) collective-permute-start(f32[40,512]{1,0:T(8,128)S(1)} %get-tuple-element.47), channel_id=1, source_target_pairs={{0,3},{1,0},{2,1},{3,2},{4,7},{5,4},{6,5},{7,6},{8,11},{9,8},{10,9... | collective-permute-start | bytes 245768 | tf_op jit(solution)/shard_map/ppermute | solution.py:26
  103.0 4.6 %collective-permute-start.14 = (f32[40,512]{1,0:T(8,128)S(1)}, f32[40,512]{1,0:T(8,128)S(1)}, u32[]{:S(2)}, u32[]{:S(2)}) collective-permute-start(f32[40,512]{1,0:T(8,128)S(1)} %get-tuple-element.46), channel_id=1, source_target_pairs={{0,1},{1,2},{2,3},{3,0},{4,5},{5,6},{6,7},{7,4},{8,9},{9,10},{10,1... | collective-permute-start | bytes 245768 | tf_op jit(solution)/shard_map/ppermute | solution.py:26
  107.6 4.7 %collective-permute-start.16 = (f32[80,512]{1,0:T(8,128)S(1)}, f32[80,512]{1,0:T(8,128)S(1)}, u32[]{:S(2)}, u32[]{:S(2)}) collective-permute-start(f32[80,512]{1,0:T(8,128)S(1)} %slice_add_fusion.1), channel_id=1, source_target_pairs={{0,4},{4,0},{8,12},{12,8},{16,20},{20,16},{24,28},{28,24},{32,36},... | collective-permute-start | bytes 491528 | tf_op jit(solution)/shard_map/ppermute | solution.py:31

commit v2 on v1

v2 whole, which is shorter than its diff:
```python
import jax
import jax.numpy as jnp
from jax import lax
from jax.sharding import PartitionSpec as P

FACTOR = 4
E = 32
EDGE = 64
S0, S1, S2, S3 = 1.0, 4.0, 16.0, 64.0


def wide(v, e):
    return jnp.pad(v, [(0, 0)] * (v.ndim - 2) + [(e, e), (0, 0)])


def regrow(v, before, after):
    return wide(v, after - before)


def edged(v):
    return jnp.pad(v, [(0, 0)] * (v.ndim - 1) + [(EDGE, EDGE)])


def shift(v, axis, by):
    n = lax.axis_size(axis)
    return lax.ppermute(v, axis, [(i, (i + by) % n) for i in range(n)])


def swap(v, bit):
    n = lax.axis_size("tm")
    return lax.ppermute(v, "tm", [(i, i ^ bit) for i in range(n)])


def hold(*values):
    return lax.optimization_barrier(values)


def step(v, d, s):
    q = jnp.pad(v, [(0, 0)] * (v.ndim - 2) + [(1, 1), (1, 1)])
    lap = q[..., 2:, 1:-1] + q[..., :-2, 1:-1] + q[..., 1:-1, 2:] + q[..., 1:-1, :-2] - 4.0 * v
    return v + (s * d) * lap


def steps(v, d, s, k):
    for _ in range(k):
        v = step(v, d, s)
    return v


def per_device(initial, diffusivity, forcing, guessed):
    p = lax.axis_index("tm")
    y = lax.axis_index("space")
    ny = lax.axis_size("space")
    rows, columns = diffusivity.shape
    z, x, c = p // 8, (p // 2) % 4, p % 2
    h = x // 2
    odd = x % 2 == 1
    core0 = c == 0
    zero = jnp.float32(0)

    sources = forcing.reshape((FACTOR, FACTOR) + forcing.shape[1:])
    first = jnp.where(p == 0, initial, zero)[None]
    cur = wide(jnp.concatenate([first, guessed], 0), 8)
    src = wide(jnp.concatenate([sources, jnp.zeros_like(sources[:1])], 0), 8)
    above = shift(diffusivity[rows - E :], "space", 1)
    below = shift(diffusivity[:E], "space", -1)
    above, below, cur, src = hold(above, below, cur, src)
    above = jnp.where(y == 0, zero, above)
    below = jnp.where(y == ny - 1, zero, below)
    dwide = jnp.concatenate([above, diffusivity, below], 0)

    def dext(e):
        return dwide[E - e : E + rows + e]

    for i in range(FACTOR):
        cur = step(cur, dext(8), S0) + src[:, i]
    relaxed, gw = cur[:4], cur[4]
    d = relaxed - wide(guessed, 8)
    dw = regrow(d, 8, 16)
    gw16 = regrow(gw, 8, 16)
    d16 = dext(16)
    xf = step(dw[0], d16, S1) + dw[1]
    xf = step(xf, d16, S1) + dw[2]
    yf = steps(step(dw[3], d16, S1) + gw16, d16, S1, 2)
    xy = steps(jnp.stack([xf, yf]), d16, S0, 4)
    theirs = swap(xy, 1)

    dpad = edged(dwide)
    dhalf = jnp.where(core0, dpad[:, :384], dpad[:, 256:])
    dquarter = jnp.where(odd, dhalf[:, 128:], dhalf[:, :256])

    def half(v):
        w = edged(v)
        return jnp.where(core0, w[..., :384], w[..., 256:])

    mine_h, theirs_h = half(xy), half(theirs)
    x0 = jnp.where(core0, mine_h[0], theirs_h[0])
    x1 = jnp.where(core0, theirs_h[0], mine_h[0])
    y0 = jnp.where(core0, mine_h[1], theirs_h[1])
    y1 = jnp.where(core0, theirs_h[1], mine_h[1])
    r = x1 + y0
    dh = dhalf[E - 16 : E + rows + 16]
    t = step(jnp.where(odd, r, x0), dh, S2) + jnp.where(odd, y1, r)
    t = step(t, dh, S2)
    f1 = jnp.where(odd, x0, t + y1)
    f2 = jnp.where(odd, step(t, dh, S2), zero)
    ff = jnp.stack([f1, f2])
    keep = jnp.where(odd, ff[..., 128:], ff[..., :256])
    give = jnp.where(odd, ff[..., :256], ff[..., 128:])
    keep = keep + swap(give, 2)

    def dq(e):
        return dquarter[E - e : E + rows + e]

    def to_psi(v):
        g = step(v[0], dq(16), S3) + v[1]
        return jnp.where(h == 0, step(g, dq(16), S3), g)

    psi = to_psi(keep)
    xy0 = jnp.where(core0, xy, theirs)
    xy1 = jnp.where(core0, theirs, xy)
    rfull = xy1[0] + xy0[1]
    ry = jnp.where(core0, rfull, xy[1])
    before, psi2, ry = hold(shift(keep, "tm", 8), shift(psi, "tm", 16), shift(ry, "tm", 2))
    before = jnp.where(z >= 1, before, zero)
    psi2 = jnp.where(z >= 2, psi2, zero)
    psi1 = to_psi(before)
    u = steps(regrow(psi2, 16, 24), dq(24), S3, 2) + regrow(psi1, 16, 24)
    u = steps(u, dq(24), S3, 2) + regrow(psi, 16, 24)
    u2, u5, d3gw, ry2 = hold(
        shift(u, "tm", 16),
        shift(u, "tm", 40),
        shift(jnp.stack([dw[3], gw16])[:, 8:-8], "tm", 1),
        swap(ry, 1),
    )
    u2 = jnp.where(z >= 2, u2, zero)
    u5 = jnp.where(z >= 5, u5, zero)
    q0 = (z == 0) & (x == 0)
    d3gw = jnp.where(p == 0, zero, d3gw)
    rp = jnp.where(q0, zero, jnp.where(core0, ry, ry2))
    yp = jnp.where(q0, zero, jnp.where(core0, ry2, ry))
    s1 = step(rp, d16, S2) + xy0[0] + yp

    dz = dq(32)
    eps = regrow(u2, 24, 32) + steps(regrow(u5, 24, 32), dz, S3, 6)
    bw, kw = regrow(before, 16, 32), regrow(keep, 16, 32)
    low = h == 0
    eps = eps + jnp.where(low, bw[0], zero)
    tau = jnp.where(low, bw[1], bw[0])
    alpha = jnp.where(low, zero, bw[1])
    b0 = jnp.where(low, kw[0], zero)
    tau2 = jnp.where(low, kw[1], kw[0])
    eps1 = step(eps, dz, S3) + tau
    tau1 = b0 + alpha
    eps2 = step(eps1, dz, S3) + tau1
    zs = steps(jnp.stack([eps, eps1, eps2]), dz, S2, 4) + jnp.stack([tau, tau1, tau2])
    zs = zs[..., EDGE:-EDGE]
    keep = jnp.where(low, zs[:2], zs[1:])
    give = jnp.where(low, zs[1:], zs[:2])
    other, s1x = hold(swap(give, 4), swap(s1, 2))
    keep = keep + other

    def r24(v):
        return regrow(v, 16, 24)

    d24 = dext(24)
    s1q = jnp.where(odd, r24(s1x), zero)
    d3p, gwp = regrow(d3gw[0], 8, 24), regrow(d3gw[1], 8, 24)
    d0 = regrow(d[0], 8, 24) + gwp
    quad = steps(jnp.stack([d3p, d0, regrow(d[1], 8, 24)]), d24, S0, 4)
    a3p, a0, a1 = quad[0], quad[1], quad[2]
    rprev = jnp.where(core0, r24(rp), r24(xy0[0] + yp))
    rown = jnp.where(core0, r24(xy0[0] + yp), r24(rfull))
    ea = jnp.where(core0, s1q, step(s1q, d24, S2) + r24(rp))
    eb = step(ea, d24, S2) + rprev
    eb = jnp.where(odd & (c == 1), zero, eb)
    pair = steps(jnp.stack([ea, eb]), d24, S1, 4)
    y_1 = step(rprev + pair[0], d24, S1) + a3p
    y_2 = step(y_1, d24, S1) + a0
    y_3 = step(y_2, d24, S1) + a1
    rel = regrow(relaxed, 8, 24)
    local = jnp.stack([rel[0] + gwp + y_1, rel[1] + y_2, rel[2] + y_3, rel[3] + rown + pair[1]])

    n = rows + 2 * E
    from_above, from_below = hold(
        shift(keep[:, n - 48 :], "space", 1), shift(keep[:, :48], "space", -1)
    )
    from_above = jnp.where(y == 0, zero, from_above)
    from_below = jnp.where(y == ny - 1, zero, from_below)
    keep = keep[:, 16:-16] + jnp.concatenate([from_above, from_below], 1)
    m = rows + 48
    other, la, lb = hold(
        swap(keep, 2), shift(local[:, m - 24 :], "space", 1), shift(local[:, :24], "space", -1)
    )
    keep = jnp.where(odd, jnp.concatenate([other, keep], 2), jnp.concatenate([keep, other], 2))
    other = swap(keep, 1)
    both = jnp.where(
        core0, jnp.concatenate([keep, other], 2), jnp.concatenate([other, keep], 2)
    )
    both = steps(both, d16, S1, 4)
    q, zn = both[0], both[1]
    q = jnp.where(odd, steps(q, d16, S2, 2), q)
    q = jnp.where(core0, q, step(q, d16, S2))
    e2b = jnp.where(odd & (c == 1), zn, step(q, d16, S2))
    t1 = step(q, d16, S1)
    t2 = step(t1, d16, S1)
    t3 = step(t2, d16, S1)
    correction = jnp.stack([t1, t2, t3, e2b])[:, 16:-16]

    la = jnp.where(y == 0, zero, la)
    lb = jnp.where(y == ny - 1, zero, lb)
    inner = local[:, 24:-24]
    inner = (
        inner
        + jnp.pad(la, ((0, 0), (0, rows - 24), (0, 0)))
        + jnp.pad(lb, ((0, 0), (rows - 24, 0), (0, 0)))
    )
    return inner + correction


def solution(mesh):
    return jax.shard_map(
        per_device,
        mesh=mesh,
        in_specs=(
            P("space", None),
            P("space", None),
            P("tm", "space", None),
            P("tm", "space", None),
        ),
        out_specs=P("tm", "space", None),
        check_vma=False,
    )
```

time: 115 us -> 90.8 us (0.79)
  waiting for transfers between devices: 55.5 us -> 29.8 us
  local copies, waits for them, and re-layouts: 1.82 us -> 3.77 us
  starting transfers between devices: 34.3 us -> 32.4 us
    ppermute x12, waiting for transfers between devices: 39 us -> 16.3 us  [shift(): return lax.ppermute(v, axis, [(i, (i + by) % n) for i in range(n)])]
    ppermute x5 -> x7, starting transfers between devices: 20.2 us -> 11.2 us  [swap(): return lax.ppermute(v, 'tm', [(i, i ^ bit) for i in range(n)])]
    ppermute x12, starting transfers between devices: 14 us -> 21.2 us  [shift(): return lax.ppermute(v, axis, [(i, (i + by) % n) for i in range(n)])]
    ppermute x5 -> x7, waiting for transfers between devices: 16.5 us -> 13.5 us  [swap(): return lax.ppermute(v, 'tm', [(i, i ^ bit) for i in range(n)])]
    pad x2 -> x3, local copies, waits for them, and re-layouts: 0.04 us -> 2.04 us  [wide(): return jnp.pad(v, [(0, 0)] * (v.ndim - 2) + [(e, e), (0, 0)])]
    add x30 -> x29, other arithmetic: 8.5 us -> 7.54 us  [step(): return v + s * d * lap]
    add x19 -> x17, other arithmetic: 7.34 us -> 6.54 us  [the longest x4 4.9 us: per_device(): cur = step(cur, dext(8), S0) + src[:, i]]
  transfers between devices with their start and end apart: 17 -> 19, of which waited for: 12 -> 9; matrix products, arithmetic and copies ran while one was open for 7% -> 12% of each run, Pallas kernels for 0% -> 0%
where the time goes in v2:
time: 90.8 us; the launch traced here: 90.4 us
  starting transfers between devices  32.4 us (36%)
  waiting for transfers between devices  29.8 us (33%)
  other arithmetic  23.6 us (26%)
  local copies, waits for them, and re-layouts  3.77 us (4%)
    ppermute x12, starting transfers between devices, shift(): return lax.ppermute(v, axis, [(i, (i + by) % n) for i in range(n)])  21.2 us
    ppermute x12, waiting for transfers between devices, shift(): return lax.ppermute(v, axis, [(i, (i + by) % n) for i in range(n)])  16.3 us
    ppermute x7, waiting for transfers between devices, swap(): return lax.ppermute(v, 'tm', [(i, i ^ bit) for i in range(n)])  13.5 us
    ppermute x7, starting transfers between devices, swap(): return lax.ppermute(v, 'tm', [(i, i ^ bit) for i in range(n)])  11.2 us
    add x29, other arithmetic, step(): return v + s * d * lap  7.54 us
    add x4, other arithmetic, per_device(): cur = step(cur, dext(8), S0) + src[:, i]  4.9 us
    concatenate x1, other arithmetic, per_device(): cur = wide(jnp.concatenate([first, guessed], 0), 8)  2.05 us
    pad x3, local copies, waits for them, and re-layouts, wide(): return jnp.pad(v, [(0, 0)] * (v.ndim - 2) + [(e, e), (0, 0)])  2.04 us
  transfers between devices with their start and end apart: 19, of which 9 were waited for; matrix products, arithmetic and copies ran while one was open for 12% of the time, Pallas kernels for 0%

profile of v2, /device:TPU:1, one launch (start us, length us, event | category | flops | bytes accessed | tf_op | source)
XLA Modules:
  0.0 90.4 jit_solution(3670112724845430055)
XLA Ops:
  0.0 1.5 %fusion.432 = (f32[32,512]{1,0:T(8,128)S(1)}, f32[32,512]{1,0:T(8,128)}) fusion(f32[64,512]{1,0:T(8,128)} %param.5), kind=kLoop, calls=%fused_computation.777 | loop fusion | bytes 262144 | tf_op jit(solution)/shard_map/slice | solution.py:66
  1.5 2.1 %collective-permute-start = (f32[32,512]{1,0:T(8,128)}, f32[32,512]{1,0:T(8,128)S(1)}, u32[]{:S(2)}, u32[]{:S(2)}) collective-permute-start(f32[32,512]{1,0:T(8,128)} %get-tuple-element.87), channel_id=1, source_target_pairs={{0,1},{1,2},{2,3},{3,0},{4,5},{5,6},{6,7},{7,4},{8,9},{9,10},{10,1... | collective-permute-start | bytes 196616 | tf_op jit(solution)/shard_map/ppermute | solution.py:26
  3.6 1.4 %collective-permute-start.1 = (f32[32,512]{1,0:T(8,128)S(1)}, f32[32,512]{1,0:T(8,128)}, u32[]{:S(2)}, u32[]{:S(2)}) collective-permute-start(f32[32,512]{1,0:T(8,128)S(1)} %get-tuple-element.86), channel_id=1, source_target_pairs={{0,3},{1,0},{2,1},{3,2},{4,7},{5,4},{6,5},{7,6},{8,11},{9,8},{10,9... | collective-permute-start | bytes 196616 | tf_op jit(solution)/shard_map/ppermute | solution.py:26
  5.1 2.1 %select_maximum_fusion = f32[5,80,512]{2,1,0:T(8,128)} fusion(f32[4,64,512]{2,1,0:T(8,128)} %param.7, f32[1,64,512]{2,1,0:T(8,128)S(1)} %select_bitcast_fusion), kind=kLoop, calls=%fused_computation.90 | loop fusion | flops 1228800 | bytes 1474560 | tf_op jit(solution)/shard_map/concatenate | solution.py:63
  7.1 2.0 %pad.416 = f32[5,4,80,512]{3,2,1,0:T(8,128)S(1)} pad(f32[4,4,64,512]{3,2,1,0:T(8,128)} %bitcast.172, f32[]{:T(128)} %constant.82.clone.1), padding=0_1x0_0x8_8x0_0 | pad | bytes 5373956 | tf_op jit(solution)/shard_map/jit(_pad)/pad | solution.py:13
  9.2 0.9 broadcast_select_fusion.8
  10.1 0.9 %pad_maximum_fusion.9 = f32[128,512]{1,0:T(8,128)S(1)} fusion(f32[32,512]{1,0:T(8,128)S(1)} %get-tuple-element.88, f32[64,512]{1,0:T(8,128)} %param.5, f32[32,512]{1,0:T(8,128)S(1)} %get-tuple-element.89), kind=kLoop, calls=%fused_computation.401 | loop fusion | flops 131072 | bytes 524288 | tf_op jit(solution)/shard_map/concatenate | solution.py:70
  11.0 3.4 %fusion.6 = f32[5,80,512]{2,1,0:T(8,128)S(1)} fusion(f32[5,80,512]{2,1,0:T(8,128)} %select_maximum_fusion, f32[80,512]{1,0:T(8,128)S(1)} %slice.1264, f32[5,4,80,512]{3,2,1,0:T(8,128)S(1)} %pad.416), kind=kLoop, calls=%fused_computation.65 | loop fusion | flops 1638400 | bytes 2621440 | tf_op jit(solution)/shard_map/add | solution.py:76
  14.4 0.5 fusion.13
  14.9 0.5 fusion.20
  15.4 0.5 fusion.27
  16.2 0.3 fusion.430
  16.5 2.3 %collective-permute-start.9 = (f32[2,80,512]{2,1,0:T(8,128)S(1)}, f32[2,80,512]{2,1,0:T(8,128)S(1)}, u32[]{:S(2)}, u32[]{:S(2)}) collective-permute-start(f32[2,80,512]{2,1,0:T(8,128)S(1)} %pad_maximum_fusion.8), channel_id=1, source_target_pairs={{0,4},{4,8},{8,12},{12,16},{16,20},{20,24},{24,28},{28,32},{32,36}... | collective-permute-start | bytes 983048 | tf_op jit(solution)/shard_map/ppermute | solution.py:26
  18.8 0.3 fusion.221
  19.3 0.3 fusion.84
  19.6 0.3 fusion.90
  19.9 0.3 fusion.96
  20.2 0.3 fusion.102
  20.5 1.6 %collective-permute-start.2 = (f32[2,96,512]{2,1,0:T(8,128)S(1)}, f32[2,96,512]{2,1,0:T(8,128)S(1)}, u32[]{:S(2)}, u32[]{:S(2)}) collective-permute-start(f32[2,96,512]{2,1,0:T(8,128)S(1)} %fusion.102), channel_id=1, source_target_pairs={{0,4},{4,0},{8,12},{12,8},{16,20},{20,16},{24,28},{28,24},{32,36},... | collective-permute-start | bytes 1179656 | tf_op jit(solution)/shard_map/ppermute | solution.py:31
  22.3 0.2 fusion.152
  22.6 0.9 collective-permute-done.2
  23.5 0.2 fusion.153
  24.3 0.3 broadcast_select_fusion
  24.7 1.5 %collective-permute-start.6 = (f32[96,512]{1,0:T(8,128)S(1)}, f32[96,512]{1,0:T(8,128)S(1)}, u32[]{:S(2)}, u32[]{:S(2)}) collective-permute-start(f32[96,512]{1,0:T(8,128)S(1)} %get-tuple-element.51), channel_id=1, source_target_pairs={{0,8},{4,12},{8,16},{12,20},{16,24},{20,28},{24,32},{28,36},{32,40... | collective-permute-start | bytes 589832 | tf_op jit(solution)/shard_map/ppermute | solution.py:26
  26.2 4.2 %collective-permute-done.3 = f32[2,96,256]{2,1,0:T(8,128)S(1)} collective-permute-done((f32[2,96,256]{2,1,0:T(8,128)S(1)}, f32[2,96,256]{2,1,0:T(8,128)S(1)}, u32[]{:S(2)}, u32[]{:S(2)}) %collective-permute-start.3) | collective-permute-done | bytes 196640 | tf_op jit(solution)/shard_map/ppermute | solution.py:31
  30.5 0.8 collective-permute-start.4
  31.5 3.2 %collective-permute-start.5 = (f32[96,256]{1,0:T(8,128)S(1)}, f32[96,256]{1,0:T(8,128)S(1)}, u32[]{:S(2)}, u32[]{:S(2)}) collective-permute-start(f32[96,256]{1,0:T(8,128)S(1)} %add_select_fusion.2), channel_id=1, source_target_pairs={{0,64},{4,68},{8,72},{12,76},{16,80},{20,84},{24,88},{28,92},{32,9... | collective-permute-start | bytes 294920 | tf_op jit(solution)/shard_map/ppermute | solution.py:26
  34.8 1.7 %collective-permute-done.6 = f32[96,512]{1,0:T(8,128)S(1)} collective-permute-done((f32[96,512]{1,0:T(8,128)S(1)}, f32[96,512]{1,0:T(8,128)S(1)}, u32[]{:S(2)}, u32[]{:S(2)}) %collective-permute-start.6) | collective-permute-done | bytes 196640 | tf_op jit(solution)/shard_map/ppermute | solution.py:26
  36.5 6.4 %collective-permute-done.5 = f32[96,256]{1,0:T(8,128)S(1)} collective-permute-done((f32[96,256]{1,0:T(8,128)S(1)}, f32[96,256]{1,0:T(8,128)S(1)}, u32[]{:S(2)}, u32[]{:S(2)}) %collective-permute-start.5) | collective-permute-done | bytes 98336 | tf_op jit(solution)/shard_map/ppermute | solution.py:26
  43.6 2.6 %collective-permute-start.10 = (f32[96,512]{1,0:T(8,128)S(1)}, f32[96,512]{1,0:T(8,128)S(1)}, u32[]{:S(2)}, u32[]{:S(2)}) collective-permute-start(f32[96,512]{1,0:T(8,128)S(1)} %collective-permute-done.6), channel_id=1, source_target_pairs={{0,4},{4,0},{8,12},{12,8},{16,20},{20,16},{24,28},{28,24},{32,36},... | collective-permute-start | bytes 589832 | tf_op jit(solution)/shard_map/ppermute | solution.py:31
  46.5 4.0 %collective-permute-start.8 = (f32[112,256]{1,0:T(8,128)S(1)}, f32[112,256]{1,0:T(8,128)S(1)}, u32[]{:S(2)}, u32[]{:S(2)}) collective-permute-start(f32[112,256]{1,0:T(8,128)S(1)} %fusion.395), channel_id=1, source_target_pairs={{0,160},{4,164},{8,168},{12,172},{16,176},{20,180},{24,184},{28,18... | collective-permute-start | bytes 344072 | tf_op jit(solution)/shard_map/ppermute | solution.py:26
  50.4 5.3 %collective-permute-done.7 = f32[112,256]{1,0:T(8,128)S(1)} collective-permute-done((f32[112,256]{1,0:T(8,128)S(1)}, f32[112,256]{1,0:T(8,128)S(1)}, u32[]{:S(2)}, u32[]{:S(2)}) %collective-permute-start.7) | collective-permute-done | bytes 114720 | tf_op jit(solution)/shard_map/ppermute | solution.py:26
  55.8 2.9 %collective-permute-done.8 = f32[112,256]{1,0:T(8,128)S(1)} collective-permute-done((f32[112,256]{1,0:T(8,128)S(1)}, f32[112,256]{1,0:T(8,128)S(1)}, u32[]{:S(2)}, u32[]{:S(2)}) %collective-permute-start.8) | collective-permute-done | bytes 114720 | tf_op jit(solution)/shard_map/ppermute | solution.py:26
  58.7 0.2 fusion.292
  58.9 1.0 %collective-permute-start.12 = (f32[96,512]{1,0:T(8,128)S(1)}, f32[96,512]{1,0:T(8,128)S(1)}, u32[]{:S(2)}, u32[]{:S(2)}) collective-permute-start(f32[96,512]{1,0:T(8,128)S(1)} %get-tuple-element.62), channel_id=1, source_target_pairs={{0,8},{4,12},{8,0},{12,4},{16,24},{20,28},{24,16},{28,20},{32,40},... | collective-permute-start | bytes 589832 | tf_op jit(solution)/shard_map/ppermute | solution.py:31
  61.1 0.3 fusion.132
  61.4 0.3 fusion.138
  61.7 0.3 fusion.144
  62.0 0.3 fusion.151
  62.4 1.0 %collective-permute-start.11 = (f32[2,128,128]{2,1,0:T(8,128)S(1)}, f32[2,128,128]{2,1,0:T(8,128)S(1)}, u32[]{:S(2)}, u32[]{:S(2)}) collective-permute-start(f32[2,128,128]{2,1,0:T(8,128)S(1)} %slice_select_fusion.4), channel_id=1, source_target_pairs={{0,16},{4,20},{8,24},{12,28},{16,0},{20,4},{24,8},{28,12},{32,48},... | collective-permute-start | bytes 393224 | tf_op jit(solution)/shard_map/ppermute | solution.py:31
  63.6 4.2 %collective-permute-done.11 = f32[2,128,128]{2,1,0:T(8,128)S(1)} collective-permute-done((f32[2,128,128]{2,1,0:T(8,128)S(1)}, f32[2,128,128]{2,1,0:T(8,128)S(1)}, u32[]{:S(2)}, u32[]{:S(2)}) %collective-permute-start.11) | collective-permute-done | bytes 131104 | tf_op jit(solution)/shard_map/ppermute | solution.py:31
  68.0 0.2 fusion.175
  68.3 0.3 fusion.60
  68.6 0.3 fusion.66
  68.9 0.3 fusion.72
  69.2 0.3 fusion.78
  69.6 0.4 fusion.34
  70.0 0.4 fusion.40
  70.5 0.4 fusion.46
  70.9 0.4 fusion.52
  72.1 2.6 %collective-permute-start.14 = (f32[2,48,128]{2,1,0:T(8,128)S(1)}, f32[2,48,128]{2,1,0:T(8,128)S(1)}, u32[]{:S(2)}, u32[]{:S(2)}) collective-permute-start(f32[2,48,128]{2,1,0:T(8,128)S(1)} %get-tuple-element.84), channel_id=1, source_target_pairs={{0,3},{1,0},{2,1},{3,2},{4,7},{5,4},{6,5},{7,6},{8,11},{9,8},{10,9... | collective-permute-start | bytes 147464 | tf_op jit(solution)/shard_map/ppermute | solution.py:26
  74.7 0.3 fusion.198
  75.0 0.3 collective-permute-start.16
  75.3 2.7 %collective-permute-start.17 = (f32[4,24,512]{2,1,0:T(8,128)S(1)}, f32[4,24,512]{2,1,0:T(8,128)S(1)}, u32[]{:S(2)}, u32[]{:S(2)}) collective-permute-start(f32[4,24,512]{2,1,0:T(8,128)S(1)} %get-tuple-element.57), channel_id=1, source_target_pairs={{0,3},{1,0},{2,1},{3,2},{4,7},{5,4},{6,5},{7,6},{8,11},{9,8},{10,9... | collective-permute-start | bytes 589832 | tf_op jit(solution)/shard_map/ppermute | solution.py:26
  78.0 0.7 collective-permute-start.15
  78.7 3.1 %collective-permute-done.15 = f32[2,96,128]{2,1,0:T(8,128)S(1)} collective-permute-done((f32[2,96,128]{2,1,0:T(8,128)S(1)}, f32[2,96,128]{2,1,0:T(8,128)S(1)}, u32[]{:S(2)}, u32[]{:S(2)}) %collective-permute-start.15) | collective-permute-done | bytes 98336 | tf_op jit(solution)/shard_map/ppermute | solution.py:31
  81.9 4.2 %collective-permute-start.18 = (f32[2,96,256]{2,1,0:T(8,128)S(1)}, f32[2,96,256]{2,1,0:T(8,128)S(1)}, u32[]{:S(2)}, u32[]{:S(2)}) collective-permute-start(f32[2,96,256]{2,1,0:T(8,128)S(1)} %maximum_select_fusion.1), channel_id=1, source_target_pairs={{0,4},{4,0},{8,12},{12,8},{16,20},{20,16},{24,28},{28,24},{32,36},... | collective-permute-start | bytes 589832 | tf_op jit(solution)/shard_map/ppermute | solution.py:31
  86.1 1.0 %collective-permute-done.18 = f32[2,96,256]{2,1,0:T(8,128)S(1)} collective-permute-done((f32[2,96,256]{2,1,0:T(8,128)S(1)}, f32[2,96,256]{2,1,0:T(8,128)S(1)}, u32[]{:S(2)}, u32[]{:S(2)}) %collective-permute-start.18) | collective-permute-done | bytes 196640 | tf_op jit(solution)/shard_map/ppermute | solution.py:31
  87.2 0.3 fusion.108
  87.4 0.3 fusion.114
  87.7 0.3 fusion.120
  88.0 0.3 fusion.126
  88.9 0.3 multiply_add_fusion
  89.5 0.9 %fusion.53 = f32[4,64,512]{2,1,0:T(8,128)} fusion(f32[1,96,512]{2,1,0:T(8,128)S(1)} %get-tuple-element.71, f32[1,96,512]{2,1,0:T(8,128)S(1)} %fusion.283, f32[1,96,512]{2,1,0:T(8,128)S(1)} %bitcast.175, f32[1,96,512]{2,1,0:T(8,128)S(1)} %bitcast.174, f32[4,112,512]{2,1,0:T(8,128)S(1)} %pad_maximum_fusion, f32[4,24,512]{2,1,0:T(8,128)S(1)} %broadcast_select_fusion.2, ...), kind=kLoop, calls=%fused_computation.167 | loop fusion | flops 786432 | bytes 2228224 | tf_op jit(solution)/shard_map/add | solution.py:218
  (90 shorter events, 6.1 us)
Async XLA Ops:
  1.5 7.7 %collective-permute-start = (f32[32,512]{1,0:T(8,128)}, f32[32,512]{1,0:T(8,128)S(1)}, u32[]{:S(2)}, u32[]{:S(2)}) collective-permute-start(f32[32,512]{1,0:T(8,128)} %get-tuple-element.87), channel_id=1, source_target_pairs={{0,1},{1,2},{2,3},{3,0},{4,5},{5,6},{6,7},{7,4},{8,9},{9,10},{10,1... | collective-permute-start | bytes 196616 | tf_op jit(solution)/shard_map/ppermute | solution.py:26
  3.6 5.6 %collective-permute-start.1 = (f32[32,512]{1,0:T(8,128)S(1)}, f32[32,512]{1,0:T(8,128)}, u32[]{:S(2)}, u32[]{:S(2)}) collective-permute-start(f32[32,512]{1,0:T(8,128)S(1)} %get-tuple-element.86), channel_id=1, source_target_pairs={{0,3},{1,0},{2,1},{3,2},{4,7},{5,4},{6,5},{7,6},{8,11},{9,8},{10,9... | collective-permute-start | bytes 196616 | tf_op jit(solution)/shard_map/ppermute | solution.py:26
  14.9 1.0 %copy-start = (f32[4,64,512]{2,1,0:T(8,128)S(1)}, f32[4,64,512]{2,1,0:T(8,128)}, u32[]{:S(2)}) copy-start(f32[4,64,512]{2,1,0:T(8,128)} %param.7) | copy-start | bytes 1572868
  16.5 34.0 %collective-permute-start.9 = (f32[2,80,512]{2,1,0:T(8,128)S(1)}, f32[2,80,512]{2,1,0:T(8,128)S(1)}, u32[]{:S(2)}, u32[]{:S(2)}) collective-permute-start(f32[2,80,512]{2,1,0:T(8,128)S(1)} %pad_maximum_fusion.8), channel_id=1, source_target_pairs={{0,4},{4,8},{8,12},{12,16},{16,20},{20,24},{24,28},{28,32},{32,36}... | collective-permute-start | bytes 983048 | tf_op jit(solution)/shard_map/ppermute | solution.py:26
  20.5 3.0 %collective-permute-start.2 = (f32[2,96,512]{2,1,0:T(8,128)S(1)}, f32[2,96,512]{2,1,0:T(8,128)S(1)}, u32[]{:S(2)}, u32[]{:S(2)}) collective-permute-start(f32[2,96,512]{2,1,0:T(8,128)S(1)} %fusion.102), channel_id=1, source_target_pairs={{0,4},{4,0},{8,12},{12,8},{16,20},{20,16},{24,28},{28,24},{32,36},... | collective-permute-start | bytes 1179656 | tf_op jit(solution)/shard_map/ppermute | solution.py:31
  24.2 6.2 %collective-permute-start.3 = (f32[2,96,256]{2,1,0:T(8,128)S(1)}, f32[2,96,256]{2,1,0:T(8,128)S(1)}, u32[]{:S(2)}, u32[]{:S(2)}) collective-permute-start(f32[2,96,256]{2,1,0:T(8,128)S(1)} %fusion.396), channel_id=1, source_target_pairs={{0,8},{4,12},{8,0},{12,4},{16,24},{20,28},{24,16},{28,20},{32,40},... | collective-permute-start | bytes 589832 | tf_op jit(solution)/shard_map/ppermute | solution.py:31
  24.7 11.8 %collective-permute-start.6 = (f32[96,512]{1,0:T(8,128)S(1)}, f32[96,512]{1,0:T(8,128)S(1)}, u32[]{:S(2)}, u32[]{:S(2)}) collective-permute-start(f32[96,512]{1,0:T(8,128)S(1)} %get-tuple-element.51), channel_id=1, source_target_pairs={{0,8},{4,12},{8,16},{12,20},{16,24},{20,28},{24,32},{28,36},{32,40... | collective-permute-start | bytes 589832 | tf_op jit(solution)/shard_map/ppermute | solution.py:26
  30.5 12.4 %collective-permute-start.4 = (f32[2,96,256]{2,1,0:T(8,128)S(1)}, f32[2,96,256]{2,1,0:T(8,128)S(1)}, u32[]{:S(2)}, u32[]{:S(2)}) collective-permute-start(f32[2,96,256]{2,1,0:T(8,128)S(1)} %select_add_fusion), channel_id=1, source_target_pairs={{0,32},{4,36},{8,40},{12,44},{16,48},{20,52},{24,56},{28,60},{32,6... | collective-permute-start | bytes 589832 | tf_op jit(solution)/shard_map/ppermute | solution.py:26
  31.5 11.4 %collective-permute-start.5 = (f32[96,256]{1,0:T(8,128)S(1)}, f32[96,256]{1,0:T(8,128)S(1)}, u32[]{:S(2)}, u32[]{:S(2)}) collective-permute-start(f32[96,256]{1,0:T(8,128)S(1)} %add_select_fusion.2), channel_id=1, source_target_pairs={{0,64},{4,68},{8,72},{12,76},{16,80},{20,84},{24,88},{28,92},{32,9... | collective-permute-start | bytes 294920 | tf_op jit(solution)/shard_map/ppermute | solution.py:26
  43.6 15.0 %collective-permute-start.10 = (f32[96,512]{1,0:T(8,128)S(1)}, f32[96,512]{1,0:T(8,128)S(1)}, u32[]{:S(2)}, u32[]{:S(2)}) collective-permute-start(f32[96,512]{1,0:T(8,128)S(1)} %collective-permute-done.6), channel_id=1, source_target_pairs={{0,4},{4,0},{8,12},{12,8},{16,20},{20,16},{24,28},{28,24},{32,36},... | collective-permute-start | bytes 589832 | tf_op jit(solution)/shard_map/ppermute | solution.py:31
  46.4 9.4 %collective-permute-start.7 = (f32[112,256]{1,0:T(8,128)S(1)}, f32[112,256]{1,0:T(8,128)S(1)}, u32[]{:S(2)}, u32[]{:S(2)}) collective-permute-start(f32[112,256]{1,0:T(8,128)S(1)} %fusion.395), channel_id=1, source_target_pairs={{0,64},{4,68},{8,72},{12,76},{16,80},{20,84},{24,88},{28,92},{32,9... | collective-permute-start | bytes 344072 | tf_op jit(solution)/shard_map/ppermute | solution.py:26
  46.5 12.2 %collective-permute-start.8 = (f32[112,256]{1,0:T(8,128)S(1)}, f32[112,256]{1,0:T(8,128)S(1)}, u32[]{:S(2)}, u32[]{:S(2)}) collective-permute-start(f32[112,256]{1,0:T(8,128)S(1)} %fusion.395), channel_id=1, source_target_pairs={{0,160},{4,164},{8,168},{12,172},{16,176},{20,180},{24,184},{28,18... | collective-permute-start | bytes 344072 | tf_op jit(solution)/shard_map/ppermute | solution.py:26
  58.9 8.9 %collective-permute-start.12 = (f32[96,512]{1,0:T(8,128)S(1)}, f32[96,512]{1,0:T(8,128)S(1)}, u32[]{:S(2)}, u32[]{:S(2)}) collective-permute-start(f32[96,512]{1,0:T(8,128)S(1)} %get-tuple-element.62), channel_id=1, source_target_pairs={{0,8},{4,12},{8,0},{12,4},{16,24},{20,28},{24,16},{28,20},{32,40},... | collective-permute-start | bytes 589832 | tf_op jit(solution)/shard_map/ppermute | solution.py:31
  62.4 5.4 %collective-permute-start.11 = (f32[2,128,128]{2,1,0:T(8,128)S(1)}, f32[2,128,128]{2,1,0:T(8,128)S(1)}, u32[]{:S(2)}, u32[]{:S(2)}) collective-permute-start(f32[2,128,128]{2,1,0:T(8,128)S(1)} %slice_select_fusion.4), channel_id=1, source_target_pairs={{0,16},{4,20},{8,24},{12,28},{16,0},{20,4},{24,8},{28,12},{32,48},... | collective-permute-start | bytes 393224 | tf_op jit(solution)/shard_map/ppermute | solution.py:31
  71.9 6.0 %collective-permute-start.13 = (f32[2,48,128]{2,1,0:T(8,128)S(1)}, f32[2,48,128]{2,1,0:T(8,128)S(1)}, u32[]{:S(2)}, u32[]{:S(2)}) collective-permute-start(f32[2,48,128]{2,1,0:T(8,128)S(1)} %get-tuple-element.85), channel_id=1, source_target_pairs={{0,1},{1,2},{2,3},{3,0},{4,5},{5,6},{6,7},{7,4},{8,9},{9,10},{10,1... | collective-permute-start | bytes 147464 | tf_op jit(solution)/shard_map/ppermute | solution.py:26
  72.1 5.9 %collective-permute-start.14 = (f32[2,48,128]{2,1,0:T(8,128)S(1)}, f32[2,48,128]{2,1,0:T(8,128)S(1)}, u32[]{:S(2)}, u32[]{:S(2)}) collective-permute-start(f32[2,48,128]{2,1,0:T(8,128)S(1)} %get-tuple-element.84), channel_id=1, source_target_pairs={{0,3},{1,0},{2,1},{3,2},{4,7},{5,4},{6,5},{7,6},{8,11},{9,8},{10,9... | collective-permute-start | bytes 147464 | tf_op jit(solution)/shard_map/ppermute | solution.py:26
  75.0 6.9 %collective-permute-start.16 = (f32[4,24,512]{2,1,0:T(8,128)S(1)}, f32[4,24,512]{2,1,0:T(8,128)S(1)}, u32[]{:S(2)}, u32[]{:S(2)}) collective-permute-start(f32[4,24,512]{2,1,0:T(8,128)S(1)} %get-tuple-element.58), channel_id=1, source_target_pairs={{0,1},{1,2},{2,3},{3,0},{4,5},{5,6},{6,7},{7,4},{8,9},{9,10},{10,1... | collective-permute-start | bytes 589832 | tf_op jit(solution)/shard_map/ppermute | solution.py:26
  75.3 6.6 %collective-permute-start.17 = (f32[4,24,512]{2,1,0:T(8,128)S(1)}, f32[4,24,512]{2,1,0:T(8,128)S(1)}, u32[]{:S(2)}, u32[]{:S(2)}) collective-permute-start(f32[4,24,512]{2,1,0:T(8,128)S(1)} %get-tuple-element.57), channel_id=1, source_target_pairs={{0,3},{1,0},{2,1},{3,2},{4,7},{5,4},{6,5},{7,6},{8,11},{9,8},{10,9... | collective-permute-start | bytes 589832 | tf_op jit(solution)/shard_map/ppermute | solution.py:26
  78.0 3.8 %collective-permute-start.15 = (f32[2,96,128]{2,1,0:T(8,128)S(1)}, f32[2,96,128]{2,1,0:T(8,128)S(1)}, u32[]{:S(2)}, u32[]{:S(2)}) collective-permute-start(f32[2,96,128]{2,1,0:T(8,128)S(1)} %slice_add_fusion.2), channel_id=1, source_target_pairs={{0,8},{4,12},{8,0},{12,4},{16,24},{20,28},{24,16},{28,20},{32,40},... | collective-permute-start | bytes 294920 | tf_op jit(solution)/shard_map/ppermute | solution.py:31
  81.9 5.3 %collective-permute-start.18 = (f32[2,96,256]{2,1,0:T(8,128)S(1)}, f32[2,96,256]{2,1,0:T(8,128)S(1)}, u32[]{:S(2)}, u32[]{:S(2)}) collective-permute-start(f32[2,96,256]{2,1,0:T(8,128)S(1)} %maximum_select_fusion.1), channel_id=1, source_target_pairs={{0,4},{4,0},{8,12},{12,8},{16,20},{20,16},{24,28},{28,24},{32,36},... | collective-permute-start | bytes 589832 | tf_op jit(solution)/shard_map/ppermute | solution.py:31

commit v3 on v2

--- a/solution.py
+++ b/solution.py
@@ -60,11 +60,21 @@
 
     sources = forcing.reshape((FACTOR, FACTOR) + forcing.shape[1:])
     first = jnp.where(p == 0, initial, zero)[None]
-    cur = wide(jnp.concatenate([first, guessed], 0), 8)
-    src = wide(jnp.concatenate([sources, jnp.zeros_like(sources[:1])], 0), 8)
     above = shift(diffusivity[rows - E :], "space", 1)
     below = shift(diffusivity[:E], "space", -1)
-    above, below, cur, src = hold(above, below, cur, src)
+
+    start = jnp.concatenate([first, guessed], 0)
+
+    def march(cur, d, src):
+        for i in range(FACTOR):
+            nxt = step(cur, d, S0)
+            cur = jnp.concatenate([nxt[..., :4, :, :] + src(i), nxt[..., 4:, :, :]], -3)
+        return cur
+
+    middle = march(start, diffusivity, lambda i: sources[:, i])
+    strips = jnp.stack([wide(start[:, :16], 8)[:, :-8], wide(start[:, 48:], 8)[:, 8:]])
+    strip_src = jnp.stack([wide(sources[:, :, :16], 8)[:, :, :-8], wide(sources[:, :, 48:], 8)[:, :, 8:]])
+    above, below, middle, strips, strip_src = hold(above, below, middle, strips, strip_src)
     above = jnp.where(y == 0, zero, above)
     below = jnp.where(y == ny - 1, zero, below)
     dwide = jnp.concatenate([above, diffusivity, below], 0)
@@ -72,8 +82,9 @@
     def dext(e):
         return dwide[E - e : E + rows + e]
 
-    for i in range(FACTOR):
-        cur = step(cur, dext(8), S0) + src[:, i]
+    dstrip = jnp.stack([dwide[E - 8 : E + 16], dwide[E + 48 : E + 72]])[:, None]
+    strips = march(strips, dstrip, lambda i: strip_src[:, :, i])
+    cur = jnp.concatenate([strips[0, :, :16], middle[:, 8:56], strips[1, :, 8:]], 1)
     relaxed, gw = cur[:4], cur[4]
     d = relaxed - wide(guessed, 8)
     dw = regrow(d, 8, 16)
@@ -83,9 +94,10 @@
     xf = step(xf, d16, S1) + dw[2]
     yf = steps(step(dw[3], d16, S1) + gw16, d16, S1, 2)
     xy = steps(jnp.stack([xf, yf]), d16, S0, 4)
+    xy, dheld = hold(xy, dwide)
     theirs = swap(xy, 1)
 
-    dpad = edged(dwide)
+    dpad = edged(dheld)
     dhalf = jnp.where(core0, dpad[:, :384], dpad[:, 256:])
     dquarter = jnp.where(odd, dhalf[:, 128:], dhalf[:, :256])
 
@@ -107,71 +119,75 @@
     ff = jnp.stack([f1, f2])
     keep = jnp.where(odd, ff[..., 128:], ff[..., :256])
     give = jnp.where(odd, ff[..., :256], ff[..., 128:])
-    keep = keep + swap(give, 2)
-
-    def dq(e):
-        return dquarter[E - e : E + rows + e]
-
-    def to_psi(v):
-        g = step(v[0], dq(16), S3) + v[1]
-        return jnp.where(h == 0, step(g, dq(16), S3), g)
-
-    psi = to_psi(keep)
     xy0 = jnp.where(core0, xy, theirs)
     xy1 = jnp.where(core0, theirs, xy)
     rfull = xy1[0] + xy0[1]
-    ry = jnp.where(core0, rfull, xy[1])
-    before, psi2, ry = hold(shift(keep, "tm", 8), shift(psi, "tm", 16), shift(ry, "tm", 2))
+    other = swap(give, 2)
+    keep = keep + other
+
+    def dq(e):
+        return dquarter[E - e : E + rows + e]
+
+    def to_psi(v):
+        g = step(v[0], dq(16), S3) + v[1]
+        return jnp.where(low, step(g, dq(16), S3), g)
+
+    low = h == 0
+    psi = to_psi(keep)
+    before, psi2, rpart, d3gw = hold(
+        shift(keep, "tm", 8),
+        shift(psi, "tm", 16),
+        shift(jnp.where(core0, rfull[:48], rfull[48:]), "tm", 2),
+        shift(jnp.stack([d[3], gw])[:, 4:-4], "tm", 1),
+    )
     before = jnp.where(z >= 1, before, zero)
     psi2 = jnp.where(z >= 2, psi2, zero)
     psi1 = to_psi(before)
-    u = steps(regrow(psi2, 16, 24), dq(24), S3, 2) + regrow(psi1, 16, 24)
-    u = steps(u, dq(24), S3, 2) + regrow(psi, 16, 24)
-    u2, u5, d3gw, ry2 = hold(
-        shift(u, "tm", 16),
-        shift(u, "tm", 40),
-        shift(jnp.stack([dw[3], gw16])[:, 8:-8], "tm", 1),
-        swap(ry, 1),
-    )
+    u = steps(regrow(psi2, 16, 20), dq(20), S3, 2) + regrow(psi1, 16, 20)
+    u = steps(u, dq(20), S3, 2) + regrow(psi, 16, 20)
+
+    q0 = (z == 0) & (x == 0)
+    d3gw = regrow(jnp.where(p == 0, zero, d3gw), 4, 16)
+    rpart = jnp.where(q0, zero, rpart)
+    yp = step(d3gw[0], d16, S1) + d3gw[1]
+    yp = steps(steps(yp, d16, S1, 2), d16, S0, 4)
+    ry = jnp.concatenate([yp, rpart], 0)
+
+    dz = dq(32)
+    bw, kw = regrow(before, 16, 32), regrow(keep, 16, 32)
+    eps = jnp.where(low, bw[0], zero)
+    tau = jnp.where(low, bw[1], bw[0])
+    tau1 = jnp.where(low, kw[0], bw[1])
+    tau2 = jnp.where(low, kw[1], kw[0])
+    eps1 = step(eps, dz, S3) + tau
+    eps2 = step(eps1, dz, S3) + tau1
+    near = steps(jnp.stack([eps, eps1, eps2]), dz, S2, 4) + jnp.stack([tau, tau1, tau2])
+    u2, u5, ry2, near = hold(shift(u, "tm", 16), shift(u, "tm", 40), swap(ry, 1), near)
+    yp = jnp.where(core0, yp, ry2[:96])
+    rother = ry2[96:]
+    rp = jnp.where(core0, jnp.concatenate([rpart, rother], 0), jnp.concatenate([rother, rpart], 0))
+    s1 = step(rp, d16, S2) + xy0[0] + yp
     u2 = jnp.where(z >= 2, u2, zero)
     u5 = jnp.where(z >= 5, u5, zero)
-    q0 = (z == 0) & (x == 0)
-    d3gw = jnp.where(p == 0, zero, d3gw)
-    rp = jnp.where(q0, zero, jnp.where(core0, ry, ry2))
-    yp = jnp.where(q0, zero, jnp.where(core0, ry2, ry))
-    s1 = step(rp, d16, S2) + xy0[0] + yp
-
-    dz = dq(32)
-    eps = regrow(u2, 24, 32) + steps(regrow(u5, 24, 32), dz, S3, 6)
-    bw, kw = regrow(before, 16, 32), regrow(keep, 16, 32)
-    low = h == 0
-    eps = eps + jnp.where(low, bw[0], zero)
-    tau = jnp.where(low, bw[1], bw[0])
-    alpha = jnp.where(low, zero, bw[1])
-    b0 = jnp.where(low, kw[0], zero)
-    tau2 = jnp.where(low, kw[1], kw[0])
-    eps1 = step(eps, dz, S3) + tau
-    tau1 = b0 + alpha
-    eps2 = step(eps1, dz, S3) + tau1
-    zs = steps(jnp.stack([eps, eps1, eps2]), dz, S2, 4) + jnp.stack([tau, tau1, tau2])
+    far = regrow(u2, 20, 32) + steps(regrow(u5, 20, 32), dz, S3, 6)
+    far = steps(far, dz, S2, 4)
+    far1 = step(far, dz, S3)
+    zs = near + jnp.stack([far, far1, step(far1, dz, S3)])
     zs = zs[..., EDGE:-EDGE]
     keep = jnp.where(low, zs[:2], zs[1:])
     give = jnp.where(low, zs[1:], zs[:2])
-    other, s1x = hold(swap(give, 4), swap(s1, 2))
-    keep = keep + other
 
     def r24(v):
         return regrow(v, 16, 24)
 
     d24 = dext(24)
-    s1q = jnp.where(odd, r24(s1x), zero)
-    d3p, gwp = regrow(d3gw[0], 8, 24), regrow(d3gw[1], 8, 24)
+    d3p, gwp = r24(d3gw[0]), r24(d3gw[1])
     d0 = regrow(d[0], 8, 24) + gwp
     quad = steps(jnp.stack([d3p, d0, regrow(d[1], 8, 24)]), d24, S0, 4)
     a3p, a0, a1 = quad[0], quad[1], quad[2]
     rprev = jnp.where(core0, r24(rp), r24(xy0[0] + yp))
     rown = jnp.where(core0, r24(xy0[0] + yp), r24(rfull))
-    ea = jnp.where(core0, s1q, step(s1q, d24, S2) + r24(rp))
+    ea = jnp.where(core0, zero, r24(rp))
     eb = step(ea, d24, S2) + rprev
     eb = jnp.where(odd & (c == 1), zero, eb)
     pair = steps(jnp.stack([ea, eb]), d24, S1, 4)
@@ -181,13 +197,33 @@
     rel = regrow(relaxed, 8, 24)
     local = jnp.stack([rel[0] + gwp + y_1, rel[1] + y_2, rel[2] + y_3, rel[3] + rown + pair[1]])
 
+    other, s1x, local = hold(swap(give, 4), swap(s1, 2), local)
+    keep = keep + other
+    s1x = jnp.where(odd, s1x, zero)
+
     n = rows + 2 * E
+
+    def packed(v):
+        return jnp.concatenate([v[0, :24], v[0, 24:], v[1, :24], v[1, 24:]], 1)
+
+    def unpacked(v):
+        return jnp.stack(
+            [
+                jnp.concatenate([v[:, :128], v[:, 128:256]], 0),
+                jnp.concatenate([v[:, 256:384], v[:, 384:]], 0),
+            ]
+        )
+
     from_above, from_below = hold(
-        shift(keep[:, n - 48 :], "space", 1), shift(keep[:, :48], "space", -1)
+        shift(jnp.stack([packed(keep[:, n - 48 :]), s1x[-24:]]), "space", 1),
+        shift(jnp.stack([packed(keep[:, :48]), s1x[:24]]), "space", -1),
     )
     from_above = jnp.where(y == 0, zero, from_above)
     from_below = jnp.where(y == ny - 1, zero, from_below)
-    keep = keep[:, 16:-16] + jnp.concatenate([from_above, from_below], 1)
+    keep = keep[:, 16:-16] + jnp.concatenate(
+        [unpacked(from_above[0]), unpacked(from_below[0])], 1
+    )
+    s1g = s1x + jnp.pad(from_above[1], ((8, 64), (0, 0))) + jnp.pad(from_below[1], ((64, 8), (0, 0)))
     m = rows + 48
     other, la, lb = hold(
         swap(keep, 2), shift(local[:, m - 24 :], "space", 1), shift(local[:, :24], "space", -1)
@@ -197,9 +233,9 @@
     both = jnp.where(
         core0, jnp.concatenate([keep, other], 2), jnp.concatenate([other, keep], 2)
     )
-    both = steps(both, d16, S1, 4)
+    q = jnp.where(odd, steps(both[0], d16, S2, 2) + s1g, both[0])
+    both = steps(jnp.stack([q, both[1]]), d16, S1, 4)
     q, zn = both[0], both[1]
-    q = jnp.where(odd, steps(q, d16, S2, 2), q)
     q = jnp.where(core0, q, step(q, d16, S2))
     e2b = jnp.where(odd & (c == 1), zn, step(q, d16, S2))
     t1 = step(q, d16, S1)

time: 90.8 us -> 81.3 us (0.90)
  waiting for transfers between devices: 29.8 us -> 21.7 us
  other arithmetic: 23.6 us -> 21.9 us
  local copies, waits for them, and re-layouts: 3.77 us -> 2.74 us
  starting transfers between devices: 32.4 us -> 33.4 us
    ppermute x7, waiting for transfers between devices: 13.5 us -> 8.41 us  [swap(): return lax.ppermute(v, 'tm', [(i, i ^ bit) for i in range(n)])]
    add x29 -> x48, other arithmetic: 7.54 us -> 12.2 us  [step(): return v + s * d * lap]
    add x9 -> x15, other arithmetic: 5.34 us -> 1.25 us  [the longest x8 0.57 us: march(): cur = jnp.concatenate([nxt[..., :4, :, :] + src(i), nxt[..., 4:, :, :]], -3)]
    ppermute x12, waiting for transfers between devices: 16.3 us -> 13.3 us  [shift(): return lax.ppermute(v, axis, [(i, (i + by) % n) for i in range(n)])]
    ppermute x7, starting transfers between devices: 11.2 us -> 13.2 us  [swap(): return lax.ppermute(v, 'tm', [(i, i ^ bit) for i in range(n)])]
    pad x3 -> x2, local copies, waits for them, and re-layouts: 2.04 us -> 0.02 us  [wide(): return jnp.pad(v, [(0, 0)] * (v.ndim - 2) + [(e, e), (0, 0)])]
    ppermute x12, starting transfers between devices: 21.2 us -> 20.1 us  [shift(): return lax.ppermute(v, axis, [(i, (i + by) % n) for i in range(n)])]
    unnamed x2 -> x6, local copies, waits for them, and re-layouts: 0.02 us -> 1.09 us
  transfers between devices with their start and end apart: 19 -> 19, of which waited for: 9 -> 10; matrix products, arithmetic and copies ran while one was open for 12% -> 15% of each run, Pallas kernels for 0% -> 0%
where the time goes in v3:
time: 81.3 us; the launch traced here: 81.2 us
  starting transfers between devices  33.4 us (41%)
  other arithmetic  21.9 us (27%)
  waiting for transfers between devices  21.7 us (27%)
  local copies, waits for them, and re-layouts  2.74 us (3%)
  between operations  1.48 us (2%)
    ppermute x12, starting transfers between devices, shift(): return lax.ppermute(v, axis, [(i, (i + by) % n) for i in range(n)])  20.1 us
    ppermute x12, waiting for transfers between devices, shift(): return lax.ppermute(v, axis, [(i, (i + by) % n) for i in range(n)])  13.3 us
    ppermute x7, starting transfers between devices, swap(): return lax.ppermute(v, 'tm', [(i, i ^ bit) for i in range(n)])  13.2 us
    add x48, other arithmetic, step(): return v + s * d * lap  12.2 us
    ppermute x7, waiting for transfers between devices, swap(): return lax.ppermute(v, 'tm', [(i, i ^ bit) for i in range(n)])  8.41 us
  transfers between devices with their start and end apart: 19, of which 10 were waited for; matrix products, arithmetic and copies ran while one was open for 15% of the time, Pallas kernels for 0%

profile of v3, /device:TPU:1, one launch (start us, length us, event | category | flops | bytes accessed | tf_op | source)
XLA Modules:
  0.0 81.2 jit_solution(1154165031948296772)
XLA Ops:
  0.0 0.9 %fusion.546 = (f32[32,512]{1,0:T(8,128)S(1)}, f32[32,512]{1,0:T(8,128)S(1)}) fusion(f32[64,512]{1,0:T(8,128)} %param.5), kind=kLoop, calls=%fused_computation.1003 | loop fusion | bytes 262144 | tf_op jit(solution)/shard_map/slice | solution.py:64
  1.0 3.6 %collective-permute-start.1 = (f32[32,512]{1,0:T(8,128)S(1)}, f32[32,512]{1,0:T(8,128)S(1)}, u32[]{:S(2)}, u32[]{:S(2)}) collective-permute-start(f32[32,512]{1,0:T(8,128)S(1)} %get-tuple-element.112), channel_id=1, source_target_pairs={{0,3},{1,0},{2,1},{3,2},{4,7},{5,4},{6,5},{7,6},{8,11},{9,8},{10,9... | collective-permute-start | bytes 196616 | tf_op jit(solution)/shard_map/ppermute | solution.py:26
  4.6 1.0 %fusion.362 = (f32[5,16,512]{2,1,0:T(8,128)S(1)}, f32[5,16,512]{2,1,0:T(8,128)S(1)}) fusion(f32[4,64,512]{2,1,0:T(8,128)} %param.7, f32[1,64,512]{2,1,0:T(8,128)S(1)} %select_bitcast_fusion), kind=kLoop, calls=%fused_computation.756 | loop fusion | flops 81920 | bytes 983040 | tf_op jit(solution)/shard_map/concatenate | solution.py:66
  5.7 0.4 fusion.31
  6.1 1.1 %copy-done.1 = f32[16,64,512]{2,1,0:T(8,128)S(1)} copy-done((f32[16,64,512]{2,1,0:T(8,128)S(1)}, f32[16,64,512]{2,1,0:T(8,128)}, u32[]{:S(2)}) %copy-start.1) | copy-done | bytes 2097176
  7.4 0.4 fusion.37
  8.0 0.4 fusion.43
  8.5 0.4 fusion.49
  9.8 0.3 fusion.60
  10.2 0.3 fusion.66
  10.7 0.3 fusion.72
  11.2 0.3 fusion.78
  12.0 0.3 fusion.545
  12.3 0.3 fusion.243
  12.8 0.3 fusion.108
  13.1 0.3 fusion.114
  13.4 0.3 fusion.120
  13.7 0.3 fusion.126
  14.0 2.5 %collective-permute-start.7 = (f32[2,72,512]{2,1,0:T(8,128)S(1)}, f32[2,72,512]{2,1,0:T(8,128)S(1)}, u32[]{:S(2)}, u32[]{:S(2)}) collective-permute-start(f32[2,72,512]{2,1,0:T(8,128)S(1)} %pad_maximum_fusion.20), channel_id=1, source_target_pairs={{0,4},{4,8},{8,12},{12,16},{16,20},{20,24},{24,28},{28,32},{32,36}... | collective-permute-start | bytes 884744 | tf_op jit(solution)/shard_map/ppermute | solution.py:26
  16.4 0.3 collective-permute-start.2
  16.9 0.2 fusion.179
  17.2 1.1 %collective-permute-done.2 = f32[2,96,512]{2,1,0:T(8,128)S(1)} collective-permute-done((f32[2,96,512]{2,1,0:T(8,128)S(1)}, f32[2,96,512]{2,1,0:T(8,128)S(1)}, u32[]{:S(2)}, u32[]{:S(2)}) %collective-permute-start.2) | collective-permute-done | bytes 393248 | tf_op jit(solution)/shard_map/ppermute | solution.py:31
  18.3 0.2 fusion.180
  19.0 1.2 %collective-permute-start.3 = (f32[2,96,256]{2,1,0:T(8,128)S(1)}, f32[2,96,256]{2,1,0:T(8,128)S(1)}, u32[]{:S(2)}, u32[]{:S(2)}) collective-permute-start(f32[2,96,256]{2,1,0:T(8,128)S(1)} %fusion.478), channel_id=1, source_target_pairs={{0,8},{4,12},{8,0},{12,4},{16,24},{20,28},{24,16},{28,20},{32,40},... | collective-permute-start | bytes 589832 | tf_op jit(solution)/shard_map/ppermute | solution.py:31
  20.4 0.5 collective-permute-start.6
  20.8 4.7 %collective-permute-done.3 = f32[2,96,256]{2,1,0:T(8,128)S(1)} collective-permute-done((f32[2,96,256]{2,1,0:T(8,128)S(1)}, f32[2,96,256]{2,1,0:T(8,128)S(1)}, u32[]{:S(2)}, u32[]{:S(2)}) %collective-permute-start.3) | collective-permute-done | bytes 196640 | tf_op jit(solution)/shard_map/ppermute | solution.py:31
  25.5 1.8 %collective-permute-start.4 = (f32[2,96,256]{2,1,0:T(8,128)S(1)}, f32[2,96,256]{2,1,0:T(8,128)S(1)}, u32[]{:S(2)}, u32[]{:S(2)}) collective-permute-start(f32[2,96,256]{2,1,0:T(8,128)S(1)} %select_add_fusion), channel_id=1, source_target_pairs={{0,32},{4,36},{8,40},{12,44},{16,48},{20,52},{24,56},{28,60},{32,6... | collective-permute-start | bytes 589832 | tf_op jit(solution)/shard_map/ppermute | solution.py:26
  27.6 3.1 %collective-permute-start.5 = (f32[96,256]{1,0:T(8,128)S(1)}, f32[96,256]{1,0:T(8,128)S(1)}, u32[]{:S(2)}, u32[]{:S(2)}) collective-permute-start(f32[96,256]{1,0:T(8,128)S(1)} %add_select_fusion.2), channel_id=1, source_target_pairs={{0,64},{4,68},{8,72},{12,76},{16,80},{20,84},{24,88},{28,92},{32,9... | collective-permute-start | bytes 294920 | tf_op jit(solution)/shard_map/ppermute | solution.py:26
  30.7 8.3 %collective-permute-done.5 = f32[96,256]{1,0:T(8,128)S(1)} collective-permute-done((f32[96,256]{1,0:T(8,128)S(1)}, f32[96,256]{1,0:T(8,128)S(1)}, u32[]{:S(2)}, u32[]{:S(2)}) %collective-permute-start.5) | collective-permute-done | bytes 98336 | tf_op jit(solution)/shard_map/ppermute | solution.py:26
  39.8 4.3 %collective-permute-start.9 = (f32[104,256]{1,0:T(8,128)S(1)}, f32[104,256]{1,0:T(8,128)S(1)}, u32[]{:S(2)}, u32[]{:S(2)}) collective-permute-start(f32[104,256]{1,0:T(8,128)S(1)} %fusion.507), channel_id=1, source_target_pairs={{0,160},{4,164},{8,168},{12,172},{16,176},{20,180},{24,184},{28,18... | collective-permute-start | bytes 319496 | tf_op jit(solution)/shard_map/ppermute | solution.py:26
  44.5 0.3 fusion.156
  44.8 0.3 fusion.162
  45.1 0.3 fusion.168
  46.7 2.8 %collective-permute-start.10 = (f32[144,512]{1,0:T(8,128)S(1)}, f32[144,512]{1,0:T(8,128)S(1)}, u32[]{:S(2)}, u32[]{:S(2)}) collective-permute-start(f32[144,512]{1,0:T(8,128)S(1)} %pad_maximum_fusion.21), channel_id=1, source_target_pairs={{0,4},{4,0},{8,12},{12,8},{16,20},{20,16},{24,28},{28,24},{32,36},... | collective-permute-start | bytes 884744 | tf_op jit(solution)/shard_map/ppermute | solution.py:31
  49.5 0.3 fusion.175
  50.1 0.6 collective-permute-done.10
  50.8 0.2 fusion.361
  53.0 2.5 %collective-permute-start.11 = (f32[2,128,128]{2,1,0:T(8,128)S(1)}, f32[2,128,128]{2,1,0:T(8,128)S(1)}, u32[]{:S(2)}, u32[]{:S(2)}) collective-permute-start(f32[2,128,128]{2,1,0:T(8,128)S(1)} %slice_select_fusion.5), channel_id=1, source_target_pairs={{0,16},{4,20},{8,24},{12,28},{16,0},{20,4},{24,8},{28,12},{32,48},... | collective-permute-start | bytes 393224 | tf_op jit(solution)/shard_map/ppermute | solution.py:31
  55.6 0.2 fusion.544
  55.8 0.4 fusion.7
  56.2 0.4 fusion.13
  56.7 0.4 fusion.19
  57.1 0.4 fusion.25
  57.6 0.3 fusion.84
  57.9 0.3 fusion.90
  58.2 0.3 fusion.96
  58.5 0.3 fusion.102
  58.9 0.2 fusion.184
  59.3 0.2 fusion.220
  59.6 1.0 %collective-permute-done.12 = f32[96,512]{1,0:T(8,128)S(1)} collective-permute-done((f32[96,512]{1,0:T(8,128)S(1)}, f32[96,512]{1,0:T(8,128)S(1)}, u32[]{:S(2)}, u32[]{:S(2)}) %collective-permute-start.12) | collective-permute-done | bytes 196640 | tf_op jit(solution)/shard_map/ppermute | solution.py:31
  61.0 2.7 %collective-permute-start.14 = (f32[2,24,512]{2,1,0:T(8,128)S(1)}, f32[2,24,512]{2,1,0:T(8,128)S(1)}, u32[]{:S(2)}, u32[]{:S(2)}) collective-permute-start(f32[2,24,512]{2,1,0:T(8,128)S(1)} %pad_maximum_fusion.28), channel_id=1, source_target_pairs={{0,3},{1,0},{2,1},{3,2},{4,7},{5,4},{6,5},{7,6},{8,11},{9,8},{10,9... | collective-permute-start | bytes 294920 | tf_op jit(solution)/shard_map/ppermute | solution.py:26
  63.7 1.5 %collective-permute-start.17 = (f32[4,24,512]{2,1,0:T(8,128)S(1)}, f32[4,24,512]{2,1,0:T(8,128)S(1)}, u32[]{:S(2)}, u32[]{:S(2)}) collective-permute-start(f32[4,24,512]{2,1,0:T(8,128)S(1)} %get-tuple-element.67), channel_id=1, source_target_pairs={{0,3},{1,0},{2,1},{3,2},{4,7},{5,4},{6,5},{7,6},{8,11},{9,8},{10,9... | collective-permute-start | bytes 589832 | tf_op jit(solution)/shard_map/ppermute | solution.py:26
  65.3 0.3 collective-permute-done.13
  65.8 1.6 %collective-permute-start.15 = (f32[2,96,128]{2,1,0:T(8,128)S(1)}, f32[2,96,128]{2,1,0:T(8,128)S(1)}, u32[]{:S(2)}, u32[]{:S(2)}) collective-permute-start(f32[2,96,128]{2,1,0:T(8,128)S(1)} %slice_add_fusion.2), channel_id=1, source_target_pairs={{0,8},{4,12},{8,0},{12,4},{16,24},{20,28},{24,16},{28,20},{32,40},... | collective-permute-start | bytes 294920 | tf_op jit(solution)/shard_map/ppermute | solution.py:31
  67.3 1.7 %collective-permute-done.17 = f32[4,24,512]{2,1,0:T(8,128)S(1)} collective-permute-done((f32[4,24,512]{2,1,0:T(8,128)S(1)}, f32[4,24,512]{2,1,0:T(8,128)S(1)}, u32[]{:S(2)}, u32[]{:S(2)}) %collective-permute-start.17) | collective-permute-done | bytes 196640 | tf_op jit(solution)/shard_map/ppermute | solution.py:26
  69.1 2.8 %collective-permute-done.16 = f32[4,24,512]{2,1,0:T(8,128)S(1)} collective-permute-done((f32[4,24,512]{2,1,0:T(8,128)S(1)}, f32[4,24,512]{2,1,0:T(8,128)S(1)}, u32[]{:S(2)}, u32[]{:S(2)}) %collective-permute-start.16) | collective-permute-done | bytes 196640 | tf_op jit(solution)/shard_map/ppermute | solution.py:26
  71.9 4.8 %collective-permute-start.18 = (f32[2,96,256]{2,1,0:T(8,128)S(1)}, f32[2,96,256]{2,1,0:T(8,128)S(1)}, u32[]{:S(2)}, u32[]{:S(2)}) collective-permute-start(f32[2,96,256]{2,1,0:T(8,128)S(1)} %maximum_select_fusion.2), channel_id=1, source_target_pairs={{0,4},{4,0},{8,12},{12,8},{16,20},{20,16},{24,28},{28,24},{32,36},... | collective-permute-start | bytes 589832 | tf_op jit(solution)/shard_map/ppermute | solution.py:31
  76.7 1.1 %collective-permute-done.18 = f32[2,96,256]{2,1,0:T(8,128)S(1)} collective-permute-done((f32[2,96,256]{2,1,0:T(8,128)S(1)}, f32[2,96,256]{2,1,0:T(8,128)S(1)}, u32[]{:S(2)}, u32[]{:S(2)}) %collective-permute-start.18) | collective-permute-done | bytes 196640 | tf_op jit(solution)/shard_map/ppermute | solution.py:31
  78.3 0.3 fusion.132
  78.5 0.3 fusion.138
  78.8 0.3 fusion.144
  79.1 0.3 fusion.150
  79.6 0.3 multiply_add_fusion
  80.2 0.9 %fusion.50 = f32[4,64,512]{2,1,0:T(8,128)} fusion(f32[1,96,512]{2,1,0:T(8,128)S(1)} %get-tuple-element.85, f32[1,96,512]{2,1,0:T(8,128)S(1)} %fusion.351, f32[1,96,512]{2,1,0:T(8,128)S(1)} %bitcast.261, f32[1,96,512]{2,1,0:T(8,128)S(1)} %bitcast.260, f32[4,24,512]{2,1,0:T(8,128)S(1)} %broadcast_select_fusion.3, ...), kind=kLoop, calls=%fused_computation.187 | loop fusion | flops 786432 | bytes 2228224 | tf_op jit(solution)/shard_map/add | solution.py:254
  (166 shorter events, 9.8 us)
Async XLA Ops:
  0.0 5.7 %copy-start = (f32[64,512]{1,0:T(8,128)S(1)}, f32[64,512]{1,0:T(8,128)}, u32[]{:S(2)}) copy-start(f32[64,512]{1,0:T(8,128)} %param.5) | copy-start | bytes 393220
  0.0 5.6 %copy-start.2 = (f32[4,64,512]{2,1,0:T(8,128)S(1)}, f32[4,64,512]{2,1,0:T(8,128)}, u32[]{:S(2)}) copy-start(f32[4,64,512]{2,1,0:T(8,128)} %param.7) | copy-start | bytes 1572868
  1.0 8.7 %collective-permute-start.1 = (f32[32,512]{1,0:T(8,128)S(1)}, f32[32,512]{1,0:T(8,128)S(1)}, u32[]{:S(2)}, u32[]{:S(2)}) collective-permute-start(f32[32,512]{1,0:T(8,128)S(1)} %get-tuple-element.112), channel_id=1, source_target_pairs={{0,3},{1,0},{2,1},{3,2},{4,7},{5,4},{6,5},{7,6},{8,11},{9,8},{10,9... | collective-permute-start | bytes 196616 | tf_op jit(solution)/shard_map/ppermute | solution.py:26
  4.6 5.1 %collective-permute-start = (f32[32,512]{1,0:T(8,128)S(1)}, f32[32,512]{1,0:T(8,128)S(1)}, u32[]{:S(2)}, u32[]{:S(2)}) collective-permute-start(f32[32,512]{1,0:T(8,128)S(1)} %get-tuple-element.113), channel_id=1, source_target_pairs={{0,1},{1,2},{2,3},{3,0},{4,5},{5,6},{6,7},{7,4},{8,9},{9,10},{10,1... | collective-permute-start | bytes 196616 | tf_op jit(solution)/shard_map/ppermute | solution.py:26
  5.6 1.6 %copy-start.1 = (f32[16,64,512]{2,1,0:T(8,128)S(1)}, f32[16,64,512]{2,1,0:T(8,128)}, u32[]{:S(2)}) copy-start(f32[16,64,512]{2,1,0:T(8,128)} %param.6) | copy-start | bytes 6291460
  14.0 16.7 %collective-permute-start.7 = (f32[2,72,512]{2,1,0:T(8,128)S(1)}, f32[2,72,512]{2,1,0:T(8,128)S(1)}, u32[]{:S(2)}, u32[]{:S(2)}) collective-permute-start(f32[2,72,512]{2,1,0:T(8,128)S(1)} %pad_maximum_fusion.20), channel_id=1, source_target_pairs={{0,4},{4,8},{8,12},{12,16},{16,20},{20,24},{24,28},{28,32},{32,36}... | collective-permute-start | bytes 884744 | tf_op jit(solution)/shard_map/ppermute | solution.py:26
  16.4 1.8 %collective-permute-start.2 = (f32[2,96,512]{2,1,0:T(8,128)S(1)}, f32[2,96,512]{2,1,0:T(8,128)S(1)}, u32[]{:S(2)}, u32[]{:S(2)}) collective-permute-start(f32[2,96,512]{2,1,0:T(8,128)S(1)} %fusion.126), channel_id=1, source_target_pairs={{0,4},{4,0},{8,12},{12,8},{16,20},{20,16},{24,28},{28,24},{32,36},... | collective-permute-start | bytes 1179656 | tf_op jit(solution)/shard_map/ppermute | solution.py:31
  19.0 6.4 %collective-permute-start.3 = (f32[2,96,256]{2,1,0:T(8,128)S(1)}, f32[2,96,256]{2,1,0:T(8,128)S(1)}, u32[]{:S(2)}, u32[]{:S(2)}) collective-permute-start(f32[2,96,256]{2,1,0:T(8,128)S(1)} %fusion.478), channel_id=1, source_target_pairs={{0,8},{4,12},{8,0},{12,4},{16,24},{20,28},{24,16},{28,20},{32,40},... | collective-permute-start | bytes 589832 | tf_op jit(solution)/shard_map/ppermute | solution.py:31
  20.4 10.3 %collective-permute-start.6 = (f32[48,512]{1,0:T(8,128)S(1)}, f32[48,512]{1,0:T(8,128)S(1)}, u32[]{:S(2)}, u32[]{:S(2)}) collective-permute-start(f32[48,512]{1,0:T(8,128)S(1)} %fusion.532), channel_id=1, source_target_pairs={{0,8},{4,12},{8,16},{12,20},{16,24},{20,28},{24,32},{28,36},{32,40... | collective-permute-start | bytes 294920 | tf_op jit(solution)/shard_map/ppermute | solution.py:26
  25.5 13.4 %collective-permute-start.4 = (f32[2,96,256]{2,1,0:T(8,128)S(1)}, f32[2,96,256]{2,1,0:T(8,128)S(1)}, u32[]{:S(2)}, u32[]{:S(2)}) collective-permute-start(f32[2,96,256]{2,1,0:T(8,128)S(1)} %select_add_fusion), channel_id=1, source_target_pairs={{0,32},{4,36},{8,40},{12,44},{16,48},{20,52},{24,56},{28,60},{32,6... | collective-permute-start | bytes 589832 | tf_op jit(solution)/shard_map/ppermute | solution.py:26
  27.6 11.4 %collective-permute-start.5 = (f32[96,256]{1,0:T(8,128)S(1)}, f32[96,256]{1,0:T(8,128)S(1)}, u32[]{:S(2)}, u32[]{:S(2)}) collective-permute-start(f32[96,256]{1,0:T(8,128)S(1)} %add_select_fusion.2), channel_id=1, source_target_pairs={{0,64},{4,68},{8,72},{12,76},{16,80},{20,84},{24,88},{28,92},{32,9... | collective-permute-start | bytes 294920 | tf_op jit(solution)/shard_map/ppermute | solution.py:26
  39.8 10.1 %collective-permute-start.9 = (f32[104,256]{1,0:T(8,128)S(1)}, f32[104,256]{1,0:T(8,128)S(1)}, u32[]{:S(2)}, u32[]{:S(2)}) collective-permute-start(f32[104,256]{1,0:T(8,128)S(1)} %fusion.507), channel_id=1, source_target_pairs={{0,160},{4,164},{8,168},{12,172},{16,176},{20,180},{24,184},{28,18... | collective-permute-start | bytes 319496 | tf_op jit(solution)/shard_map/ppermute | solution.py:26
  44.1 6.0 %collective-permute-start.8 = (f32[104,256]{1,0:T(8,128)S(1)}, f32[104,256]{1,0:T(8,128)S(1)}, u32[]{:S(2)}, u32[]{:S(2)}) collective-permute-start(f32[104,256]{1,0:T(8,128)S(1)} %fusion.507), channel_id=1, source_target_pairs={{0,64},{4,68},{8,72},{12,76},{16,80},{20,84},{24,88},{28,92},{32,9... | collective-permute-start | bytes 319496 | tf_op jit(solution)/shard_map/ppermute | solution.py:26
  46.7 4.0 %collective-permute-start.10 = (f32[144,512]{1,0:T(8,128)S(1)}, f32[144,512]{1,0:T(8,128)S(1)}, u32[]{:S(2)}, u32[]{:S(2)}) collective-permute-start(f32[144,512]{1,0:T(8,128)S(1)} %pad_maximum_fusion.21), channel_id=1, source_target_pairs={{0,4},{4,0},{8,12},{12,8},{16,20},{20,16},{24,28},{28,24},{32,36},... | collective-permute-start | bytes 884744 | tf_op jit(solution)/shard_map/ppermute | solution.py:31
  53.0 6.6 %collective-permute-start.11 = (f32[2,128,128]{2,1,0:T(8,128)S(1)}, f32[2,128,128]{2,1,0:T(8,128)S(1)}, u32[]{:S(2)}, u32[]{:S(2)}) collective-permute-start(f32[2,128,128]{2,1,0:T(8,128)S(1)} %slice_select_fusion.5), channel_id=1, source_target_pairs={{0,16},{4,20},{8,24},{12,28},{16,0},{20,4},{24,8},{28,12},{32,48},... | collective-permute-start | bytes 393224 | tf_op jit(solution)/shard_map/ppermute | solution.py:31
  55.5 5.1 %collective-permute-start.12 = (f32[96,512]{1,0:T(8,128)S(1)}, f32[96,512]{1,0:T(8,128)S(1)}, u32[]{:S(2)}, u32[]{:S(2)}) collective-permute-start(f32[96,512]{1,0:T(8,128)S(1)} %get-tuple-element.70), channel_id=1, source_target_pairs={{0,8},{4,12},{8,0},{12,4},{16,24},{20,28},{24,16},{28,20},{32,40},... | collective-permute-start | bytes 589832 | tf_op jit(solution)/shard_map/ppermute | solution.py:31
  60.8 4.8 %collective-permute-start.13 = (f32[2,24,512]{2,1,0:T(8,128)S(1)}, f32[2,24,512]{2,1,0:T(8,128)S(1)}, u32[]{:S(2)}, u32[]{:S(2)}) collective-permute-start(f32[2,24,512]{2,1,0:T(8,128)S(1)} %pad_maximum_fusion.27), channel_id=1, source_target_pairs={{0,1},{1,2},{2,3},{3,0},{4,5},{5,6},{6,7},{7,4},{8,9},{9,10},{10,1... | collective-permute-start | bytes 294920 | tf_op jit(solution)/shard_map/ppermute | solution.py:26
  61.0 4.6 %collective-permute-start.14 = (f32[2,24,512]{2,1,0:T(8,128)S(1)}, f32[2,24,512]{2,1,0:T(8,128)S(1)}, u32[]{:S(2)}, u32[]{:S(2)}) collective-permute-start(f32[2,24,512]{2,1,0:T(8,128)S(1)} %pad_maximum_fusion.28), channel_id=1, source_target_pairs={{0,3},{1,0},{2,1},{3,2},{4,7},{5,4},{6,5},{7,6},{8,11},{9,8},{10,9... | collective-permute-start | bytes 294920 | tf_op jit(solution)/shard_map/ppermute | solution.py:26
  63.7 5.4 %collective-permute-start.17 = (f32[4,24,512]{2,1,0:T(8,128)S(1)}, f32[4,24,512]{2,1,0:T(8,128)S(1)}, u32[]{:S(2)}, u32[]{:S(2)}) collective-permute-start(f32[4,24,512]{2,1,0:T(8,128)S(1)} %get-tuple-element.67), channel_id=1, source_target_pairs={{0,3},{1,0},{2,1},{3,2},{4,7},{5,4},{6,5},{7,6},{8,11},{9,8},{10,9... | collective-permute-start | bytes 589832 | tf_op jit(solution)/shard_map/ppermute | solution.py:26
  65.2 6.6 %collective-permute-start.16 = (f32[4,24,512]{2,1,0:T(8,128)S(1)}, f32[4,24,512]{2,1,0:T(8,128)S(1)}, u32[]{:S(2)}, u32[]{:S(2)}) collective-permute-start(f32[4,24,512]{2,1,0:T(8,128)S(1)} %get-tuple-element.68), channel_id=1, source_target_pairs={{0,1},{1,2},{2,3},{3,0},{4,5},{5,6},{6,7},{7,4},{8,9},{9,10},{10,1... | collective-permute-start | bytes 589832 | tf_op jit(solution)/shard_map/ppermute | solution.py:26
  65.8 6.1 %collective-permute-start.15 = (f32[2,96,128]{2,1,0:T(8,128)S(1)}, f32[2,96,128]{2,1,0:T(8,128)S(1)}, u32[]{:S(2)}, u32[]{:S(2)}) collective-permute-start(f32[2,96,128]{2,1,0:T(8,128)S(1)} %slice_add_fusion.2), channel_id=1, source_target_pairs={{0,8},{4,12},{8,0},{12,4},{16,24},{20,28},{24,16},{28,20},{32,40},... | collective-permute-start | bytes 294920 | tf_op jit(solution)/shard_map/ppermute | solution.py:31
  71.9 5.9 %collective-permute-start.18 = (f32[2,96,256]{2,1,0:T(8,128)S(1)}, f32[2,96,256]{2,1,0:T(8,128)S(1)}, u32[]{:S(2)}, u32[]{:S(2)}) collective-permute-start(f32[2,96,256]{2,1,0:T(8,128)S(1)} %maximum_select_fusion.2), channel_id=1, source_target_pairs={{0,4},{4,0},{8,12},{12,8},{16,20},{20,16},{24,28},{28,24},{32,36},... | collective-permute-start | bytes 589832 | tf_op jit(solution)/shard_map/ppermute | solution.py:31

commit v4 on v3

v4 whole, which is shorter than its diff:
```python
import jax
import jax.numpy as jnp
from jax import lax
from jax.sharding import PartitionSpec as P

FACTOR = 4
E = 32
EDGE = 64
S0, S1, S2, S3 = 1.0, 4.0, 16.0, 64.0


def wide(v, e):
    return jnp.pad(v, [(0, 0)] * (v.ndim - 2) + [(e, e), (0, 0)])


def regrow(v, before, after):
    return wide(v, after - before)


def edged(v):
    return jnp.pad(v, [(0, 0)] * (v.ndim - 1) + [(EDGE, EDGE)])


def shift(v, axis, by):
    n = lax.axis_size(axis)
    return lax.ppermute(v, axis, [(i, (i + by) % n) for i in range(n)])


def swap(v, bit):
    n = lax.axis_size("tm")
    return lax.ppermute(v, "tm", [(i, i ^ bit) for i in range(n)])


def hold(*values):
    return lax.optimization_barrier(values)


def step(v, d, s):
    q = jnp.pad(v, [(0, 0)] * (v.ndim - 2) + [(1, 1), (1, 1)])
    lap = q[..., 2:, 1:-1] + q[..., :-2, 1:-1] + q[..., 1:-1, 2:] + q[..., 1:-1, :-2] - 4.0 * v
    return v + (s * d) * lap


def steps(v, d, s, k):
    for _ in range(k):
        v = step(v, d, s)
    return v


def per_device(initial, diffusivity, forcing, guessed):
    p = lax.axis_index("tm")
    y = lax.axis_index("space")
    ny = lax.axis_size("space")
    rows, columns = diffusivity.shape
    z, x, c = p // 8, (p // 2) % 4, p % 2
    h = x // 2
    odd = x % 2 == 1
    upper = odd != (h == 1)
    core0 = c == 0
    zero = jnp.float32(0)

    sources = forcing.reshape((FACTOR, FACTOR) + forcing.shape[1:])
    first = jnp.where(p == 0, initial, zero)[None]
    above = shift(diffusivity[rows - E :], "space", 1)
    below = shift(diffusivity[:E], "space", -1)

    cur = wide(jnp.concatenate([first, guessed], 0), 8)
    src = wide(sources, 8)
    above, below, cur = hold(above, below, cur)
    above = jnp.where(y == 0, zero, above)
    below = jnp.where(y == ny - 1, zero, below)
    dwide = jnp.concatenate([above, diffusivity, below], 0)

    def dext(e):
        return dwide[E - e : E + rows + e]

    for i in range(FACTOR):
        cur = step(cur, dext(8), S0)
        cur = jnp.concatenate([cur[:4] + src[:, i], cur[4:]], 0)
    relaxed, gw = cur[:4], cur[4]
    d = relaxed - wide(guessed, 8)
    dw = regrow(d, 8, 16)
    gw16 = regrow(gw, 8, 16)
    d16 = dext(16)
    xf = step(dw[0], d16, S1) + dw[1]
    xf = step(xf, d16, S1) + dw[2]
    yf = steps(step(dw[3], d16, S1) + gw16, d16, S1, 2)
    xy = steps(jnp.stack([xf, yf]), d16, S0, 4)
    xy, dheld = hold(xy, dwide)
    d24 = dext(24)
    own = steps(regrow(d[:2], 8, 24), d24, S0, 2)
    theirs, own = hold(swap(xy, 1), own)

    dpad = edged(dheld)
    dhalf = jnp.where(core0, dpad[:, :384], dpad[:, 256:])
    dquarter = jnp.where(upper, dhalf[:, 128:], dhalf[:, :256])

    def half(v):
        w = edged(v)
        return jnp.where(core0, w[..., :384], w[..., 256:])

    mine_h, theirs_h = half(xy), half(theirs)
    x0 = jnp.where(core0, mine_h[0], theirs_h[0])
    x1 = jnp.where(core0, theirs_h[0], mine_h[0])
    y0 = jnp.where(core0, mine_h[1], theirs_h[1])
    y1 = jnp.where(core0, theirs_h[1], mine_h[1])
    r = x1 + y0
    dh = dhalf[E - 16 : E + rows + 16]
    t = step(jnp.where(odd, r, x0), dh, S2) + jnp.where(odd, y1, r)
    t = step(t, dh, S2)
    f1 = jnp.where(odd, x0, t + y1)
    f2 = jnp.where(odd, step(t, dh, S2), zero)
    xy0 = jnp.where(core0, xy, theirs)
    xy1 = jnp.where(core0, theirs, xy)
    rfull = xy1[0] + xy0[1]
    rfull_y = jnp.stack([rfull, xy1[1]])
    rpart = jnp.where(core0, rfull_y[:, :48], rfull_y[:, 48:])
    ff, own, d3gw, rpart = hold(
        jnp.stack([f1, f2]), own, jnp.stack([d[3], gw])[:, 4:-4], rpart
    )
    keep = jnp.where(upper, ff[..., 128:], ff[..., :256])
    give = jnp.where(upper, ff[..., :256], ff[..., 128:])
    def r24(v):
        return regrow(v, 16, 24)

    own = steps(own, d24, S0, 2)
    other, own = hold(swap(give, 2), own)
    keep = keep + other

    def dq(e):
        return dquarter[E - e : E + rows + e]

    def to_psi(v):
        g = step(v[0], dq(16), S3) + v[1]
        return jnp.where(low, step(g, dq(16), S3), g)

    low = h == 0
    psi = to_psi(keep)
    before, after, rpart, d3gw = hold(
        shift(keep, "tm", 8),
        shift(psi, "tm", -8),
        shift(rpart, "tm", 2),
        shift(d3gw, "tm", 1),
    )
    before = jnp.where(z >= 1, before, zero)
    last = z == 7
    u = steps(regrow(to_psi(before), 16, 20), dq(20), S3, 2) + regrow(psi, 16, 20)
    u = jnp.where(last, zero, steps(u, dq(20), S3, 2)) + regrow(after, 16, 20)

    q0 = (z == 0) & (x == 0)
    d3gw = regrow(jnp.where(p == 0, zero, d3gw), 4, 16)
    rpart = jnp.where(q0, zero, rpart)
    dz = dq(32)
    bw, kw = regrow(before, 16, 32), regrow(keep, 16, 32)
    eps = jnp.where(low, bw[0], zero)
    tau = jnp.where(low, bw[1], bw[0])
    tau1 = jnp.where(low, kw[0], bw[1])
    tau2 = jnp.where(low, kw[1], kw[0])
    eps1 = step(eps, dz, S3) + tau
    eps2 = step(eps1, dz, S3) + tau1
    near = steps(jnp.stack([eps, eps1, eps2]), dz, S2, 4) + jnp.stack([tau, tau1, tau2])
    sent = steps(r24(d3gw), d24, S0, 4)
    u3raw = shift(u, "tm", 24)
    u6, ry2, near, sent = hold(shift(u, "tm", -16), swap(rpart, 1), near, sent)
    ry = jnp.where(
        core0, jnp.concatenate([rpart, ry2], 1), jnp.concatenate([ry2, rpart], 1)
    )
    rp, yp = ry[0], ry[1]
    s1 = step(rp, d16, S2) + xy0[0] + yp
    s1 = jnp.where(core0, s1[:, :256], s1[:, 256:])
    u6 = steps(jnp.where(z >= 5, regrow(u6, 20, 32), zero), dz, S3, 6)
    u3, u6 = hold(u3raw, u6)
    u3 = jnp.where(z >= 2, u3, zero)
    far = regrow(u3, 20, 32) + u6
    far = steps(far, dz, S2, 4)
    far1 = step(far, dz, S3)
    zs = near + jnp.stack([far, far1, step(far1, dz, S3)])
    zs = zs[..., EDGE:-EDGE]
    keep = jnp.where(low, zs[:2], zs[1:])
    give = jnp.where(low, zs[1:], zs[:2])

    gwp = r24(d3gw[1])
    a3p, a0, a1 = sent[0], own[0] + sent[1], own[1]
    rprev = jnp.where(core0, r24(rp), r24(xy0[0] + yp))
    rown = jnp.where(core0, r24(xy0[0] + yp), r24(rfull))
    ea = jnp.where(core0, zero, r24(rp))
    eb = step(ea, d24, S2) + rprev
    eb = jnp.where(odd & (c == 1), zero, eb)
    pair = steps(jnp.stack([ea, eb]), d24, S1, 4)
    y_1 = step(rprev + pair[0], d24, S1) + a3p
    y_2 = step(y_1, d24, S1) + a0
    y_3 = step(y_2, d24, S1) + a1
    rel = regrow(relaxed, 8, 24)
    local = jnp.stack([rel[0] + gwp + y_1, rel[1] + y_2, rel[2] + y_3, rel[3] + rown + pair[1]])

    other, s1x, local = hold(swap(give, 6), swap(s1, 2), local)
    keep = keep + other
    s1x = jnp.where(odd, s1x, zero)

    n = rows + 2 * E

    m = rows + 48

    def packed(v, w):
        return jnp.concatenate([v[0, :24], v[0, 24:], v[1, :24], v[1, 24:], w], 1)

    def unpacked(v):
        z0 = jnp.concatenate([v[:, :128], v[:, 128:256]], 0)
        z1 = jnp.concatenate([v[:, 256:384], v[:, 384:512]], 0)
        return jnp.stack([z0, z1]), v[:, 512:]

    from_above, from_below = hold(
        shift(packed(keep[:, n - 48 :], s1x[-24:]), "space", 1),
        shift(packed(keep[:, :48], s1x[:24]), "space", -1),
    )
    from_above = jnp.where(y == 0, zero, from_above)
    from_below = jnp.where(y == ny - 1, zero, from_below)
    za, sa = unpacked(from_above)
    zb, sb = unpacked(from_below)
    keep = keep[:, 16:-16] + jnp.concatenate([za, zb], 1)
    s1g = s1x + jnp.pad(sa, ((8, 64), (0, 0))) + jnp.pad(sb, ((64, 8), (0, 0)))
    other, la, lb = hold(
        swap(keep, 2), shift(local[:, m - 24 :], "space", 1), shift(local[:, :24], "space", -1)
    )
    la = jnp.where(y == 0, zero, la)
    lb = jnp.where(y == ny - 1, zero, lb)
    keep = jnp.where(upper, jnp.concatenate([other, keep], 2), jnp.concatenate([keep, other], 2))
    keep = jnp.concatenate([keep, s1g[None]], 0)
    other = swap(keep, 1)
    both = jnp.where(
        core0, jnp.concatenate([keep, other], 2), jnp.concatenate([other, keep], 2)
    )
    d8 = dext(8)
    q = jnp.where(odd, steps(both[0], d16, S2, 2) + both[2], both[0])[8:-8]
    both = steps(jnp.stack([q, both[1, 8:-8]]), d8, S1, 4)
    q, zn = both[0], both[1]
    q = jnp.where(core0, q, step(q, d8, S2))
    e2b = jnp.where(odd & (c == 1), zn, step(q, d8, S2))
    t1 = step(q, d8, S1)
    t2 = step(t1, d8, S1)
    t3 = step(t2, d8, S1)
    correction = jnp.stack([t1, t2, t3, e2b])[:, 8:-8]

    inner = local[:, 24:-24]
    inner = (
        inner
        + jnp.pad(la, ((0, 0), (0, rows - 24), (0, 0)))
        + jnp.pad(lb, ((0, 0), (rows - 24, 0), (0, 0)))
    )
    return inner + correction


def solution(mesh):
    return jax.shard_map(
        per_device,
        mesh=mesh,
        in_specs=(
            P("space", None),
            P("space", None),
            P("tm", "space", None),
            P("tm", "space", None),
        ),
        out_specs=P("tm", "space", None),
        check_vma=False,
    )
```

time: 81.3 us -> 76 us (0.935)
  waiting for transfers between devices: 21.7 us -> 17.6 us
  other arithmetic: 21.9 us -> 19.9 us
  starting transfers between devices: 33.4 us -> 34.5 us
  local copies, waits for them, and re-layouts: 2.74 us -> 1.78 us
    ppermute x12, waiting for transfers between devices: 13.3 us -> 9.46 us  [shift(): return lax.ppermute(v, axis, [(i, (i + by) % n) for i in range(n)])]
    ppermute x7, starting transfers between devices: 13.2 us -> 15.4 us  [swap(): return lax.ppermute(v, 'tm', [(i, i ^ bit) for i in range(n)])]
    add x48 -> x44, other arithmetic: 12.2 us -> 11.1 us  [step(): return v + s * d * lap]
    ppermute x12, starting transfers between devices: 20.1 us -> 19.1 us  [shift(): return lax.ppermute(v, axis, [(i, (i + by) % n) for i in range(n)])]
  transfers between devices with their start and end apart: 19 -> 19, of which waited for: 10 -> 13; matrix products, arithmetic and copies ran while one was open for 15% -> 12% of each run, Pallas kernels for 0% -> 0%
where the time goes in v4:
time: 76 us; the launch traced here: 75.2 us
  starting transfers between devices  34.5 us (45%)
  other arithmetic  19.9 us (26%)
  waiting for transfers between devices  17.6 us (23%)
  local copies, waits for them, and re-layouts  1.78 us (2%)
  between operations  1.34 us (2%)
    ppermute x12, starting transfers between devices, shift(): return lax.ppermute(v, axis, [(i, (i + by) % n) for i in range(n)])  19.1 us
    ppermute x7, starting transfers between devices, swap(): return lax.ppermute(v, 'tm', [(i, i ^ bit) for i in range(n)])  15.4 us
    add x44, other arithmetic, step(): return v + s * d * lap  11.1 us
    ppermute x12, waiting for transfers between devices, shift(): return lax.ppermute(v, axis, [(i, (i + by) % n) for i in range(n)])  9.46 us
    ppermute x7, waiting for transfers between devices, swap(): return lax.ppermute(v, 'tm', [(i, i ^ bit) for i in range(n)])  8.14 us
  transfers between devices with their start and end apart: 19, of which 13 were waited for; matrix products, arithmetic and copies ran while one was open for 12% of the time, Pallas kernels for 0%

profile of v4, /device:TPU:1, one launch (start us, length us, event | category | flops | bytes accessed | tf_op | source)
XLA Modules:
  0.0 75.2 jit_solution(12078673928443997533)
XLA Ops:
  0.0 0.9 %fusion.489 = (f32[32,512]{1,0:T(8,128)S(1)}, f32[32,512]{1,0:T(8,128)S(1)}) fusion(f32[64,512]{1,0:T(8,128)} %param.5), kind=kLoop, calls=%fused_computation.894 | loop fusion | bytes 262144 | tf_op jit(solution)/shard_map/slice | solution.py:65
  0.9 3.6 %collective-permute-start.1 = (f32[32,512]{1,0:T(8,128)S(1)}, f32[32,512]{1,0:T(8,128)S(1)}, u32[]{:S(2)}, u32[]{:S(2)}) collective-permute-start(f32[32,512]{1,0:T(8,128)S(1)} %get-tuple-element.120), channel_id=1, source_target_pairs={{0,3},{1,0},{2,1},{3,2},{4,7},{5,4},{6,5},{7,6},{8,11},{9,8},{10,9... | collective-permute-start | bytes 196616 | tf_op jit(solution)/shard_map/ppermute | solution.py:26
  4.6 1.1 %select_maximum_fusion = f32[5,80,512]{2,1,0:T(8,128)S(1)} fusion(f32[4,64,512]{2,1,0:T(8,128)} %param.7, f32[1,64,512]{2,1,0:T(8,128)S(1)} %select_bitcast_fusion), kind=kLoop, calls=%fused_computation.71 | loop fusion | flops 1228800 | bytes 1474560 | tf_op jit(solution)/shard_map/concatenate | solution.py:67
  5.9 3.0 %collective-permute-done = f32[32,512]{1,0:T(8,128)S(1)} collective-permute-done((f32[32,512]{1,0:T(8,128)S(1)}, f32[32,512]{1,0:T(8,128)S(1)}, u32[]{:S(2)}, u32[]{:S(2)}) %collective-permute-start) | collective-permute-done | bytes 65568 | tf_op jit(solution)/shard_map/ppermute | solution.py:26
  9.0 0.5 fusion.5
  9.7 0.5 fusion.11
  10.4 0.5 fusion.17
  11.2 0.5 fusion.23
  11.7 0.4 copy-done.1
  12.7 0.3 fusion.488
  13.2 0.3 fusion.111
  13.5 0.3 fusion.117
  13.8 0.3 fusion.123
  14.1 0.3 fusion.129
  14.3 2.2 %collective-permute-start.2 = (f32[2,96,512]{2,1,0:T(8,128)S(1)}, f32[2,96,512]{2,1,0:T(8,128)S(1)}, u32[]{:S(2)}, u32[]{:S(2)}) collective-permute-start(f32[2,96,512]{2,1,0:T(8,128)S(1)} %fusion.129), channel_id=1, source_target_pairs={{0,4},{4,0},{8,12},{12,8},{16,20},{20,16},{24,28},{28,24},{32,36},... | collective-permute-start | bytes 1179656 | tf_op jit(solution)/shard_map/ppermute | solution.py:31
  16.6 0.3 fusion.39
  17.1 0.2 fusion.179
  17.4 0.3 fusion.45
  17.9 0.2 fusion.180
  18.8 0.3 fusion.51
  19.2 1.3 %collective-permute-start.3 = (f32[2,96,256]{2,1,0:T(8,128)S(1)}, f32[2,96,256]{2,1,0:T(8,128)S(1)}, u32[]{:S(2)}, u32[]{:S(2)}) collective-permute-start(f32[2,96,256]{2,1,0:T(8,128)S(1)} %slice_select_fusion), channel_id=1, source_target_pairs={{0,8},{4,12},{8,0},{12,4},{16,24},{20,28},{24,16},{28,20},{32,40},... | collective-permute-start | bytes 589832 | tf_op jit(solution)/shard_map/ppermute | solution.py:31
  20.5 0.3 collective-permute-start.6
  20.7 2.7 %collective-permute-start.7 = (f32[2,72,512]{2,1,0:T(8,128)S(1)}, f32[2,72,512]{2,1,0:T(8,128)S(1)}, u32[]{:S(2)}, u32[]{:S(2)}) collective-permute-start(f32[2,72,512]{2,1,0:T(8,128)S(1)} %pad_maximum_fusion.11), channel_id=1, source_target_pairs={{0,4},{4,8},{8,12},{12,16},{16,20},{20,24},{24,28},{28,32},{32,36}... | collective-permute-start | bytes 884744 | tf_op jit(solution)/shard_map/ppermute | solution.py:26
  23.4 0.3 fusion.57
  23.7 1.6 %collective-permute-done.3 = f32[2,96,256]{2,1,0:T(8,128)S(1)} collective-permute-done((f32[2,96,256]{2,1,0:T(8,128)S(1)}, f32[2,96,256]{2,1,0:T(8,128)S(1)}, u32[]{:S(2)}, u32[]{:S(2)}) %collective-permute-start.3) | collective-permute-done | bytes 196640 | tf_op jit(solution)/shard_map/ppermute | solution.py:31
  25.4 1.9 %collective-permute-start.4 = (f32[2,96,256]{2,1,0:T(8,128)S(1)}, f32[2,96,256]{2,1,0:T(8,128)S(1)}, u32[]{:S(2)}, u32[]{:S(2)}) collective-permute-start(f32[2,96,256]{2,1,0:T(8,128)S(1)} %select_add_fusion), channel_id=1, source_target_pairs={{0,32},{4,36},{8,40},{12,44},{16,48},{20,52},{24,56},{28,60},{32,6... | collective-permute-start | bytes 589832 | tf_op jit(solution)/shard_map/ppermute | solution.py:26
  27.6 4.0 %collective-permute-start.5 = (f32[96,256]{1,0:T(8,128)S(1)}, f32[96,256]{1,0:T(8,128)S(1)}, u32[]{:S(2)}, u32[]{:S(2)}) collective-permute-start(f32[96,256]{1,0:T(8,128)S(1)} %add_select_fusion.2), channel_id=1, source_target_pairs={{0,224},{4,228},{8,232},{12,236},{16,240},{20,244},{24,248},{28,25... | collective-permute-start | bytes 294920 | tf_op jit(solution)/shard_map/ppermute | solution.py:26
  31.6 0.6 collective-permute-done.6
  32.2 1.0 %collective-permute-done.5 = f32[96,256]{1,0:T(8,128)S(1)} collective-permute-done((f32[96,256]{1,0:T(8,128)S(1)}, f32[96,256]{1,0:T(8,128)S(1)}, u32[]{:S(2)}, u32[]{:S(2)}) %collective-permute-start.5) | collective-permute-done | bytes 98336 | tf_op jit(solution)/shard_map/ppermute | solution.py:26
  33.3 2.0 %collective-permute-done.4 = f32[2,96,256]{2,1,0:T(8,128)S(1)} collective-permute-done((f32[2,96,256]{2,1,0:T(8,128)S(1)}, f32[2,96,256]{2,1,0:T(8,128)S(1)}, u32[]{:S(2)}, u32[]{:S(2)}) %collective-permute-start.4) | collective-permute-done | bytes 196640 | tf_op jit(solution)/shard_map/ppermute | solution.py:26
  36.1 2.7 %collective-permute-start.10 = (f32[104,256]{1,0:T(8,128)S(1)}, f32[104,256]{1,0:T(8,128)S(1)}, u32[]{:S(2)}, u32[]{:S(2)}) collective-permute-start(f32[104,256]{1,0:T(8,128)S(1)} %fusion.453), channel_id=1, source_target_pairs={{0,96},{4,100},{8,104},{12,108},{16,112},{20,116},{24,120},{28,124... | collective-permute-start | bytes 319496 | tf_op jit(solution)/shard_map/ppermute | solution.py:26
  38.8 0.8 %collective-permute-start.8 = (f32[104,256]{1,0:T(8,128)S(1)}, f32[104,256]{1,0:T(8,128)S(1)}, u32[]{:S(2)}, u32[]{:S(2)}) collective-permute-start(f32[104,256]{1,0:T(8,128)S(1)} %fusion.453), channel_id=1, source_target_pairs={{0,192},{4,196},{8,200},{12,204},{16,208},{20,212},{24,216},{28,22... | collective-permute-start | bytes 319496 | tf_op jit(solution)/shard_map/ppermute | solution.py:26
  40.0 0.3 fusion.135
  40.3 0.3 fusion.141
  40.5 0.3 fusion.147
  40.9 2.2 %collective-permute-start.9 = (f32[2,48,512]{2,1,0:T(8,128)S(1)}, f32[2,48,512]{2,1,0:T(8,128)S(1)}, u32[]{:S(2)}, u32[]{:S(2)}) collective-permute-start(f32[2,48,512]{2,1,0:T(8,128)S(1)} %broadcast_select_fusion.5), channel_id=1, source_target_pairs={{0,4},{4,0},{8,12},{12,8},{16,20},{20,16},{24,28},{28,24},{32,36},... | collective-permute-start | bytes 589832 | tf_op jit(solution)/shard_map/ppermute | solution.py:31
  43.2 0.3 fusion.63
  43.5 0.3 fusion.69
  43.8 0.3 fusion.75
  44.2 0.3 fusion.81
  44.5 0.3 fusion.154
  45.8 0.2 fusion.284
  47.1 4.2 %collective-permute-start.11 = (f32[2,128,128]{2,1,0:T(8,128)S(1)}, f32[2,128,128]{2,1,0:T(8,128)S(1)}, u32[]{:S(2)}, u32[]{:S(2)}) collective-permute-start(f32[2,128,128]{2,1,0:T(8,128)S(1)} %slice_select_fusion.5), channel_id=1, source_target_pairs={{0,24},{4,28},{8,16},{12,20},{16,8},{20,12},{24,0},{28,4},{32,56},... | collective-permute-start | bytes 393224 | tf_op jit(solution)/shard_map/ppermute | solution.py:31
  51.4 0.2 broadcast_multiply_fusion
  51.7 0.3 fusion.87
  52.0 0.3 fusion.93
  52.3 0.3 fusion.99
  52.6 0.3 fusion.105
  53.2 0.2 fusion.222
  53.4 0.2 fusion.215
  53.7 1.4 %collective-permute-done.12 = f32[96,256]{1,0:T(8,128)S(1)} collective-permute-done((f32[96,256]{1,0:T(8,128)S(1)}, f32[96,256]{1,0:T(8,128)S(1)}, u32[]{:S(2)}, u32[]{:S(2)}) %collective-permute-start.12) | collective-permute-done | bytes 98336 | tf_op jit(solution)/shard_map/ppermute | solution.py:31
  55.5 1.5 %collective-permute-start.13 = (f32[24,768]{1,0:T(8,128)S(1)}, f32[24,768]{1,0:T(8,128)S(1)}, u32[]{:S(2)}, u32[]{:S(2)}) collective-permute-start(f32[24,768]{1,0:T(8,128)S(1)} %get-tuple-element.123), channel_id=1, source_target_pairs={{0,1},{1,2},{2,3},{3,0},{4,5},{5,6},{6,7},{7,4},{8,9},{9,10},{10,1... | collective-permute-start | bytes 221192 | tf_op jit(solution)/shard_map/ppermute | solution.py:26
  56.9 1.6 %collective-permute-start.17 = (f32[4,24,512]{2,1,0:T(8,128)S(1)}, f32[4,24,512]{2,1,0:T(8,128)S(1)}, u32[]{:S(2)}, u32[]{:S(2)}) collective-permute-start(f32[4,24,512]{2,1,0:T(8,128)S(1)} %get-tuple-element.83), channel_id=1, source_target_pairs={{0,3},{1,0},{2,1},{3,2},{4,7},{5,4},{6,5},{7,6},{8,11},{9,8},{10,9... | collective-permute-start | bytes 589832 | tf_op jit(solution)/shard_map/ppermute | solution.py:26
  58.7 1.5 %collective-permute-done.13 = f32[24,768]{1,0:T(8,128)S(1)} collective-permute-done((f32[24,768]{1,0:T(8,128)S(1)}, f32[24,768]{1,0:T(8,128)S(1)}, u32[]{:S(2)}, u32[]{:S(2)}) %collective-permute-start.13) | collective-permute-done | bytes 73760 | tf_op jit(solution)/shard_map/ppermute | solution.py:26
  60.5 3.7 %collective-permute-done.15 = f32[2,96,128]{2,1,0:T(8,128)S(1)} collective-permute-done((f32[2,96,128]{2,1,0:T(8,128)S(1)}, f32[2,96,128]{2,1,0:T(8,128)S(1)}, u32[]{:S(2)}, u32[]{:S(2)}) %collective-permute-start.15) | collective-permute-done | bytes 98336 | tf_op jit(solution)/shard_map/ppermute | solution.py:31
  64.2 1.1 %collective-permute-done.16 = f32[4,24,512]{2,1,0:T(8,128)S(1)} collective-permute-done((f32[4,24,512]{2,1,0:T(8,128)S(1)}, f32[4,24,512]{2,1,0:T(8,128)S(1)}, u32[]{:S(2)}, u32[]{:S(2)}) %collective-permute-start.16) | collective-permute-done | bytes 196640 | tf_op jit(solution)/shard_map/ppermute | solution.py:26
  65.3 5.3 %collective-permute-start.18 = (f32[3,96,256]{2,1,0:T(8,128)S(1)}, f32[3,96,256]{2,1,0:T(8,128)S(1)}, u32[]{:S(2)}, u32[]{:S(2)}) collective-permute-start(f32[3,96,256]{2,1,0:T(8,128)S(1)} %pad_maximum_fusion.13), channel_id=1, source_target_pairs={{0,4},{4,0},{8,12},{12,8},{16,20},{20,16},{24,28},{28,24},{32,36},... | collective-permute-start | bytes 884744 | tf_op jit(solution)/shard_map/ppermute | solution.py:31
  70.7 1.2 %collective-permute-done.18 = f32[3,96,256]{2,1,0:T(8,128)S(1)} collective-permute-done((f32[3,96,256]{2,1,0:T(8,128)S(1)}, f32[3,96,256]{2,1,0:T(8,128)S(1)}, u32[]{:S(2)}, u32[]{:S(2)}) %collective-permute-start.18) | collective-permute-done | bytes 294944 | tf_op jit(solution)/shard_map/ppermute | solution.py:31
  72.5 0.2 fusion.160
  72.7 0.2 fusion.166
  73.0 0.2 fusion.172
  73.2 0.2 fusion.178
  73.7 0.2 multiply_add_fusion
  74.2 0.9 %fusion.33 = f32[4,64,512]{2,1,0:T(8,128)} fusion(f32[1,80,512]{2,1,0:T(8,128)S(1)} %get-tuple-element.98, f32[1,80,512]{2,1,0:T(8,128)S(1)} %fusion.306, f32[1,80,512]{2,1,0:T(8,128)S(1)} %bitcast.223, f32[1,80,512]{2,1,0:T(8,128)S(1)} %bitcast.222, f32[4,24,512]{2,1,0:T(8,128)S(1)} %broadcast_select_fusion.3, ...), kind=kLoop, calls=%fused_computation.167 | loop fusion | flops 786432 | bytes 2097152 | tf_op jit(solution)/shard_map/add | solution.py:250
  (139 shorter events, 8.3 us)
Async XLA Ops:
  0.0 8.9 %copy-start.2 = (f32[64,512]{1,0:T(8,128)S(1)}, f32[64,512]{1,0:T(8,128)}, u32[]{:S(2)}) copy-start(f32[64,512]{1,0:T(8,128)} %param.5) | copy-start | bytes 393220
  0.9 5.0 %collective-permute-start.1 = (f32[32,512]{1,0:T(8,128)S(1)}, f32[32,512]{1,0:T(8,128)S(1)}, u32[]{:S(2)}, u32[]{:S(2)}) collective-permute-start(f32[32,512]{1,0:T(8,128)S(1)} %get-tuple-element.120), channel_id=1, source_target_pairs={{0,3},{1,0},{2,1},{3,2},{4,7},{5,4},{6,5},{7,6},{8,11},{9,8},{10,9... | collective-permute-start | bytes 196616 | tf_op jit(solution)/shard_map/ppermute | solution.py:26
  4.6 4.3 %collective-permute-start = (f32[32,512]{1,0:T(8,128)S(1)}, f32[32,512]{1,0:T(8,128)S(1)}, u32[]{:S(2)}, u32[]{:S(2)}) collective-permute-start(f32[32,512]{1,0:T(8,128)S(1)} %get-tuple-element.121), channel_id=1, source_target_pairs={{0,1},{1,2},{2,3},{3,0},{4,5},{5,6},{6,7},{7,4},{8,9},{9,10},{10,1... | collective-permute-start | bytes 196616 | tf_op jit(solution)/shard_map/ppermute | solution.py:26
  5.7 3.8 %copy-start = (f32[16,64,512]{2,1,0:T(8,128)S(1)}, f32[16,64,512]{2,1,0:T(8,128)}, u32[]{:S(2)}) copy-start(f32[16,64,512]{2,1,0:T(8,128)} %param.6) | copy-start | bytes 6291460
  11.1 1.0 %copy-start.1 = (f32[4,64,512]{2,1,0:T(8,128)S(1)}, f32[4,64,512]{2,1,0:T(8,128)}, u32[]{:S(2)}) copy-start(f32[4,64,512]{2,1,0:T(8,128)} %param.7) | copy-start | bytes 1572868
  14.3 3.5 %collective-permute-start.2 = (f32[2,96,512]{2,1,0:T(8,128)S(1)}, f32[2,96,512]{2,1,0:T(8,128)S(1)}, u32[]{:S(2)}, u32[]{:S(2)}) collective-permute-start(f32[2,96,512]{2,1,0:T(8,128)S(1)} %fusion.129), channel_id=1, source_target_pairs={{0,4},{4,0},{8,12},{12,8},{16,20},{20,16},{24,28},{28,24},{32,36},... | collective-permute-start | bytes 1179656 | tf_op jit(solution)/shard_map/ppermute | solution.py:31
  19.2 6.2 %collective-permute-start.3 = (f32[2,96,256]{2,1,0:T(8,128)S(1)}, f32[2,96,256]{2,1,0:T(8,128)S(1)}, u32[]{:S(2)}, u32[]{:S(2)}) collective-permute-start(f32[2,96,256]{2,1,0:T(8,128)S(1)} %slice_select_fusion), channel_id=1, source_target_pairs={{0,8},{4,12},{8,0},{12,4},{16,24},{20,28},{24,16},{28,20},{32,40},... | collective-permute-start | bytes 589832 | tf_op jit(solution)/shard_map/ppermute | solution.py:31
  20.5 11.8 %collective-permute-start.6 = (f32[2,48,512]{2,1,0:T(8,128)S(1)}, f32[2,48,512]{2,1,0:T(8,128)S(1)}, u32[]{:S(2)}, u32[]{:S(2)}) collective-permute-start(f32[2,48,512]{2,1,0:T(8,128)S(1)} %fusion.279), channel_id=1, source_target_pairs={{0,8},{4,12},{8,16},{12,20},{16,24},{20,28},{24,32},{28,36},{32,40... | collective-permute-start | bytes 589832 | tf_op jit(solution)/shard_map/ppermute | solution.py:26
  20.7 12.5 %collective-permute-start.7 = (f32[2,72,512]{2,1,0:T(8,128)S(1)}, f32[2,72,512]{2,1,0:T(8,128)S(1)}, u32[]{:S(2)}, u32[]{:S(2)}) collective-permute-start(f32[2,72,512]{2,1,0:T(8,128)S(1)} %pad_maximum_fusion.11), channel_id=1, source_target_pairs={{0,4},{4,8},{8,12},{12,16},{16,20},{20,24},{24,28},{28,32},{32,36}... | collective-permute-start | bytes 884744 | tf_op jit(solution)/shard_map/ppermute | solution.py:26
  25.4 9.9 %collective-permute-start.4 = (f32[2,96,256]{2,1,0:T(8,128)S(1)}, f32[2,96,256]{2,1,0:T(8,128)S(1)}, u32[]{:S(2)}, u32[]{:S(2)}) collective-permute-start(f32[2,96,256]{2,1,0:T(8,128)S(1)} %select_add_fusion), channel_id=1, source_target_pairs={{0,32},{4,36},{8,40},{12,44},{16,48},{20,52},{24,56},{28,60},{32,6... | collective-permute-start | bytes 589832 | tf_op jit(solution)/shard_map/ppermute | solution.py:26
  27.6 5.7 %collective-permute-start.5 = (f32[96,256]{1,0:T(8,128)S(1)}, f32[96,256]{1,0:T(8,128)S(1)}, u32[]{:S(2)}, u32[]{:S(2)}) collective-permute-start(f32[96,256]{1,0:T(8,128)S(1)} %add_select_fusion.2), channel_id=1, source_target_pairs={{0,224},{4,228},{8,232},{12,236},{16,240},{20,244},{24,248},{28,25... | collective-permute-start | bytes 294920 | tf_op jit(solution)/shard_map/ppermute | solution.py:26
  36.1 9.9 %collective-permute-start.10 = (f32[104,256]{1,0:T(8,128)S(1)}, f32[104,256]{1,0:T(8,128)S(1)}, u32[]{:S(2)}, u32[]{:S(2)}) collective-permute-start(f32[104,256]{1,0:T(8,128)S(1)} %fusion.453), channel_id=1, source_target_pairs={{0,96},{4,100},{8,104},{12,108},{16,112},{20,116},{24,120},{28,124... | collective-permute-start | bytes 319496 | tf_op jit(solution)/shard_map/ppermute | solution.py:26
  38.8 6.0 %collective-permute-start.8 = (f32[104,256]{1,0:T(8,128)S(1)}, f32[104,256]{1,0:T(8,128)S(1)}, u32[]{:S(2)}, u32[]{:S(2)}) collective-permute-start(f32[104,256]{1,0:T(8,128)S(1)} %fusion.453), channel_id=1, source_target_pairs={{0,192},{4,196},{8,200},{12,204},{16,208},{20,212},{24,216},{28,22... | collective-permute-start | bytes 319496 | tf_op jit(solution)/shard_map/ppermute | solution.py:26
  40.9 3.9 %collective-permute-start.9 = (f32[2,48,512]{2,1,0:T(8,128)S(1)}, f32[2,48,512]{2,1,0:T(8,128)S(1)}, u32[]{:S(2)}, u32[]{:S(2)}) collective-permute-start(f32[2,48,512]{2,1,0:T(8,128)S(1)} %broadcast_select_fusion.5), channel_id=1, source_target_pairs={{0,4},{4,0},{8,12},{12,8},{16,20},{20,16},{24,28},{28,24},{32,36},... | collective-permute-start | bytes 589832 | tf_op jit(solution)/shard_map/ppermute | solution.py:31
  47.1 8.0 %collective-permute-start.11 = (f32[2,128,128]{2,1,0:T(8,128)S(1)}, f32[2,128,128]{2,1,0:T(8,128)S(1)}, u32[]{:S(2)}, u32[]{:S(2)}) collective-permute-start(f32[2,128,128]{2,1,0:T(8,128)S(1)} %slice_select_fusion.5), channel_id=1, source_target_pairs={{0,24},{4,28},{8,16},{12,20},{16,8},{20,12},{24,0},{28,4},{32,56},... | collective-permute-start | bytes 393224 | tf_op jit(solution)/shard_map/ppermute | solution.py:31
  51.3 3.8 %collective-permute-start.12 = (f32[96,256]{1,0:T(8,128)S(1)}, f32[96,256]{1,0:T(8,128)S(1)}, u32[]{:S(2)}, u32[]{:S(2)}) collective-permute-start(f32[96,256]{1,0:T(8,128)S(1)} %slice_select_fusion.6), channel_id=1, source_target_pairs={{0,8},{4,12},{8,0},{12,4},{16,24},{20,28},{24,16},{28,20},{32,40},... | collective-permute-start | bytes 294920 | tf_op jit(solution)/shard_map/ppermute | solution.py:31
  55.4 3.3 %collective-permute-start.14 = (f32[24,768]{1,0:T(8,128)S(1)}, f32[24,768]{1,0:T(8,128)S(1)}, u32[]{:S(2)}, u32[]{:S(2)}) collective-permute-start(f32[24,768]{1,0:T(8,128)S(1)} %get-tuple-element.122), channel_id=1, source_target_pairs={{0,3},{1,0},{2,1},{3,2},{4,7},{5,4},{6,5},{7,6},{8,11},{9,8},{10,9... | collective-permute-start | bytes 221192 | tf_op jit(solution)/shard_map/ppermute | solution.py:26
  55.5 4.7 %collective-permute-start.13 = (f32[24,768]{1,0:T(8,128)S(1)}, f32[24,768]{1,0:T(8,128)S(1)}, u32[]{:S(2)}, u32[]{:S(2)}) collective-permute-start(f32[24,768]{1,0:T(8,128)S(1)} %get-tuple-element.123), channel_id=1, source_target_pairs={{0,1},{1,2},{2,3},{3,0},{4,5},{5,6},{6,7},{7,4},{8,9},{9,10},{10,1... | collective-permute-start | bytes 221192 | tf_op jit(solution)/shard_map/ppermute | solution.py:26
  56.9 7.2 %collective-permute-start.17 = (f32[4,24,512]{2,1,0:T(8,128)S(1)}, f32[4,24,512]{2,1,0:T(8,128)S(1)}, u32[]{:S(2)}, u32[]{:S(2)}) collective-permute-start(f32[4,24,512]{2,1,0:T(8,128)S(1)} %get-tuple-element.83), channel_id=1, source_target_pairs={{0,3},{1,0},{2,1},{3,2},{4,7},{5,4},{6,5},{7,6},{8,11},{9,8},{10,9... | collective-permute-start | bytes 589832 | tf_op jit(solution)/shard_map/ppermute | solution.py:26
  58.5 6.7 %collective-permute-start.16 = (f32[4,24,512]{2,1,0:T(8,128)S(1)}, f32[4,24,512]{2,1,0:T(8,128)S(1)}, u32[]{:S(2)}, u32[]{:S(2)}) collective-permute-start(f32[4,24,512]{2,1,0:T(8,128)S(1)} %get-tuple-element.84), channel_id=1, source_target_pairs={{0,1},{1,2},{2,3},{3,0},{4,5},{5,6},{6,7},{7,4},{8,9},{9,10},{10,1... | collective-permute-start | bytes 589832 | tf_op jit(solution)/shard_map/ppermute | solution.py:26
  60.3 3.8 %collective-permute-start.15 = (f32[2,96,128]{2,1,0:T(8,128)S(1)}, f32[2,96,128]{2,1,0:T(8,128)S(1)}, u32[]{:S(2)}, u32[]{:S(2)}) collective-permute-start(f32[2,96,128]{2,1,0:T(8,128)S(1)} %slice_add_fusion.3), channel_id=1, source_target_pairs={{0,8},{4,12},{8,0},{12,4},{16,24},{20,28},{24,16},{28,20},{32,40},... | collective-permute-start | bytes 294920 | tf_op jit(solution)/shard_map/ppermute | solution.py:31
  65.3 6.6 %collective-permute-start.18 = (f32[3,96,256]{2,1,0:T(8,128)S(1)}, f32[3,96,256]{2,1,0:T(8,128)S(1)}, u32[]{:S(2)}, u32[]{:S(2)}) collective-permute-start(f32[3,96,256]{2,1,0:T(8,128)S(1)} %pad_maximum_fusion.13), channel_id=1, source_target_pairs={{0,4},{4,0},{8,12},{12,8},{16,20},{20,16},{24,28},{28,24},{32,36},... | collective-permute-start | bytes 884744 | tf_op jit(solution)/shard_map/ppermute | solution.py:31

commit v5 on v4

--- a/solution.py
+++ b/solution.py
@@ -5,7 +5,7 @@
 
 FACTOR = 4
 E = 32
-EDGE = 64
+EDGE = 32
 S0, S1, S2, S3 = 1.0, 4.0, 16.0, 64.0
 
 
@@ -33,6 +33,19 @@
 
 def hold(*values):
     return lax.optimization_barrier(values)
+
+
+def thin(v):
+    r = v.shape[-2]
+    k = -(-r // 16) * 8
+    tail = jnp.concatenate([v[..., :k, 128:], v[..., r - k :, 128:]], -1)
+    return jnp.concatenate([v[..., :128], tail], -2)
+
+
+def thick(m, r):
+    k = -(-r // 16) * 8
+    low, high = m[..., r:, :64], m[..., r + 2 * k - r :, 64:]
+    return jnp.concatenate([m[..., :r, :], jnp.concatenate([low, high], -2)], -1)
 
 
 def step(v, d, s):
@@ -92,12 +105,12 @@
     theirs, own = hold(swap(xy, 1), own)
 
     dpad = edged(dheld)
-    dhalf = jnp.where(core0, dpad[:, :384], dpad[:, 256:])
-    dquarter = jnp.where(upper, dhalf[:, 128:], dhalf[:, :256])
+    dhalf = jnp.where(core0, dpad[:, :320], dpad[:, 256:])
+    dquarter = jnp.where(upper, dhalf[:, 128:], dhalf[:, :192])
 
     def half(v):
         w = edged(v)
-        return jnp.where(core0, w[..., :384], w[..., 256:])
+        return jnp.where(core0, w[..., :320], w[..., 256:])
 
     mine_h, theirs_h = half(xy), half(theirs)
     x0 = jnp.where(core0, mine_h[0], theirs_h[0])
@@ -118,14 +131,15 @@
     ff, own, d3gw, rpart = hold(
         jnp.stack([f1, f2]), own, jnp.stack([d[3], gw])[:, 4:-4], rpart
     )
-    keep = jnp.where(upper, ff[..., 128:], ff[..., :256])
-    give = jnp.where(upper, ff[..., :256], ff[..., 128:])
+    keep = jnp.where(upper, ff[..., 128:], ff[..., :192])
+    give = jnp.where(upper, ff[..., :192], ff[..., 128:])
     def r24(v):
         return regrow(v, 16, 24)
 
     own = steps(own, d24, S0, 2)
-    other, own = hold(swap(give, 2), own)
-    keep = keep + other
+    other, own, packed_keep = hold(swap(thin(give), 2), own, thin(keep))
+    packed_keep = packed_keep + other
+    keep = thick(packed_keep, 96)
 
     def dq(e):
         return dquarter[E - e : E + rows + e]
@@ -137,12 +151,13 @@
     low = h == 0
     psi = to_psi(keep)
     before, after, rpart, d3gw = hold(
-        shift(keep, "tm", 8),
-        shift(psi, "tm", -8),
+        shift(packed_keep, "tm", 8),
+        shift(thin(psi), "tm", -8),
         shift(rpart, "tm", 2),
         shift(d3gw, "tm", 1),
     )
-    before = jnp.where(z >= 1, before, zero)
+    before = jnp.where(z >= 1, thick(before, 96), zero)
+    after = thick(after, 96)
     last = z == 7
     u = steps(regrow(to_psi(before), 16, 20), dq(20), S3, 2) + regrow(psi, 16, 20)
     u = jnp.where(last, zero, steps(u, dq(20), S3, 2)) + regrow(after, 16, 20)
@@ -160,17 +175,17 @@
     eps2 = step(eps1, dz, S3) + tau1
     near = steps(jnp.stack([eps, eps1, eps2]), dz, S2, 4) + jnp.stack([tau, tau1, tau2])
     sent = steps(r24(d3gw), d24, S0, 4)
-    u3raw = shift(u, "tm", 24)
-    u6, ry2, near, sent = hold(shift(u, "tm", -16), swap(rpart, 1), near, sent)
+    u3raw = shift(thin(u), "tm", 24)
+    u6, ry2, near, sent = hold(shift(thin(u), "tm", -16), swap(rpart, 1), near, sent)
     ry = jnp.where(
         core0, jnp.concatenate([rpart, ry2], 1), jnp.concatenate([ry2, rpart], 1)
     )
     rp, yp = ry[0], ry[1]
     s1 = step(rp, d16, S2) + xy0[0] + yp
     s1 = jnp.where(core0, s1[:, :256], s1[:, 256:])
-    u6 = steps(jnp.where(z >= 5, regrow(u6, 20, 32), zero), dz, S3, 6)
+    u6 = steps(jnp.where(z >= 5, regrow(thick(u6, 104), 20, 32), zero), dz, S3, 6)
     u3, u6 = hold(u3raw, u6)
-    u3 = jnp.where(z >= 2, u3, zero)
+    u3 = jnp.where(z >= 2, thick(u3, 104), zero)
     far = regrow(u3, 20, 32) + u6
     far = steps(far, dz, S2, 4)
     far1 = step(far, dz, S3)

time: 76 us -> 74.1 us (0.975)
  waiting for transfers between devices: 17.6 us -> 14.8 us
    ppermute x7, waiting for transfers between devices: 8.14 us -> 6.65 us  [swap(): return lax.ppermute(v, 'tm', [(i, i ^ bit) for i in range(n)])]
    ppermute x12, waiting for transfers between devices: 9.46 us -> 8.14 us  [shift(): return lax.ppermute(v, axis, [(i, (i + by) % n) for i in range(n)])]
  transfers between devices with their start and end apart: 19 -> 19, of which waited for: 13 -> 12; matrix products, arithmetic and copies ran while one was open for 12% -> 13% of each run, Pallas kernels for 0% -> 0%
where the time goes in v5:
time: 74.1 us; the launch traced here: 73.7 us
  starting transfers between devices  35 us (47%)
  other arithmetic  20.3 us (27%)
  waiting for transfers between devices  14.8 us (20%)
  local copies, waits for them, and re-layouts  2.25 us (3%)
  between operations  1.43 us (2%)
    ppermute x12, starting transfers between devices, shift(): return lax.ppermute(v, axis, [(i, (i + by) % n) for i in range(n)])  19.8 us
    ppermute x7, starting transfers between devices, swap(): return lax.ppermute(v, 'tm', [(i, i ^ bit) for i in range(n)])  15.1 us
    add x44, other arithmetic, step(): return v + s * d * lap  11.1 us
    ppermute x12, waiting for transfers between devices, shift(): return lax.ppermute(v, axis, [(i, (i + by) % n) for i in range(n)])  8.14 us
    ppermute x7, waiting for transfers between devices, swap(): return lax.ppermute(v, 'tm', [(i, i ^ bit) for i in range(n)])  6.65 us
  transfers between devices with their start and end apart: 19, of which 12 were waited for; matrix products, arithmetic and copies ran while one was open for 13% of the time, Pallas kernels for 0%

profile of v5, /device:TPU:1, one launch (start us, length us, event | category | flops | bytes accessed | tf_op | source)
XLA Modules:
  0.0 73.7 jit_solution(5415177070524811671)
XLA Ops:
  0.0 0.9 %fusion.402 = (f32[32,512]{1,0:T(8,128)S(1)}, f32[32,512]{1,0:T(8,128)S(1)}) fusion(f32[64,512]{1,0:T(8,128)} %param.5), kind=kLoop, calls=%fused_computation.801 | loop fusion | bytes 262144 | tf_op jit(solution)/shard_map/slice | solution.py:78
  0.9 3.6 %collective-permute-start.1 = (f32[32,512]{1,0:T(8,128)S(1)}, f32[32,512]{1,0:T(8,128)S(1)}, u32[]{:S(2)}, u32[]{:S(2)}) collective-permute-start(f32[32,512]{1,0:T(8,128)S(1)} %get-tuple-element.132), channel_id=1, source_target_pairs={{0,3},{1,0},{2,1},{3,2},{4,7},{5,4},{6,5},{7,6},{8,11},{9,8},{10,9... | collective-permute-start | bytes 196616 | tf_op jit(solution)/shard_map/ppermute | solution.py:26
  4.6 1.1 %select_maximum_fusion = f32[5,80,512]{2,1,0:T(8,128)S(1)} fusion(f32[4,64,512]{2,1,0:T(8,128)} %param.7, f32[1,64,512]{2,1,0:T(8,128)S(1)} %select_bitcast_fusion), kind=kLoop, calls=%fused_computation.55 | loop fusion | flops 1228800 | bytes 1474560 | tf_op jit(solution)/shard_map/concatenate | solution.py:80
  5.9 3.0 %collective-permute-done = f32[32,512]{1,0:T(8,128)S(1)} collective-permute-done((f32[32,512]{1,0:T(8,128)S(1)}, f32[32,512]{1,0:T(8,128)S(1)}, u32[]{:S(2)}, u32[]{:S(2)}) %collective-permute-start) | collective-permute-done | bytes 65568 | tf_op jit(solution)/shard_map/ppermute | solution.py:26
  9.0 0.5 fusion.5
  9.7 0.5 fusion.11
  10.4 0.5 fusion.17
  11.2 0.5 fusion.23
  11.7 0.4 copy-done.1
  12.7 0.3 fusion.397
  13.2 0.3 fusion.111
  13.5 0.3 fusion.117
  13.8 0.3 fusion.123
  14.1 0.3 fusion.129
  14.3 2.2 %collective-permute-start.2 = (f32[2,96,512]{2,1,0:T(8,128)S(1)}, f32[2,96,512]{2,1,0:T(8,128)S(1)}, u32[]{:S(2)}, u32[]{:S(2)}) collective-permute-start(f32[2,96,512]{2,1,0:T(8,128)S(1)} %fusion.129), channel_id=1, source_target_pairs={{0,4},{4,0},{8,12},{12,8},{16,20},{20,16},{24,28},{28,24},{32,36},... | collective-permute-start | bytes 1179656 | tf_op jit(solution)/shard_map/ppermute | solution.py:31
  16.6 0.3 fusion.39
  17.1 0.2 fusion.158
  17.4 0.3 fusion.45
  17.9 0.2 fusion.159
  19.0 1.3 %collective-permute-start.3 = (f32[2,144,128]{2,1,0:T(8,128)S(1)}, f32[2,144,128]{2,1,0:T(8,128)S(1)}, u32[]{:S(2)}, u32[]{:S(2)}) collective-permute-start(f32[2,144,128]{2,1,0:T(8,128)S(1)} %maximum_maximum_fusion.1), channel_id=1, source_target_pairs={{0,8},{4,12},{8,0},{12,4},{16,24},{20,28},{24,16},{28,20},{32,40},... | collective-permute-start | bytes 442376 | tf_op jit(solution)/shard_map/ppermute | solution.py:31
  20.3 0.3 collective-permute-start.6
  20.5 2.7 %collective-permute-start.7 = (f32[2,72,512]{2,1,0:T(8,128)S(1)}, f32[2,72,512]{2,1,0:T(8,128)S(1)}, u32[]{:S(2)}, u32[]{:S(2)}) collective-permute-start(f32[2,72,512]{2,1,0:T(8,128)S(1)} %pad_maximum_fusion.11), channel_id=1, source_target_pairs={{0,4},{4,8},{8,12},{12,16},{16,20},{20,24},{24,28},{28,32},{32,36}... | collective-permute-start | bytes 884744 | tf_op jit(solution)/shard_map/ppermute | solution.py:26
  23.2 0.3 fusion.51
  23.5 0.3 fusion.57
  24.6 1.9 %collective-permute-start.4 = (f32[2,144,128]{2,1,0:T(8,128)S(1)}, f32[2,144,128]{2,1,0:T(8,128)S(1)}, u32[]{:S(2)}, u32[]{:S(2)}) collective-permute-start(f32[2,144,128]{2,1,0:T(8,128)S(1)} %add.1277), channel_id=1, source_target_pairs={{0,32},{4,36},{8,40},{12,44},{16,48},{20,52},{24,56},{28,60},{32,6... | collective-permute-start | bytes 442376 | tf_op jit(solution)/shard_map/ppermute | solution.py:26
  26.5 4.0 %collective-permute-start.5 = (f32[144,128]{1,0:T(8,128)S(1)}, f32[144,128]{1,0:T(8,128)S(1)}, u32[]{:S(2)}, u32[]{:S(2)}) collective-permute-start(f32[144,128]{1,0:T(8,128)S(1)} %maximum_maximum_fusion.4), channel_id=1, source_target_pairs={{0,224},{4,228},{8,232},{12,236},{16,240},{20,244},{24,248},{28,25... | collective-permute-start | bytes 221192 | tf_op jit(solution)/shard_map/ppermute | solution.py:26
  30.5 1.5 %collective-permute-done.6 = f32[2,48,512]{2,1,0:T(8,128)S(1)} collective-permute-done((f32[2,48,512]{2,1,0:T(8,128)S(1)}, f32[2,48,512]{2,1,0:T(8,128)S(1)}, u32[]{:S(2)}, u32[]{:S(2)}) %collective-permute-start.6) | collective-permute-done | bytes 196640 | tf_op jit(solution)/shard_map/ppermute | solution.py:26
  32.0 1.3 %collective-permute-done.4 = f32[2,144,128]{2,1,0:T(8,128)S(1)} collective-permute-done((f32[2,144,128]{2,1,0:T(8,128)S(1)}, f32[2,144,128]{2,1,0:T(8,128)S(1)}, u32[]{:S(2)}, u32[]{:S(2)}) %collective-permute-start.4) | collective-permute-done | bytes 147488 | tf_op jit(solution)/shard_map/ppermute | solution.py:26
  34.5 3.5 %collective-permute-start.10 = (f32[160,128]{1,0:T(8,128)S(1)}, f32[160,128]{1,0:T(8,128)S(1)}, u32[]{:S(2)}, u32[]{:S(2)}) collective-permute-start(f32[160,128]{1,0:T(8,128)S(1)} %maximum_maximum_fusion.3), channel_id=1, source_target_pairs={{0,96},{4,100},{8,104},{12,108},{16,112},{20,116},{24,120},{28,124... | collective-permute-start | bytes 245768 | tf_op jit(solution)/shard_map/ppermute | solution.py:26
  38.0 0.6 collective-permute-start.8
  39.0 0.3 multiply_add_fusion.2
  39.2 0.3 multiply_add_fusion.1
  39.5 0.3 multiply_add_fusion
  39.8 2.1 %collective-permute-start.9 = (f32[2,48,512]{2,1,0:T(8,128)S(1)}, f32[2,48,512]{2,1,0:T(8,128)S(1)}, u32[]{:S(2)}, u32[]{:S(2)}) collective-permute-start(f32[2,48,512]{2,1,0:T(8,128)S(1)} %broadcast_select_fusion.5), channel_id=1, source_target_pairs={{0,4},{4,0},{8,12},{12,8},{16,20},{20,16},{24,28},{28,24},{32,36},... | collective-permute-start | bytes 589832 | tf_op jit(solution)/shard_map/ppermute | solution.py:31
  42.1 0.3 fusion.63
  42.4 0.3 fusion.69
  42.7 0.3 fusion.75
  43.0 0.3 fusion.81
  43.4 0.3 maximum_add_fusion
  44.8 0.2 fusion.263
  46.2 5.1 %collective-permute-start.11 = (f32[2,128,128]{2,1,0:T(8,128)S(1)}, f32[2,128,128]{2,1,0:T(8,128)S(1)}, u32[]{:S(2)}, u32[]{:S(2)}) collective-permute-start(f32[2,128,128]{2,1,0:T(8,128)S(1)} %slice_select_fusion.6), channel_id=1, source_target_pairs={{0,24},{4,28},{8,16},{12,20},{16,8},{20,12},{24,0},{28,4},{32,56},... | collective-permute-start | bytes 393224 | tf_op jit(solution)/shard_map/ppermute | solution.py:31
  51.4 0.2 broadcast_multiply_fusion
  51.7 0.3 fusion.87
  52.0 0.3 fusion.93
  52.3 0.3 fusion.99
  52.6 0.3 fusion.105
  53.0 0.2 fusion.198
  53.2 0.2 fusion.201
  53.4 0.2 fusion.194
  53.7 1.4 %collective-permute-done.12 = f32[96,256]{1,0:T(8,128)S(1)} collective-permute-done((f32[96,256]{1,0:T(8,128)S(1)}, f32[96,256]{1,0:T(8,128)S(1)}, u32[]{:S(2)}, u32[]{:S(2)}) %collective-permute-start.12) | collective-permute-done | bytes 98336 | tf_op jit(solution)/shard_map/ppermute | solution.py:31
  55.4 0.3 collective-permute-start.14
  55.7 1.5 %collective-permute-start.13 = (f32[24,768]{1,0:T(8,128)S(1)}, f32[24,768]{1,0:T(8,128)S(1)}, u32[]{:S(2)}, u32[]{:S(2)}) collective-permute-start(f32[24,768]{1,0:T(8,128)S(1)} %get-tuple-element.137), channel_id=1, source_target_pairs={{0,1},{1,2},{2,3},{3,0},{4,5},{5,6},{6,7},{7,4},{8,9},{9,10},{10,1... | collective-permute-start | bytes 221192 | tf_op jit(solution)/shard_map/ppermute | solution.py:26
  57.2 1.4 %collective-permute-start.17 = (f32[4,24,512]{2,1,0:T(8,128)S(1)}, f32[4,24,512]{2,1,0:T(8,128)S(1)}, u32[]{:S(2)}, u32[]{:S(2)}) collective-permute-start(f32[4,24,512]{2,1,0:T(8,128)S(1)} %get-tuple-element.85), channel_id=1, source_target_pairs={{0,3},{1,0},{2,1},{3,2},{4,7},{5,4},{6,5},{7,6},{8,11},{9,8},{10,9... | collective-permute-start | bytes 589832 | tf_op jit(solution)/shard_map/ppermute | solution.py:26
  58.9 1.3 %collective-permute-done.13 = f32[24,768]{1,0:T(8,128)S(1)} collective-permute-done((f32[24,768]{1,0:T(8,128)S(1)}, f32[24,768]{1,0:T(8,128)S(1)}, u32[]{:S(2)}, u32[]{:S(2)}) %collective-permute-start.13) | collective-permute-done | bytes 73760 | tf_op jit(solution)/shard_map/ppermute | solution.py:26
  60.5 3.7 %collective-permute-done.15 = f32[2,96,128]{2,1,0:T(8,128)S(1)} collective-permute-done((f32[2,96,128]{2,1,0:T(8,128)S(1)}, f32[2,96,128]{2,1,0:T(8,128)S(1)}, u32[]{:S(2)}, u32[]{:S(2)}) %collective-permute-start.15) | collective-permute-done | bytes 98336 | tf_op jit(solution)/shard_map/ppermute | solution.py:31
  64.2 0.8 %collective-permute-done.16 = f32[4,24,512]{2,1,0:T(8,128)S(1)} collective-permute-done((f32[4,24,512]{2,1,0:T(8,128)S(1)}, f32[4,24,512]{2,1,0:T(8,128)S(1)}, u32[]{:S(2)}, u32[]{:S(2)}) %collective-permute-start.16) | collective-permute-done | bytes 196640 | tf_op jit(solution)/shard_map/ppermute | solution.py:26
  65.0 4.2 %collective-permute-start.18 = (f32[3,96,256]{2,1,0:T(8,128)S(1)}, f32[3,96,256]{2,1,0:T(8,128)S(1)}, u32[]{:S(2)}, u32[]{:S(2)}) collective-permute-start(f32[3,96,256]{2,1,0:T(8,128)S(1)} %pad_maximum_fusion.13), channel_id=1, source_target_pairs={{0,4},{4,0},{8,12},{12,8},{16,20},{20,16},{24,28},{28,24},{32,36},... | collective-permute-start | bytes 884744 | tf_op jit(solution)/shard_map/ppermute | solution.py:31
  69.3 1.2 %collective-permute-done.18 = f32[3,96,256]{2,1,0:T(8,128)S(1)} collective-permute-done((f32[3,96,256]{2,1,0:T(8,128)S(1)}, f32[3,96,256]{2,1,0:T(8,128)S(1)}, u32[]{:S(2)}, u32[]{:S(2)}) %collective-permute-start.18) | collective-permute-done | bytes 294944 | tf_op jit(solution)/shard_map/ppermute | solution.py:31
  71.0 0.2 fusion.139
  71.3 0.2 fusion.145
  71.5 0.2 fusion.151
  71.8 0.2 fusion.157
  72.2 0.2 multiply_add_fusion.3
  72.8 0.9 %fusion.33 = f32[4,64,512]{2,1,0:T(8,128)} fusion(f32[1,80,512]{2,1,0:T(8,128)S(1)} %get-tuple-element.100, f32[1,80,512]{2,1,0:T(8,128)S(1)} %fusion.285, f32[1,80,512]{2,1,0:T(8,128)S(1)} %bitcast.225, f32[1,80,512]{2,1,0:T(8,128)S(1)} %bitcast.224, f32[4,24,512]{2,1,0:T(8,128)S(1)} %broadcast_select_fusion.3, ...), kind=kLoop, calls=%fused_computation.151 | loop fusion | flops 786432 | bytes 2097152 | tf_op jit(solution)/shard_map/add | solution.py:265
  (164 shorter events, 9.2 us)
Async XLA Ops:
  0.0 8.9 %copy-start.2 = (f32[64,512]{1,0:T(8,128)S(1)}, f32[64,512]{1,0:T(8,128)}, u32[]{:S(2)}) copy-start(f32[64,512]{1,0:T(8,128)} %param.5) | copy-start | bytes 393220
  0.9 5.0 %collective-permute-start.1 = (f32[32,512]{1,0:T(8,128)S(1)}, f32[32,512]{1,0:T(8,128)S(1)}, u32[]{:S(2)}, u32[]{:S(2)}) collective-permute-start(f32[32,512]{1,0:T(8,128)S(1)} %get-tuple-element.132), channel_id=1, source_target_pairs={{0,3},{1,0},{2,1},{3,2},{4,7},{5,4},{6,5},{7,6},{8,11},{9,8},{10,9... | collective-permute-start | bytes 196616 | tf_op jit(solution)/shard_map/ppermute | solution.py:26
  4.6 4.3 %collective-permute-start = (f32[32,512]{1,0:T(8,128)S(1)}, f32[32,512]{1,0:T(8,128)S(1)}, u32[]{:S(2)}, u32[]{:S(2)}) collective-permute-start(f32[32,512]{1,0:T(8,128)S(1)} %get-tuple-element.133), channel_id=1, source_target_pairs={{0,1},{1,2},{2,3},{3,0},{4,5},{5,6},{6,7},{7,4},{8,9},{9,10},{10,1... | collective-permute-start | bytes 196616 | tf_op jit(solution)/shard_map/ppermute | solution.py:26
  5.7 3.8 %copy-start = (f32[16,64,512]{2,1,0:T(8,128)S(1)}, f32[16,64,512]{2,1,0:T(8,128)}, u32[]{:S(2)}) copy-start(f32[16,64,512]{2,1,0:T(8,128)} %param.6) | copy-start | bytes 6291460
  11.1 1.0 %copy-start.1 = (f32[4,64,512]{2,1,0:T(8,128)S(1)}, f32[4,64,512]{2,1,0:T(8,128)}, u32[]{:S(2)}) copy-start(f32[4,64,512]{2,1,0:T(8,128)} %param.7) | copy-start | bytes 1572868
  14.3 3.5 %collective-permute-start.2 = (f32[2,96,512]{2,1,0:T(8,128)S(1)}, f32[2,96,512]{2,1,0:T(8,128)S(1)}, u32[]{:S(2)}, u32[]{:S(2)}) collective-permute-start(f32[2,96,512]{2,1,0:T(8,128)S(1)} %fusion.129), channel_id=1, source_target_pairs={{0,4},{4,0},{8,12},{12,8},{16,20},{20,16},{24,28},{28,24},{32,36},... | collective-permute-start | bytes 1179656 | tf_op jit(solution)/shard_map/ppermute | solution.py:31
  19.0 5.1 %collective-permute-start.3 = (f32[2,144,128]{2,1,0:T(8,128)S(1)}, f32[2,144,128]{2,1,0:T(8,128)S(1)}, u32[]{:S(2)}, u32[]{:S(2)}) collective-permute-start(f32[2,144,128]{2,1,0:T(8,128)S(1)} %maximum_maximum_fusion.1), channel_id=1, source_target_pairs={{0,8},{4,12},{8,0},{12,4},{16,24},{20,28},{24,16},{28,20},{32,40},... | collective-permute-start | bytes 442376 | tf_op jit(solution)/shard_map/ppermute | solution.py:31
  20.3 11.8 %collective-permute-start.6 = (f32[2,48,512]{2,1,0:T(8,128)S(1)}, f32[2,48,512]{2,1,0:T(8,128)S(1)}, u32[]{:S(2)}, u32[]{:S(2)}) collective-permute-start(f32[2,48,512]{2,1,0:T(8,128)S(1)} %fusion.258), channel_id=1, source_target_pairs={{0,8},{4,12},{8,16},{12,20},{16,24},{20,28},{24,32},{28,36},{32,40... | collective-permute-start | bytes 589832 | tf_op jit(solution)/shard_map/ppermute | solution.py:26
  20.5 11.5 %collective-permute-start.7 = (f32[2,72,512]{2,1,0:T(8,128)S(1)}, f32[2,72,512]{2,1,0:T(8,128)S(1)}, u32[]{:S(2)}, u32[]{:S(2)}) collective-permute-start(f32[2,72,512]{2,1,0:T(8,128)S(1)} %pad_maximum_fusion.11), channel_id=1, source_target_pairs={{0,4},{4,8},{8,12},{12,16},{16,20},{20,24},{24,28},{28,32},{32,36}... | collective-permute-start | bytes 884744 | tf_op jit(solution)/shard_map/ppermute | solution.py:26
  24.6 8.8 %collective-permute-start.4 = (f32[2,144,128]{2,1,0:T(8,128)S(1)}, f32[2,144,128]{2,1,0:T(8,128)S(1)}, u32[]{:S(2)}, u32[]{:S(2)}) collective-permute-start(f32[2,144,128]{2,1,0:T(8,128)S(1)} %add.1277), channel_id=1, source_target_pairs={{0,32},{4,36},{8,40},{12,44},{16,48},{20,52},{24,56},{28,60},{32,6... | collective-permute-start | bytes 442376 | tf_op jit(solution)/shard_map/ppermute | solution.py:26
  26.5 5.5 %collective-permute-start.5 = (f32[144,128]{1,0:T(8,128)S(1)}, f32[144,128]{1,0:T(8,128)S(1)}, u32[]{:S(2)}, u32[]{:S(2)}) collective-permute-start(f32[144,128]{1,0:T(8,128)S(1)} %maximum_maximum_fusion.4), channel_id=1, source_target_pairs={{0,224},{4,228},{8,232},{12,236},{16,240},{20,244},{24,248},{28,25... | collective-permute-start | bytes 221192 | tf_op jit(solution)/shard_map/ppermute | solution.py:26
  34.5 10.2 %collective-permute-start.10 = (f32[160,128]{1,0:T(8,128)S(1)}, f32[160,128]{1,0:T(8,128)S(1)}, u32[]{:S(2)}, u32[]{:S(2)}) collective-permute-start(f32[160,128]{1,0:T(8,128)S(1)} %maximum_maximum_fusion.3), channel_id=1, source_target_pairs={{0,96},{4,100},{8,104},{12,108},{16,112},{20,116},{24,120},{28,124... | collective-permute-start | bytes 245768 | tf_op jit(solution)/shard_map/ppermute | solution.py:26
  38.0 5.7 %collective-permute-start.8 = (f32[160,128]{1,0:T(8,128)S(1)}, f32[160,128]{1,0:T(8,128)S(1)}, u32[]{:S(2)}, u32[]{:S(2)}) collective-permute-start(f32[160,128]{1,0:T(8,128)S(1)} %maximum_maximum_fusion.3), channel_id=1, source_target_pairs={{0,192},{4,196},{8,200},{12,204},{16,208},{20,212},{24,216},{28,22... | collective-permute-start | bytes 245768 | tf_op jit(solution)/shard_map/ppermute | solution.py:26
  39.8 3.8 %collective-permute-start.9 = (f32[2,48,512]{2,1,0:T(8,128)S(1)}, f32[2,48,512]{2,1,0:T(8,128)S(1)}, u32[]{:S(2)}, u32[]{:S(2)}) collective-permute-start(f32[2,48,512]{2,1,0:T(8,128)S(1)} %broadcast_select_fusion.5), channel_id=1, source_target_pairs={{0,4},{4,0},{8,12},{12,8},{16,20},{20,16},{24,28},{28,24},{32,36},... | collective-permute-start | bytes 589832 | tf_op jit(solution)/shard_map/ppermute | solution.py:31
  46.2 9.0 %collective-permute-start.11 = (f32[2,128,128]{2,1,0:T(8,128)S(1)}, f32[2,128,128]{2,1,0:T(8,128)S(1)}, u32[]{:S(2)}, u32[]{:S(2)}) collective-permute-start(f32[2,128,128]{2,1,0:T(8,128)S(1)} %slice_select_fusion.6), channel_id=1, source_target_pairs={{0,24},{4,28},{8,16},{12,20},{16,8},{20,12},{24,0},{28,4},{32,56},... | collective-permute-start | bytes 393224 | tf_op jit(solution)/shard_map/ppermute | solution.py:31
  51.3 3.8 %collective-permute-start.12 = (f32[96,256]{1,0:T(8,128)S(1)}, f32[96,256]{1,0:T(8,128)S(1)}, u32[]{:S(2)}, u32[]{:S(2)}) collective-permute-start(f32[96,256]{1,0:T(8,128)S(1)} %slice_select_fusion.7), channel_id=1, source_target_pairs={{0,8},{4,12},{8,0},{12,4},{16,24},{20,28},{24,16},{28,20},{32,40},... | collective-permute-start | bytes 294920 | tf_op jit(solution)/shard_map/ppermute | solution.py:31
  55.4 3.5 %collective-permute-start.14 = (f32[24,768]{1,0:T(8,128)S(1)}, f32[24,768]{1,0:T(8,128)S(1)}, u32[]{:S(2)}, u32[]{:S(2)}) collective-permute-start(f32[24,768]{1,0:T(8,128)S(1)} %get-tuple-element.136), channel_id=1, source_target_pairs={{0,3},{1,0},{2,1},{3,2},{4,7},{5,4},{6,5},{7,6},{8,11},{9,8},{10,9... | collective-permute-start | bytes 221192 | tf_op jit(solution)/shard_map/ppermute | solution.py:26
  55.7 4.5 %collective-permute-start.13 = (f32[24,768]{1,0:T(8,128)S(1)}, f32[24,768]{1,0:T(8,128)S(1)}, u32[]{:S(2)}, u32[]{:S(2)}) collective-permute-start(f32[24,768]{1,0:T(8,128)S(1)} %get-tuple-element.137), channel_id=1, source_target_pairs={{0,1},{1,2},{2,3},{3,0},{4,5},{5,6},{6,7},{7,4},{8,9},{9,10},{10,1... | collective-permute-start | bytes 221192 | tf_op jit(solution)/shard_map/ppermute | solution.py:26
  57.2 7.0 %collective-permute-start.17 = (f32[4,24,512]{2,1,0:T(8,128)S(1)}, f32[4,24,512]{2,1,0:T(8,128)S(1)}, u32[]{:S(2)}, u32[]{:S(2)}) collective-permute-start(f32[4,24,512]{2,1,0:T(8,128)S(1)} %get-tuple-element.85), channel_id=1, source_target_pairs={{0,3},{1,0},{2,1},{3,2},{4,7},{5,4},{6,5},{7,6},{8,11},{9,8},{10,9... | collective-permute-start | bytes 589832 | tf_op jit(solution)/shard_map/ppermute | solution.py:26
  58.6 6.4 %collective-permute-start.16 = (f32[4,24,512]{2,1,0:T(8,128)S(1)}, f32[4,24,512]{2,1,0:T(8,128)S(1)}, u32[]{:S(2)}, u32[]{:S(2)}) collective-permute-start(f32[4,24,512]{2,1,0:T(8,128)S(1)} %get-tuple-element.86), channel_id=1, source_target_pairs={{0,1},{1,2},{2,3},{3,0},{4,5},{5,6},{6,7},{7,4},{8,9},{9,10},{10,1... | collective-permute-start | bytes 589832 | tf_op jit(solution)/shard_map/ppermute | solution.py:26
  60.4 3.8 %collective-permute-start.15 = (f32[2,96,128]{2,1,0:T(8,128)S(1)}, f32[2,96,128]{2,1,0:T(8,128)S(1)}, u32[]{:S(2)}, u32[]{:S(2)}) collective-permute-start(f32[2,96,128]{2,1,0:T(8,128)S(1)} %slice_add_fusion.3), channel_id=1, source_target_pairs={{0,8},{4,12},{8,0},{12,4},{16,24},{20,28},{24,16},{28,20},{32,40},... | collective-permute-start | bytes 294920 | tf_op jit(solution)/shard_map/ppermute | solution.py:31
  65.0 5.4 %collective-permute-start.18 = (f32[3,96,256]{2,1,0:T(8,128)S(1)}, f32[3,96,256]{2,1,0:T(8,128)S(1)}, u32[]{:S(2)}, u32[]{:S(2)}) collective-permute-start(f32[3,96,256]{2,1,0:T(8,128)S(1)} %pad_maximum_fusion.13), channel_id=1, source_target_pairs={{0,4},{4,0},{8,12},{12,8},{16,20},{20,16},{24,28},{28,24},{32,36},... | collective-permute-start | bytes 884744 | tf_op jit(solution)/shard_map/ppermute | solution.py:31

commit v6 on v5

--- a/solution.py
+++ b/solution.py
@@ -101,7 +101,7 @@
     xy = steps(jnp.stack([xf, yf]), d16, S0, 4)
     xy, dheld = hold(xy, dwide)
     d24 = dext(24)
-    own = steps(regrow(d[:2], 8, 24), d24, S0, 2)
+    own = steps(regrow(d[:2], 8, 24), d24, S0, 3)
     theirs, own = hold(swap(xy, 1), own)
 
     dpad = edged(dheld)
@@ -136,7 +136,7 @@
     def r24(v):
         return regrow(v, 16, 24)
 
-    own = steps(own, d24, S0, 2)
+    own = step(own, d24, S0)
     other, own, packed_keep = hold(swap(thin(give), 2), own, thin(keep))
     packed_keep = packed_keep + other
     keep = thick(packed_keep, 96)

time: 74.1 us -> 74.8 us (level)
  transfers between devices with their start and end apart: 19 -> 19, of which waited for: 12 -> 12; matrix products, arithmetic and copies ran while one was open for 13% -> 12% of each run, Pallas kernels for 0% -> 0%
where the time goes in v6:
time: 74.8 us; the launch traced here: 74.4 us
  starting transfers between devices  35 us (47%)
  other arithmetic  20.3 us (27%)
  waiting for transfers between devices  15.5 us (21%)
  local copies, waits for them, and re-layouts  2.26 us (3%)
  between operations  1.43 us (2%)
    ppermute x12, starting transfers between devices, shift(): return lax.ppermute(v, axis, [(i, (i + by) % n) for i in range(n)])  19.8 us
    ppermute x7, starting transfers between devices, swap(): return lax.ppermute(v, 'tm', [(i, i ^ bit) for i in range(n)])  15.1 us
    add x44, other arithmetic, step(): return v + s * d * lap  11.1 us
    ppermute x12, waiting for transfers between devices, shift(): return lax.ppermute(v, axis, [(i, (i + by) % n) for i in range(n)])  8.14 us
    ppermute x7, waiting for transfers between devices, swap(): return lax.ppermute(v, 'tm', [(i, i ^ bit) for i in range(n)])  7.33 us
  transfers between devices with their start and end apart: 19, of which 12 were waited for; matrix products, arithmetic and copies ran while one was open for 12% of the time, Pallas kernels for 0%

profile of v6, /device:TPU:1, one launch (start us, length us, event | category | flops | bytes accessed | tf_op | source)
XLA Modules:
  0.0 74.4 jit_solution(13114845144939214571)
XLA Ops:
  0.0 0.9 %fusion.402 = (f32[32,512]{1,0:T(8,128)S(1)}, f32[32,512]{1,0:T(8,128)S(1)}) fusion(f32[64,512]{1,0:T(8,128)} %param.5), kind=kLoop, calls=%fused_computation.801 | loop fusion | bytes 262144 | tf_op jit(solution)/shard_map/slice | solution.py:78
  0.9 3.6 %collective-permute-start.1 = (f32[32,512]{1,0:T(8,128)S(1)}, f32[32,512]{1,0:T(8,128)S(1)}, u32[]{:S(2)}, u32[]{:S(2)}) collective-permute-start(f32[32,512]{1,0:T(8,128)S(1)} %get-tuple-element.132), channel_id=1, source_target_pairs={{0,3},{1,0},{2,1},{3,2},{4,7},{5,4},{6,5},{7,6},{8,11},{9,8},{10,9... | collective-permute-start | bytes 196616 | tf_op jit(solution)/shard_map/ppermute | solution.py:26
  4.6 1.1 %select_maximum_fusion = f32[5,80,512]{2,1,0:T(8,128)S(1)} fusion(f32[4,64,512]{2,1,0:T(8,128)} %param.7, f32[1,64,512]{2,1,0:T(8,128)S(1)} %select_bitcast_fusion), kind=kLoop, calls=%fused_computation.55 | loop fusion | flops 1228800 | bytes 1474560 | tf_op jit(solution)/shard_map/concatenate | solution.py:80
  5.9 3.0 %collective-permute-done = f32[32,512]{1,0:T(8,128)S(1)} collective-permute-done((f32[32,512]{1,0:T(8,128)S(1)}, f32[32,512]{1,0:T(8,128)S(1)}, u32[]{:S(2)}, u32[]{:S(2)}) %collective-permute-start) | collective-permute-done | bytes 65568 | tf_op jit(solution)/shard_map/ppermute | solution.py:26
  9.0 0.5 fusion.5
  9.7 0.5 fusion.11
  10.4 0.5 fusion.17
  11.2 0.5 fusion.23
  11.7 0.4 copy-done.1
  12.4 0.3 fusion.39
  12.7 0.3 fusion.45
  13.4 0.3 fusion.397
  13.9 0.3 fusion.111
  14.2 0.3 fusion.117
  14.5 0.3 fusion.123
  14.8 0.3 fusion.129
  15.0 2.2 %collective-permute-start.2 = (f32[2,96,512]{2,1,0:T(8,128)S(1)}, f32[2,96,512]{2,1,0:T(8,128)S(1)}, u32[]{:S(2)}, u32[]{:S(2)}) collective-permute-start(f32[2,96,512]{2,1,0:T(8,128)S(1)} %fusion.129), channel_id=1, source_target_pairs={{0,4},{4,0},{8,12},{12,8},{16,20},{20,16},{24,28},{28,24},{32,36},... | collective-permute-start | bytes 1179656 | tf_op jit(solution)/shard_map/ppermute | solution.py:31
  17.4 0.2 fusion.158
  17.7 0.3 fusion.51
  18.0 0.5 collective-permute-done.2
  18.6 0.2 fusion.159
  19.7 1.3 %collective-permute-start.3 = (f32[2,144,128]{2,1,0:T(8,128)S(1)}, f32[2,144,128]{2,1,0:T(8,128)S(1)}, u32[]{:S(2)}, u32[]{:S(2)}) collective-permute-start(f32[2,144,128]{2,1,0:T(8,128)S(1)} %maximum_maximum_fusion.1), channel_id=1, source_target_pairs={{0,8},{4,12},{8,0},{12,4},{16,24},{20,28},{24,16},{28,20},{32,40},... | collective-permute-start | bytes 442376 | tf_op jit(solution)/shard_map/ppermute | solution.py:31
  21.0 0.3 collective-permute-start.6
  21.2 2.7 %collective-permute-start.7 = (f32[2,72,512]{2,1,0:T(8,128)S(1)}, f32[2,72,512]{2,1,0:T(8,128)S(1)}, u32[]{:S(2)}, u32[]{:S(2)}) collective-permute-start(f32[2,72,512]{2,1,0:T(8,128)S(1)} %pad_maximum_fusion.11), channel_id=1, source_target_pairs={{0,4},{4,8},{8,12},{12,16},{16,20},{20,24},{24,28},{28,32},{32,36}... | collective-permute-start | bytes 884744 | tf_op jit(solution)/shard_map/ppermute | solution.py:26
  23.9 0.3 fusion.57
  24.4 0.5 collective-permute-done.3
  25.3 1.9 %collective-permute-start.4 = (f32[2,144,128]{2,1,0:T(8,128)S(1)}, f32[2,144,128]{2,1,0:T(8,128)S(1)}, u32[]{:S(2)}, u32[]{:S(2)}) collective-permute-start(f32[2,144,128]{2,1,0:T(8,128)S(1)} %add.1277), channel_id=1, source_target_pairs={{0,32},{4,36},{8,40},{12,44},{16,48},{20,52},{24,56},{28,60},{32,6... | collective-permute-start | bytes 442376 | tf_op jit(solution)/shard_map/ppermute | solution.py:26
  27.2 4.0 %collective-permute-start.5 = (f32[144,128]{1,0:T(8,128)S(1)}, f32[144,128]{1,0:T(8,128)S(1)}, u32[]{:S(2)}, u32[]{:S(2)}) collective-permute-start(f32[144,128]{1,0:T(8,128)S(1)} %maximum_maximum_fusion.4), channel_id=1, source_target_pairs={{0,224},{4,228},{8,232},{12,236},{16,240},{20,244},{24,248},{28,25... | collective-permute-start | bytes 221192 | tf_op jit(solution)/shard_map/ppermute | solution.py:26
  31.2 1.5 %collective-permute-done.6 = f32[2,48,512]{2,1,0:T(8,128)S(1)} collective-permute-done((f32[2,48,512]{2,1,0:T(8,128)S(1)}, f32[2,48,512]{2,1,0:T(8,128)S(1)}, u32[]{:S(2)}, u32[]{:S(2)}) %collective-permute-start.6) | collective-permute-done | bytes 196640 | tf_op jit(solution)/shard_map/ppermute | solution.py:26
  32.7 1.3 %collective-permute-done.4 = f32[2,144,128]{2,1,0:T(8,128)S(1)} collective-permute-done((f32[2,144,128]{2,1,0:T(8,128)S(1)}, f32[2,144,128]{2,1,0:T(8,128)S(1)}, u32[]{:S(2)}, u32[]{:S(2)}) %collective-permute-start.4) | collective-permute-done | bytes 147488 | tf_op jit(solution)/shard_map/ppermute | solution.py:26
  35.2 3.5 %collective-permute-start.10 = (f32[160,128]{1,0:T(8,128)S(1)}, f32[160,128]{1,0:T(8,128)S(1)}, u32[]{:S(2)}, u32[]{:S(2)}) collective-permute-start(f32[160,128]{1,0:T(8,128)S(1)} %maximum_maximum_fusion.3), channel_id=1, source_target_pairs={{0,96},{4,100},{8,104},{12,108},{16,112},{20,116},{24,120},{28,124... | collective-permute-start | bytes 245768 | tf_op jit(solution)/shard_map/ppermute | solution.py:26
  38.7 0.6 collective-permute-start.8
  39.7 0.3 multiply_add_fusion.2
  39.9 0.3 multiply_add_fusion.1
  40.2 0.3 multiply_add_fusion
  40.5 2.1 %collective-permute-start.9 = (f32[2,48,512]{2,1,0:T(8,128)S(1)}, f32[2,48,512]{2,1,0:T(8,128)S(1)}, u32[]{:S(2)}, u32[]{:S(2)}) collective-permute-start(f32[2,48,512]{2,1,0:T(8,128)S(1)} %broadcast_select_fusion.5), channel_id=1, source_target_pairs={{0,4},{4,0},{8,12},{12,8},{16,20},{20,16},{24,28},{28,24},{32,36},... | collective-permute-start | bytes 589832 | tf_op jit(solution)/shard_map/ppermute | solution.py:31
  42.8 0.3 fusion.63
  43.1 0.3 fusion.69
  43.4 0.3 fusion.75
  43.7 0.3 fusion.81
  44.0 0.3 maximum_add_fusion
  46.9 5.1 %collective-permute-start.11 = (f32[2,128,128]{2,1,0:T(8,128)S(1)}, f32[2,128,128]{2,1,0:T(8,128)S(1)}, u32[]{:S(2)}, u32[]{:S(2)}) collective-permute-start(f32[2,128,128]{2,1,0:T(8,128)S(1)} %slice_select_fusion.6), channel_id=1, source_target_pairs={{0,24},{4,28},{8,16},{12,20},{16,8},{20,12},{24,0},{28,4},{32,56},... | collective-permute-start | bytes 393224 | tf_op jit(solution)/shard_map/ppermute | solution.py:31
  52.1 0.2 broadcast_multiply_fusion
  52.4 0.3 fusion.87
  52.7 0.3 fusion.93
  53.0 0.3 fusion.99
  53.3 0.3 fusion.105
  53.9 0.2 fusion.201
  54.1 0.2 fusion.194
  54.4 1.4 %collective-permute-done.12 = f32[96,256]{1,0:T(8,128)S(1)} collective-permute-done((f32[96,256]{1,0:T(8,128)S(1)}, f32[96,256]{1,0:T(8,128)S(1)}, u32[]{:S(2)}, u32[]{:S(2)}) %collective-permute-start.12) | collective-permute-done | bytes 98336 | tf_op jit(solution)/shard_map/ppermute | solution.py:31
  56.1 0.3 collective-permute-start.14
  56.4 1.5 %collective-permute-start.13 = (f32[24,768]{1,0:T(8,128)S(1)}, f32[24,768]{1,0:T(8,128)S(1)}, u32[]{:S(2)}, u32[]{:S(2)}) collective-permute-start(f32[24,768]{1,0:T(8,128)S(1)} %get-tuple-element.137), channel_id=1, source_target_pairs={{0,1},{1,2},{2,3},{3,0},{4,5},{5,6},{6,7},{7,4},{8,9},{9,10},{10,1... | collective-permute-start | bytes 221192 | tf_op jit(solution)/shard_map/ppermute | solution.py:26
  57.9 1.4 %collective-permute-start.17 = (f32[4,24,512]{2,1,0:T(8,128)S(1)}, f32[4,24,512]{2,1,0:T(8,128)S(1)}, u32[]{:S(2)}, u32[]{:S(2)}) collective-permute-start(f32[4,24,512]{2,1,0:T(8,128)S(1)} %get-tuple-element.85), channel_id=1, source_target_pairs={{0,3},{1,0},{2,1},{3,2},{4,7},{5,4},{6,5},{7,6},{8,11},{9,8},{10,9... | collective-permute-start | bytes 589832 | tf_op jit(solution)/shard_map/ppermute | solution.py:26
  59.6 1.3 %collective-permute-done.13 = f32[24,768]{1,0:T(8,128)S(1)} collective-permute-done((f32[24,768]{1,0:T(8,128)S(1)}, f32[24,768]{1,0:T(8,128)S(1)}, u32[]{:S(2)}, u32[]{:S(2)}) %collective-permute-start.13) | collective-permute-done | bytes 73760 | tf_op jit(solution)/shard_map/ppermute | solution.py:26
  61.2 3.7 %collective-permute-done.15 = f32[2,96,128]{2,1,0:T(8,128)S(1)} collective-permute-done((f32[2,96,128]{2,1,0:T(8,128)S(1)}, f32[2,96,128]{2,1,0:T(8,128)S(1)}, u32[]{:S(2)}, u32[]{:S(2)}) %collective-permute-start.15) | collective-permute-done | bytes 98336 | tf_op jit(solution)/shard_map/ppermute | solution.py:31
  64.9 0.8 %collective-permute-done.16 = f32[4,24,512]{2,1,0:T(8,128)S(1)} collective-permute-done((f32[4,24,512]{2,1,0:T(8,128)S(1)}, f32[4,24,512]{2,1,0:T(8,128)S(1)}, u32[]{:S(2)}, u32[]{:S(2)}) %collective-permute-start.16) | collective-permute-done | bytes 196640 | tf_op jit(solution)/shard_map/ppermute | solution.py:26
  65.7 4.2 %collective-permute-start.18 = (f32[3,96,256]{2,1,0:T(8,128)S(1)}, f32[3,96,256]{2,1,0:T(8,128)S(1)}, u32[]{:S(2)}, u32[]{:S(2)}) collective-permute-start(f32[3,96,256]{2,1,0:T(8,128)S(1)} %pad_maximum_fusion.13), channel_id=1, source_target_pairs={{0,4},{4,0},{8,12},{12,8},{16,20},{20,16},{24,28},{28,24},{32,36},... | collective-permute-start | bytes 884744 | tf_op jit(solution)/shard_map/ppermute | solution.py:31
  70.0 1.2 %collective-permute-done.18 = f32[3,96,256]{2,1,0:T(8,128)S(1)} collective-permute-done((f32[3,96,256]{2,1,0:T(8,128)S(1)}, f32[3,96,256]{2,1,0:T(8,128)S(1)}, u32[]{:S(2)}, u32[]{:S(2)}) %collective-permute-start.18) | collective-permute-done | bytes 294944 | tf_op jit(solution)/shard_map/ppermute | solution.py:31
  71.7 0.2 fusion.139
  72.0 0.2 fusion.145
  72.2 0.2 fusion.151
  72.5 0.2 fusion.157
  72.9 0.2 multiply_add_fusion.3
  73.5 0.9 %fusion.33 = f32[4,64,512]{2,1,0:T(8,128)} fusion(f32[1,80,512]{2,1,0:T(8,128)S(1)} %get-tuple-element.100, f32[1,80,512]{2,1,0:T(8,128)S(1)} %fusion.285, f32[1,80,512]{2,1,0:T(8,128)S(1)} %bitcast.225, f32[1,80,512]{2,1,0:T(8,128)S(1)} %bitcast.224, f32[4,24,512]{2,1,0:T(8,128)S(1)} %broadcast_select_fusion.3, ...), kind=kLoop, calls=%fused_computation.151 | loop fusion | flops 786432 | bytes 2097152 | tf_op jit(solution)/shard_map/add | solution.py:265
  (164 shorter events, 9.3 us)
Async XLA Ops:
  0.0 8.9 %copy-start.2 = (f32[64,512]{1,0:T(8,128)S(1)}, f32[64,512]{1,0:T(8,128)}, u32[]{:S(2)}) copy-start(f32[64,512]{1,0:T(8,128)} %param.5) | copy-start | bytes 393220
  0.9 5.0 %collective-permute-start.1 = (f32[32,512]{1,0:T(8,128)S(1)}, f32[32,512]{1,0:T(8,128)S(1)}, u32[]{:S(2)}, u32[]{:S(2)}) collective-permute-start(f32[32,512]{1,0:T(8,128)S(1)} %get-tuple-element.132), channel_id=1, source_target_pairs={{0,3},{1,0},{2,1},{3,2},{4,7},{5,4},{6,5},{7,6},{8,11},{9,8},{10,9... | collective-permute-start | bytes 196616 | tf_op jit(solution)/shard_map/ppermute | solution.py:26
  4.6 4.3 %collective-permute-start = (f32[32,512]{1,0:T(8,128)S(1)}, f32[32,512]{1,0:T(8,128)S(1)}, u32[]{:S(2)}, u32[]{:S(2)}) collective-permute-start(f32[32,512]{1,0:T(8,128)S(1)} %get-tuple-element.133), channel_id=1, source_target_pairs={{0,1},{1,2},{2,3},{3,0},{4,5},{5,6},{6,7},{7,4},{8,9},{9,10},{10,1... | collective-permute-start | bytes 196616 | tf_op jit(solution)/shard_map/ppermute | solution.py:26
  5.7 3.8 %copy-start = (f32[16,64,512]{2,1,0:T(8,128)S(1)}, f32[16,64,512]{2,1,0:T(8,128)}, u32[]{:S(2)}) copy-start(f32[16,64,512]{2,1,0:T(8,128)} %param.6) | copy-start | bytes 6291460
  11.1 1.0 %copy-start.1 = (f32[4,64,512]{2,1,0:T(8,128)S(1)}, f32[4,64,512]{2,1,0:T(8,128)}, u32[]{:S(2)}) copy-start(f32[4,64,512]{2,1,0:T(8,128)} %param.7) | copy-start | bytes 1572868
  15.0 3.5 %collective-permute-start.2 = (f32[2,96,512]{2,1,0:T(8,128)S(1)}, f32[2,96,512]{2,1,0:T(8,128)S(1)}, u32[]{:S(2)}, u32[]{:S(2)}) collective-permute-start(f32[2,96,512]{2,1,0:T(8,128)S(1)} %fusion.129), channel_id=1, source_target_pairs={{0,4},{4,0},{8,12},{12,8},{16,20},{20,16},{24,28},{28,24},{32,36},... | collective-permute-start | bytes 1179656 | tf_op jit(solution)/shard_map/ppermute | solution.py:31
  19.7 5.1 %collective-permute-start.3 = (f32[2,144,128]{2,1,0:T(8,128)S(1)}, f32[2,144,128]{2,1,0:T(8,128)S(1)}, u32[]{:S(2)}, u32[]{:S(2)}) collective-permute-start(f32[2,144,128]{2,1,0:T(8,128)S(1)} %maximum_maximum_fusion.1), channel_id=1, source_target_pairs={{0,8},{4,12},{8,0},{12,4},{16,24},{20,28},{24,16},{28,20},{32,40},... | collective-permute-start | bytes 442376 | tf_op jit(solution)/shard_map/ppermute | solution.py:31
  21.0 11.8 %collective-permute-start.6 = (f32[2,48,512]{2,1,0:T(8,128)S(1)}, f32[2,48,512]{2,1,0:T(8,128)S(1)}, u32[]{:S(2)}, u32[]{:S(2)}) collective-permute-start(f32[2,48,512]{2,1,0:T(8,128)S(1)} %fusion.258), channel_id=1, source_target_pairs={{0,8},{4,12},{8,16},{12,20},{16,24},{20,28},{24,32},{28,36},{32,40... | collective-permute-start | bytes 589832 | tf_op jit(solution)/shard_map/ppermute | solution.py:26
  21.2 11.5 %collective-permute-start.7 = (f32[2,72,512]{2,1,0:T(8,128)S(1)}, f32[2,72,512]{2,1,0:T(8,128)S(1)}, u32[]{:S(2)}, u32[]{:S(2)}) collective-permute-start(f32[2,72,512]{2,1,0:T(8,128)S(1)} %pad_maximum_fusion.11), channel_id=1, source_target_pairs={{0,4},{4,8},{8,12},{12,16},{16,20},{20,24},{24,28},{28,32},{32,36}... | collective-permute-start | bytes 884744 | tf_op jit(solution)/shard_map/ppermute | solution.py:26
  25.3 8.8 %collective-permute-start.4 = (f32[2,144,128]{2,1,0:T(8,128)S(1)}, f32[2,144,128]{2,1,0:T(8,128)S(1)}, u32[]{:S(2)}, u32[]{:S(2)}) collective-permute-start(f32[2,144,128]{2,1,0:T(8,128)S(1)} %add.1277), channel_id=1, source_target_pairs={{0,32},{4,36},{8,40},{12,44},{16,48},{20,52},{24,56},{28,60},{32,6... | collective-permute-start | bytes 442376 | tf_op jit(solution)/shard_map/ppermute | solution.py:26
  27.2 5.5 %collective-permute-start.5 = (f32[144,128]{1,0:T(8,128)S(1)}, f32[144,128]{1,0:T(8,128)S(1)}, u32[]{:S(2)}, u32[]{:S(2)}) collective-permute-start(f32[144,128]{1,0:T(8,128)S(1)} %maximum_maximum_fusion.4), channel_id=1, source_target_pairs={{0,224},{4,228},{8,232},{12,236},{16,240},{20,244},{24,248},{28,25... | collective-permute-start | bytes 221192 | tf_op jit(solution)/shard_map/ppermute | solution.py:26
  35.2 10.2 %collective-permute-start.10 = (f32[160,128]{1,0:T(8,128)S(1)}, f32[160,128]{1,0:T(8,128)S(1)}, u32[]{:S(2)}, u32[]{:S(2)}) collective-permute-start(f32[160,128]{1,0:T(8,128)S(1)} %maximum_maximum_fusion.3), channel_id=1, source_target_pairs={{0,96},{4,100},{8,104},{12,108},{16,112},{20,116},{24,120},{28,124... | collective-permute-start | bytes 245768 | tf_op jit(solution)/shard_map/ppermute | solution.py:26
  38.7 5.7 %collective-permute-start.8 = (f32[160,128]{1,0:T(8,128)S(1)}, f32[160,128]{1,0:T(8,128)S(1)}, u32[]{:S(2)}, u32[]{:S(2)}) collective-permute-start(f32[160,128]{1,0:T(8,128)S(1)} %maximum_maximum_fusion.3), channel_id=1, source_target_pairs={{0,192},{4,196},{8,200},{12,204},{16,208},{20,212},{24,216},{28,22... | collective-permute-start | bytes 245768 | tf_op jit(solution)/shard_map/ppermute | solution.py:26
  40.5 3.8 %collective-permute-start.9 = (f32[2,48,512]{2,1,0:T(8,128)S(1)}, f32[2,48,512]{2,1,0:T(8,128)S(1)}, u32[]{:S(2)}, u32[]{:S(2)}) collective-permute-start(f32[2,48,512]{2,1,0:T(8,128)S(1)} %broadcast_select_fusion.5), channel_id=1, source_target_pairs={{0,4},{4,0},{8,12},{12,8},{16,20},{20,16},{24,28},{28,24},{32,36},... | collective-permute-start | bytes 589832 | tf_op jit(solution)/shard_map/ppermute | solution.py:31
  46.9 9.0 %collective-permute-start.11 = (f32[2,128,128]{2,1,0:T(8,128)S(1)}, f32[2,128,128]{2,1,0:T(8,128)S(1)}, u32[]{:S(2)}, u32[]{:S(2)}) collective-permute-start(f32[2,128,128]{2,1,0:T(8,128)S(1)} %slice_select_fusion.6), channel_id=1, source_target_pairs={{0,24},{4,28},{8,16},{12,20},{16,8},{20,12},{24,0},{28,4},{32,56},... | collective-permute-start | bytes 393224 | tf_op jit(solution)/shard_map/ppermute | solution.py:31
  52.0 3.8 %collective-permute-start.12 = (f32[96,256]{1,0:T(8,128)S(1)}, f32[96,256]{1,0:T(8,128)S(1)}, u32[]{:S(2)}, u32[]{:S(2)}) collective-permute-start(f32[96,256]{1,0:T(8,128)S(1)} %slice_select_fusion.7), channel_id=1, source_target_pairs={{0,8},{4,12},{8,0},{12,4},{16,24},{20,28},{24,16},{28,20},{32,40},... | collective-permute-start | bytes 294920 | tf_op jit(solution)/shard_map/ppermute | solution.py:31
  56.1 3.5 %collective-permute-start.14 = (f32[24,768]{1,0:T(8,128)S(1)}, f32[24,768]{1,0:T(8,128)S(1)}, u32[]{:S(2)}, u32[]{:S(2)}) collective-permute-start(f32[24,768]{1,0:T(8,128)S(1)} %get-tuple-element.136), channel_id=1, source_target_pairs={{0,3},{1,0},{2,1},{3,2},{4,7},{5,4},{6,5},{7,6},{8,11},{9,8},{10,9... | collective-permute-start | bytes 221192 | tf_op jit(solution)/shard_map/ppermute | solution.py:26
  56.4 4.5 %collective-permute-start.13 = (f32[24,768]{1,0:T(8,128)S(1)}, f32[24,768]{1,0:T(8,128)S(1)}, u32[]{:S(2)}, u32[]{:S(2)}) collective-permute-start(f32[24,768]{1,0:T(8,128)S(1)} %get-tuple-element.137), channel_id=1, source_target_pairs={{0,1},{1,2},{2,3},{3,0},{4,5},{5,6},{6,7},{7,4},{8,9},{9,10},{10,1... | collective-permute-start | bytes 221192 | tf_op jit(solution)/shard_map/ppermute | solution.py:26
  57.9 7.0 %collective-permute-start.17 = (f32[4,24,512]{2,1,0:T(8,128)S(1)}, f32[4,24,512]{2,1,0:T(8,128)S(1)}, u32[]{:S(2)}, u32[]{:S(2)}) collective-permute-start(f32[4,24,512]{2,1,0:T(8,128)S(1)} %get-tuple-element.85), channel_id=1, source_target_pairs={{0,3},{1,0},{2,1},{3,2},{4,7},{5,4},{6,5},{7,6},{8,11},{9,8},{10,9... | collective-permute-start | bytes 589832 | tf_op jit(solution)/shard_map/ppermute | solution.py:26
  59.3 6.4 %collective-permute-start.16 = (f32[4,24,512]{2,1,0:T(8,128)S(1)}, f32[4,24,512]{2,1,0:T(8,128)S(1)}, u32[]{:S(2)}, u32[]{:S(2)}) collective-permute-start(f32[4,24,512]{2,1,0:T(8,128)S(1)} %get-tuple-element.86), channel_id=1, source_target_pairs={{0,1},{1,2},{2,3},{3,0},{4,5},{5,6},{6,7},{7,4},{8,9},{9,10},{10,1... | collective-permute-start | bytes 589832 | tf_op jit(solution)/shard_map/ppermute | solution.py:26
  61.0 3.8 %collective-permute-start.15 = (f32[2,96,128]{2,1,0:T(8,128)S(1)}, f32[2,96,128]{2,1,0:T(8,128)S(1)}, u32[]{:S(2)}, u32[]{:S(2)}) collective-permute-start(f32[2,96,128]{2,1,0:T(8,128)S(1)} %slice_add_fusion.3), channel_id=1, source_target_pairs={{0,8},{4,12},{8,0},{12,4},{16,24},{20,28},{24,16},{28,20},{32,40},... | collective-permute-start | bytes 294920 | tf_op jit(solution)/shard_map/ppermute | solution.py:31
  65.7 5.4 %collective-permute-start.18 = (f32[3,96,256]{2,1,0:T(8,128)S(1)}, f32[3,96,256]{2,1,0:T(8,128)S(1)}, u32[]{:S(2)}, u32[]{:S(2)}) collective-permute-start(f32[3,96,256]{2,1,0:T(8,128)S(1)} %pad_maximum_fusion.13), channel_id=1, source_target_pairs={{0,4},{4,0},{8,12},{12,8},{16,20},{20,16},{24,28},{28,24},{32,36},... | collective-permute-start | bytes 884744 | tf_op jit(solution)/shard_map/ppermute | solution.py:31
